TPU v7x, 256 devices: a whole 4x4x8 slice. The times are simulated.
256 devices in a mesh: tm: 16 (over z, core), space: 16 (over x, y).
Axes of the slice: x: 4, y: 4, z: 8, core: 2. Of those that a mesh axis runs over, the one named last changes fastest.
Arguments:
- c_guess: float32 [16, 64, 32, 1024], P('tm', 'space'), may hold values from -6 to 6
- source: float32 [64, 32, 1024], P('space'), may hold values from -4 to 4
- rate: float32 [64, 32, 1024], P('space'), may hold values from 0.25 to 4
Outputs:
- fine_solution: float32 [16, 2, 64, 32, 1024], P('tm', None, 'space')
- coarse_residual: float32 [16, 64, 32, 1024], P('tm', 'space')
All inputs are finite; a program needn't handle non-finite values.
Results may differ from a plain program's by a relative error of at most 0.00002.
Values sent between devices are 32-bit elements; how exact they have to be, the bound alone decides.
No kernel may reach another device: no remote copies, remote signals or barrier semaphores. Data moves between devices by JAX's collectives and lax.ppermute only.
A program may use at most 64 MiB of HBM per device.

v0:
```python
import jax
import jax.numpy as jnp
from jax import lax
from jax.sharding import PartitionSpec as P

M = 2
SWEEPS = 4


def padded_2(cells, sides, width):
    for axis, dim in sides:
        count = lax.axis_size(axis)
        ends = count - 1
        head = lax.slice_in_dim(cells, 0, width, axis=dim)
        tail = lax.slice_in_dim(cells, cells.shape[dim] - width, cells.shape[dim], axis=dim)
        cells = jnp.concatenate(
            [
                lax.ppermute(tail, axis, [(i, (i + 1) % count) for i in range(ends)]),
                cells,
                lax.ppermute(head, axis, [((i + 1) % count, i) for i in range(ends)]),
            ],
            axis=dim,
        )
    return cells


def passed_along(value, axis, steps):
    count = lax.axis_size(axis)
    initial, last = (max(0, -steps), min(count, count - steps))
    return lax.ppermute(value, axis, [(source, source + steps) for source in range(initial, last)])


def relax_sweep(iterate, right_side, rate_ext):
    interior = iterate[1:-1]
    padded = jnp.pad(interior, ((0, 0), (1, 1), (1, 1)))
    neighbours = iterate[2:] + iterate[:-2]
    neighbours = neighbours + padded[:, 2:, 1:-1] + padded[:, :-2, 1:-1]
    neighbours = neighbours + padded[:, 1:-1, 2:] + padded[:, 1:-1, :-2]
    rate_in = rate_ext[1:-1]
    return (right_side[1:-1] + rate_in * neighbours) / (1.0 + 6.0 * rate_in)


def fine_border(field, rim_depth):
    return padded_2(field, (("space", 0),), rim_depth)


def coarse_border(field, rim_depth):
    return padded_2(field, (("space", 0),), rim_depth)


def implicit_step(state, source_ext, rate_ext, rim_depth, border_fn):
    cell_rows = state.shape[0]
    iterate = border_fn(state, rim_depth)
    right_side = iterate if source_ext is None else iterate + source_ext
    for sweep_no in range(SWEEPS):
        if sweep_no > 0 and sweep_no % rim_depth == 0:
            iterate = border_fn(iterate, rim_depth)
        extent = rim_depth - sweep_no % rim_depth
        offset = rim_depth - extent
        length = cell_rows + 2 * extent
        iterate = relax_sweep(
            iterate, right_side[offset : offset + length], rate_ext[offset : offset + length]
        )
    return iterate


def body(c_guess, source, rate):
    owner_index = lax.axis_index("tm")
    owners = lax.axis_size("tm")
    rim_depth = 2
    stacked = jnp.stack((source, rate))
    rimmed = padded_2(stacked, (("space", 1),), rim_depth)
    source_ext = rimmed[0]
    rate_ext = rimmed[1]
    coarse_rate = M * rate_ext

    def fine_step(state):
        return implicit_step(state, source_ext, rate_ext, rim_depth, fine_border)

    def coarse_step(state):
        return implicit_step(state, None, coarse_rate, rim_depth, coarse_border)

    start_guess = c_guess[0]
    relaxed = start_guess
    relaxed = fine_step(relaxed)
    arrived = passed_along(relaxed, "tm", 1)
    cpoint = jnp.where(owner_index == 0, start_guess, fine_step(arrived))
    forward = cpoint
    for step_no in range(M):
        forward = fine_step(forward)
    incoming = passed_along(forward, "tm", 1)
    residual = jnp.where(owner_index == 0, jnp.zeros_like(cpoint), incoming - cpoint)

    def relay_turn(turn_no, corrected_now):
        outgoing = forward + coarse_step(corrected_now - cpoint)
        received = passed_along(outgoing, "tm", 1)
        return jnp.where(owner_index == 0, cpoint, received)

    initial = jnp.where(owner_index == 0, cpoint, incoming)
    corrected = lax.fori_loop(0, owners - 2, relay_turn, initial)
    fine_points = [corrected]
    fine_points.append(fine_step(fine_points[-1]))
    return (jnp.stack(fine_points)[None], residual[None])


def solution(mesh):
    placed = (P("tm", "space", None, None), P("space", None, None), P("space", None, None))
    return jax.shard_map(
        body,
        mesh=mesh,
        in_specs=placed,
        out_specs=(P("tm", None, "space", None, None), P("tm", "space", None, None)),
        check_vma=False,
    )
```

profile of v0, /device:TPU:88, one launch (start us, length us, event | category | flops | bytes accessed | tf_op | source)
XLA Modules:
  0.0 815.8 jit_solution(8687046143704070284)
XLA Ops:
  18.8 5.2 collective-permute-done.8
  46.0 8.6 %collective-permute-done.11 = f32[4,32,1024]{2,1,0:T(8,128)S(1)} collective-permute-done((f32[4,32,1024]{2,1,0:T(8,128)S(1)}, f32[4,32,1024]{2,1,0:T(8,128)S(1)}, u32[]{:S(2)}, u32[]{:S(2)}) %collective-permute-start.11) | collective-permute-done | bytes 524320 | tf_op jit(solution)/shard_map/ppermute | solution.py:30
  146.0 8.5 %collective-permute-done.24 = f32[4,32,1024]{2,1,0:T(8,128)S(1)} collective-permute-done((f32[4,32,1024]{2,1,0:T(8,128)S(1)}, f32[4,32,1024]{2,1,0:T(8,128)S(1)}, u32[]{:S(2)}, u32[]{:S(2)}) %collective-permute-start.24) | collective-permute-done | bytes 524320 | tf_op jit(solution)/shard_map/ppermute | solution.py:30
  155.5 623.2 %while.12 = (s32[]{:T(128)}, f32[4,32,1024]{2,1,0:T(8,128)}, pred[]{:T(512)}, f32[4,32,1024]{2,1,0:T(8,128)}, f32[8,32,1024]{2,1,0:T(8,128)S(1)}, /*index=5*/f32[4,32,1024]{2,1,0:T(8,128)}, s32[]{:T(128)}) while((s32[]{:T(128)}, f32[4,32,1024]{2,1,0:T(8,128)}, pred[]{:T(512)}, f32[4,32,1024]{2,1,0:T(8,128)}, f32[8,32,1024]{2,1,0:T(8,128)S(1)}, ...), condition=%wide.region_1.2_spmd, body=%wide.region_0.1_spmd.sunk | while | flops 11266026 | bytes 36226960 | solution.py:100
  158.8 6.0 collective-permute-start.1
  172.9 6.5 collective-permute-start.3
  191.4 8.3 %collective-permute-done.4 = f32[4,32,1024]{2,1,0:T(8,128)} collective-permute-done((f32[4,32,1024]{2,1,0:T(8,128)}, f32[4,32,1024]{2,1,0:T(8,128)}, u32[]{:S(2)}, u32[]{:S(2)}) %collective-permute-start.4) | collective-permute-done | bytes 524320 | tf_op jit(solution)/shard_map/while/body/eval_jaxpr/ppermute | solution.py:30
  204.8 6.5 collective-permute-start.1
  219.7 6.5 collective-permute-start.3
  235.8 8.9 %collective-permute-done.4 = f32[4,32,1024]{2,1,0:T(8,128)} collective-permute-done((f32[4,32,1024]{2,1,0:T(8,128)}, f32[4,32,1024]{2,1,0:T(8,128)}, u32[]{:S(2)}, u32[]{:S(2)}) %collective-permute-start.4) | collective-permute-done | bytes 524320 | tf_op jit(solution)/shard_map/while/body/eval_jaxpr/ppermute | solution.py:30
  249.9 6.5 collective-permute-start.1
  263.4 6.5 collective-permute-start.3
  279.0 8.9 %collective-permute-done.4 = f32[4,32,1024]{2,1,0:T(8,128)} collective-permute-done((f32[4,32,1024]{2,1,0:T(8,128)}, f32[4,32,1024]{2,1,0:T(8,128)}, u32[]{:S(2)}, u32[]{:S(2)}) %collective-permute-start.4) | collective-permute-done | bytes 524320 | tf_op jit(solution)/shard_map/while/body/eval_jaxpr/ppermute | solution.py:30
  293.0 6.5 collective-permute-start.1
  307.1 6.5 collective-permute-start.3
  322.7 8.9 %collective-permute-done.4 = f32[4,32,1024]{2,1,0:T(8,128)} collective-permute-done((f32[4,32,1024]{2,1,0:T(8,128)}, f32[4,32,1024]{2,1,0:T(8,128)}, u32[]{:S(2)}, u32[]{:S(2)}) %collective-permute-start.4) | collective-permute-done | bytes 524320 | tf_op jit(solution)/shard_map/while/body/eval_jaxpr/ppermute | solution.py:30
  336.7 6.5 collective-permute-start.1
  351.6 6.5 collective-permute-start.3
  367.6 8.9 %collective-permute-done.4 = f32[4,32,1024]{2,1,0:T(8,128)} collective-permute-done((f32[4,32,1024]{2,1,0:T(8,128)}, f32[4,32,1024]{2,1,0:T(8,128)}, u32[]{:S(2)}, u32[]{:S(2)}) %collective-permute-start.4) | collective-permute-done | bytes 524320 | tf_op jit(solution)/shard_map/while/body/eval_jaxpr/ppermute | solution.py:30
  381.7 6.5 collective-permute-start.1
  396.5 6.5 collective-permute-start.3
  415.0 8.4 %collective-permute-done.4 = f32[4,32,1024]{2,1,0:T(8,128)} collective-permute-done((f32[4,32,1024]{2,1,0:T(8,128)}, f32[4,32,1024]{2,1,0:T(8,128)}, u32[]{:S(2)}, u32[]{:S(2)}) %collective-permute-start.4) | collective-permute-done | bytes 524320 | tf_op jit(solution)/shard_map/while/body/eval_jaxpr/ppermute | solution.py:30
  428.6 6.5 collective-permute-start.1
  442.6 6.5 collective-permute-start.3
  458.2 8.9 %collective-permute-done.4 = f32[4,32,1024]{2,1,0:T(8,128)} collective-permute-done((f32[4,32,1024]{2,1,0:T(8,128)}, f32[4,32,1024]{2,1,0:T(8,128)}, u32[]{:S(2)}, u32[]{:S(2)}) %collective-permute-start.4) | collective-permute-done | bytes 524320 | tf_op jit(solution)/shard_map/while/body/eval_jaxpr/ppermute | solution.py:30
  472.2 6.5 collective-permute-start.1
  486.2 6.5 collective-permute-start.3
  501.8 8.9 %collective-permute-done.4 = f32[4,32,1024]{2,1,0:T(8,128)} collective-permute-done((f32[4,32,1024]{2,1,0:T(8,128)}, f32[4,32,1024]{2,1,0:T(8,128)}, u32[]{:S(2)}, u32[]{:S(2)}) %collective-permute-start.4) | collective-permute-done | bytes 524320 | tf_op jit(solution)/shard_map/while/body/eval_jaxpr/ppermute | solution.py:30
  515.9 6.5 collective-permute-start.1
  530.9 6.5 collective-permute-start.3
  547.1 8.9 %collective-permute-done.4 = f32[4,32,1024]{2,1,0:T(8,128)} collective-permute-done((f32[4,32,1024]{2,1,0:T(8,128)}, f32[4,32,1024]{2,1,0:T(8,128)}, u32[]{:S(2)}, u32[]{:S(2)}) %collective-permute-start.4) | collective-permute-done | bytes 524320 | tf_op jit(solution)/shard_map/while/body/eval_jaxpr/ppermute | solution.py:30
  561.1 6.5 collective-permute-start.1
  574.9 6.5 collective-permute-start.3
  590.5 8.9 %collective-permute-done.4 = f32[4,32,1024]{2,1,0:T(8,128)} collective-permute-done((f32[4,32,1024]{2,1,0:T(8,128)}, f32[4,32,1024]{2,1,0:T(8,128)}, u32[]{:S(2)}, u32[]{:S(2)}) %collective-permute-start.4) | collective-permute-done | bytes 524320 | tf_op jit(solution)/shard_map/while/body/eval_jaxpr/ppermute | solution.py:30
  604.6 6.5 collective-permute-start.1
  619.6 6.5 collective-permute-start.3
  635.8 8.9 %collective-permute-done.4 = f32[4,32,1024]{2,1,0:T(8,128)} collective-permute-done((f32[4,32,1024]{2,1,0:T(8,128)}, f32[4,32,1024]{2,1,0:T(8,128)}, u32[]{:S(2)}, u32[]{:S(2)}) %collective-permute-start.4) | collective-permute-done | bytes 524320 | tf_op jit(solution)/shard_map/while/body/eval_jaxpr/ppermute | solution.py:30
  649.8 6.5 collective-permute-start.1
  663.7 6.5 collective-permute-start.3
  679.3 8.9 %collective-permute-done.4 = f32[4,32,1024]{2,1,0:T(8,128)} collective-permute-done((f32[4,32,1024]{2,1,0:T(8,128)}, f32[4,32,1024]{2,1,0:T(8,128)}, u32[]{:S(2)}, u32[]{:S(2)}) %collective-permute-start.4) | collective-permute-done | bytes 524320 | tf_op jit(solution)/shard_map/while/body/eval_jaxpr/ppermute | solution.py:30
  693.3 6.5 collective-permute-start.1
  708.3 6.5 collective-permute-start.3
  724.5 8.9 %collective-permute-done.4 = f32[4,32,1024]{2,1,0:T(8,128)} collective-permute-done((f32[4,32,1024]{2,1,0:T(8,128)}, f32[4,32,1024]{2,1,0:T(8,128)}, u32[]{:S(2)}, u32[]{:S(2)}) %collective-permute-start.4) | collective-permute-done | bytes 524320 | tf_op jit(solution)/shard_map/while/body/eval_jaxpr/ppermute | solution.py:30
  738.5 6.5 collective-permute-start.1
  752.4 6.5 collective-permute-start.3
  768.0 8.9 %collective-permute-done.4 = f32[4,32,1024]{2,1,0:T(8,128)} collective-permute-done((f32[4,32,1024]{2,1,0:T(8,128)}, f32[4,32,1024]{2,1,0:T(8,128)}, u32[]{:S(2)}, u32[]{:S(2)}) %collective-permute-start.4) | collective-permute-done | bytes 524320 | tf_op jit(solution)/shard_map/while/body/eval_jaxpr/ppermute | solution.py:30
  779.9 6.5 collective-permute-start.25
  791.9 6.1 collective-permute-done.26
  (423 shorter events, 473.0 us)
Async XLA Ops:
  2.1 16.7 %collective-permute-start.7 = (f32[2,2,32,1024]{3,2,1,0:T(8,128)S(1)}, f32[2,2,32,1024]{3,2,1,0:T(8,128)S(1)}, u32[]{:S(2)}, u32[]{:S(2)}) collective-permute-start(f32[2,2,32,1024]{3,2,1,0:T(8,128)S(1)} %get-tuple-element.106), channel_id=1, source_target_pairs={{0,1},{1,2},{2,3},{3,4},{4,5},{5,6},{6,7},{7,8},{8,9},{9,10},{10,1... | collective-permute-start | bytes 1572872 | tf_op jit(solution)/shard_map/ppermute | solution.py:18
  5.1 18.9 %collective-permute-start.8 = (f32[2,2,32,1024]{3,2,1,0:T(8,128)S(1)}, f32[2,2,32,1024]{3,2,1,0:T(8,128)S(1)}, u32[]{:S(2)}, u32[]{:S(2)}) collective-permute-start(f32[2,2,32,1024]{3,2,1,0:T(8,128)S(1)} %get-tuple-element.107), channel_id=1, source_target_pairs={{1,0},{2,1},{3,2},{4,3},{5,4},{6,5},{7,6},{8,7},{9,8},{10,9},{11,1... | collective-permute-start | bytes 1572872 | tf_op jit(solution)/shard_map/ppermute | solution.py:20
  8.0 16.2 %collective-permute-start.5 = (f32[2,32,1024]{2,1,0:T(8,128)S(1)}, f32[2,32,1024]{2,1,0:T(8,128)S(1)}, u32[]{:S(2)}, u32[]{:S(2)}) collective-permute-start(f32[2,32,1024]{2,1,0:T(8,128)S(1)} %get-tuple-element.126), channel_id=1, source_target_pairs={{0,1},{1,2},{2,3},{3,4},{4,5},{5,6},{6,7},{7,8},{8,9},{9,10},{10,1... | collective-permute-start | bytes 786440 | tf_op jit(solution)/shard_map/ppermute | solution.py:18
  13.2 15.0 %collective-permute-start.6 = (f32[2,32,1024]{2,1,0:T(8,128)S(1)}, f32[2,32,1024]{2,1,0:T(8,128)S(1)}, u32[]{:S(2)}, u32[]{:S(2)}) collective-permute-start(f32[2,32,1024]{2,1,0:T(8,128)S(1)} %get-tuple-element.127), channel_id=1, source_target_pairs={{1,0},{2,1},{3,2},{4,3},{5,4},{6,5},{7,6},{8,7},{9,8},{10,9},{11,1... | collective-permute-start | bytes 786440 | tf_op jit(solution)/shard_map/ppermute | solution.py:20
  31.6 10.9 %collective-permute-start.9 = (f32[2,32,1024]{2,1,0:T(8,128)S(1)}, f32[2,32,1024]{2,1,0:T(8,128)S(1)}, u32[]{:S(2)}, u32[]{:S(2)}) collective-permute-start(f32[2,32,1024]{2,1,0:T(8,128)S(1)} %get-tuple-element.125), channel_id=1, source_target_pairs={{1,0},{2,1},{3,2},{4,3},{5,4},{6,5},{7,6},{8,7},{9,8},{10,9},{11,1... | collective-permute-start | bytes 786440 | tf_op jit(solution)/shard_map/ppermute | solution.py:20
  56.5 11.8 %collective-permute-start.13 = (f32[2,32,1024]{2,1,0:T(8,128)S(1)}, f32[2,32,1024]{2,1,0:T(8,128)S(1)}, u32[]{:S(2)}, u32[]{:S(2)}) collective-permute-start(f32[2,32,1024]{2,1,0:T(8,128)S(1)} %get-tuple-element.122), channel_id=1, source_target_pairs={{1,0},{2,1},{3,2},{4,3},{5,4},{6,5},{7,6},{8,7},{9,8},{10,9},{11,1... | collective-permute-start | bytes 786440 | tf_op jit(solution)/shard_map/ppermute | solution.py:20
  72.7 11.2 %collective-permute-start.14 = (f32[2,32,1024]{2,1,0:T(8,128)}, f32[2,32,1024]{2,1,0:T(8,128)}, u32[]{:S(2)}, u32[]{:S(2)}) collective-permute-start(f32[2,32,1024]{2,1,0:T(8,128)} %get-tuple-element.121), channel_id=1, source_target_pairs={{1,0},{2,1},{3,2},{4,3},{5,4},{6,5},{7,6},{8,7},{9,8},{10,9},{11,1... | collective-permute-start | bytes 786440 | tf_op jit(solution)/shard_map/ppermute | solution.py:20
  156.9 11.2 %collective-permute-start = (f32[2,32,1024]{2,1,0:T(8,128)S(1)}, f32[2,32,1024]{2,1,0:T(8,128)S(1)}, u32[]{:S(2)}, u32[]{:S(2)}) collective-permute-start(f32[2,32,1024]{2,1,0:T(8,128)S(1)} %get-tuple-element.169), channel_id=1, source_target_pairs={{1,0},{2,1},{3,2},{4,3},{5,4},{6,5},{7,6},{8,7},{9,8},{10,9},{11,1... | collective-permute-start | bytes 786440 | tf_op jit(solution)/shard_map/while/body/eval_jaxpr/ppermute | solution.py:20
  158.8 11.0 %collective-permute-start.1 = (f32[2,32,1024]{2,1,0:T(8,128)S(1)}, f32[2,32,1024]{2,1,0:T(8,128)S(1)}, u32[]{:S(2)}, u32[]{:S(2)}) collective-permute-start(f32[2,32,1024]{2,1,0:T(8,128)S(1)} %get-tuple-element.170), channel_id=1, source_target_pairs={{0,1},{1,2},{2,3},{3,4},{4,5},{5,6},{6,7},{7,8},{8,9},{9,10},{10,1... | collective-permute-start | bytes 786440 | tf_op jit(solution)/shard_map/while/body/eval_jaxpr/ppermute | solution.py:18
  171.0 12.8 %collective-permute-start.2 = (f32[2,32,1024]{2,1,0:T(8,128)S(1)}, f32[2,32,1024]{2,1,0:T(8,128)S(1)}, u32[]{:S(2)}, u32[]{:S(2)}) collective-permute-start(f32[2,32,1024]{2,1,0:T(8,128)S(1)} %get-tuple-element.171), channel_id=1, source_target_pairs={{1,0},{2,1},{3,2},{4,3},{5,4},{6,5},{7,6},{8,7},{9,8},{10,9},{11,1... | collective-permute-start | bytes 786440 | tf_op jit(solution)/shard_map/while/body/eval_jaxpr/ppermute | solution.py:20
  172.9 12.7 %collective-permute-start.3 = (f32[2,32,1024]{2,1,0:T(8,128)S(1)}, f32[2,32,1024]{2,1,0:T(8,128)S(1)}, u32[]{:S(2)}, u32[]{:S(2)}) collective-permute-start(f32[2,32,1024]{2,1,0:T(8,128)S(1)} %get-tuple-element.172), channel_id=1, source_target_pairs={{0,1},{1,2},{2,3},{3,4},{4,5},{5,6},{6,7},{7,8},{8,9},{9,10},{10,1... | collective-permute-start | bytes 786440 | tf_op jit(solution)/shard_map/while/body/eval_jaxpr/ppermute | solution.py:18
  202.9 12.5 %collective-permute-start = (f32[2,32,1024]{2,1,0:T(8,128)S(1)}, f32[2,32,1024]{2,1,0:T(8,128)S(1)}, u32[]{:S(2)}, u32[]{:S(2)}) collective-permute-start(f32[2,32,1024]{2,1,0:T(8,128)S(1)} %get-tuple-element.169), channel_id=1, source_target_pairs={{1,0},{2,1},{3,2},{4,3},{5,4},{6,5},{7,6},{8,7},{9,8},{10,9},{11,1... | collective-permute-start | bytes 786440 | tf_op jit(solution)/shard_map/while/body/eval_jaxpr/ppermute | solution.py:20
  204.8 11.8 %collective-permute-start.1 = (f32[2,32,1024]{2,1,0:T(8,128)S(1)}, f32[2,32,1024]{2,1,0:T(8,128)S(1)}, u32[]{:S(2)}, u32[]{:S(2)}) collective-permute-start(f32[2,32,1024]{2,1,0:T(8,128)S(1)} %get-tuple-element.170), channel_id=1, source_target_pairs={{0,1},{1,2},{2,3},{3,4},{4,5},{5,6},{6,7},{7,8},{8,9},{9,10},{10,1... | collective-permute-start | bytes 786440 | tf_op jit(solution)/shard_map/while/body/eval_jaxpr/ppermute | solution.py:18
  217.8 11.6 %collective-permute-start.2 = (f32[2,32,1024]{2,1,0:T(8,128)S(1)}, f32[2,32,1024]{2,1,0:T(8,128)S(1)}, u32[]{:S(2)}, u32[]{:S(2)}) collective-permute-start(f32[2,32,1024]{2,1,0:T(8,128)S(1)} %get-tuple-element.171), channel_id=1, source_target_pairs={{1,0},{2,1},{3,2},{4,3},{5,4},{6,5},{7,6},{8,7},{9,8},{10,9},{11,1... | collective-permute-start | bytes 786440 | tf_op jit(solution)/shard_map/while/body/eval_jaxpr/ppermute | solution.py:20
  219.7 10.9 %collective-permute-start.3 = (f32[2,32,1024]{2,1,0:T(8,128)S(1)}, f32[2,32,1024]{2,1,0:T(8,128)S(1)}, u32[]{:S(2)}, u32[]{:S(2)}) collective-permute-start(f32[2,32,1024]{2,1,0:T(8,128)S(1)} %get-tuple-element.172), channel_id=1, source_target_pairs={{0,1},{1,2},{2,3},{3,4},{4,5},{5,6},{6,7},{7,8},{8,9},{9,10},{10,1... | collective-permute-start | bytes 786440 | tf_op jit(solution)/shard_map/while/body/eval_jaxpr/ppermute | solution.py:18
  247.9 10.8 %collective-permute-start = (f32[2,32,1024]{2,1,0:T(8,128)S(1)}, f32[2,32,1024]{2,1,0:T(8,128)S(1)}, u32[]{:S(2)}, u32[]{:S(2)}) collective-permute-start(f32[2,32,1024]{2,1,0:T(8,128)S(1)} %get-tuple-element.169), channel_id=1, source_target_pairs={{1,0},{2,1},{3,2},{4,3},{5,4},{6,5},{7,6},{8,7},{9,8},{10,9},{11,1... | collective-permute-start | bytes 786440 | tf_op jit(solution)/shard_map/while/body/eval_jaxpr/ppermute | solution.py:20
  261.4 10.8 %collective-permute-start.2 = (f32[2,32,1024]{2,1,0:T(8,128)S(1)}, f32[2,32,1024]{2,1,0:T(8,128)S(1)}, u32[]{:S(2)}, u32[]{:S(2)}) collective-permute-start(f32[2,32,1024]{2,1,0:T(8,128)S(1)} %get-tuple-element.171), channel_id=1, source_target_pairs={{1,0},{2,1},{3,2},{4,3},{5,4},{6,5},{7,6},{8,7},{9,8},{10,9},{11,1... | collective-permute-start | bytes 786440 | tf_op jit(solution)/shard_map/while/body/eval_jaxpr/ppermute | solution.py:20
  291.1 11.7 %collective-permute-start = (f32[2,32,1024]{2,1,0:T(8,128)S(1)}, f32[2,32,1024]{2,1,0:T(8,128)S(1)}, u32[]{:S(2)}, u32[]{:S(2)}) collective-permute-start(f32[2,32,1024]{2,1,0:T(8,128)S(1)} %get-tuple-element.169), channel_id=1, source_target_pairs={{1,0},{2,1},{3,2},{4,3},{5,4},{6,5},{7,6},{8,7},{9,8},{10,9},{11,1... | collective-permute-start | bytes 786440 | tf_op jit(solution)/shard_map/while/body/eval_jaxpr/ppermute | solution.py:20
  293.0 11.0 %collective-permute-start.1 = (f32[2,32,1024]{2,1,0:T(8,128)S(1)}, f32[2,32,1024]{2,1,0:T(8,128)S(1)}, u32[]{:S(2)}, u32[]{:S(2)}) collective-permute-start(f32[2,32,1024]{2,1,0:T(8,128)S(1)} %get-tuple-element.170), channel_id=1, source_target_pairs={{0,1},{1,2},{2,3},{3,4},{4,5},{5,6},{6,7},{7,8},{8,9},{9,10},{10,1... | collective-permute-start | bytes 786440 | tf_op jit(solution)/shard_map/while/body/eval_jaxpr/ppermute | solution.py:18
  305.2 10.8 %collective-permute-start.2 = (f32[2,32,1024]{2,1,0:T(8,128)S(1)}, f32[2,32,1024]{2,1,0:T(8,128)S(1)}, u32[]{:S(2)}, u32[]{:S(2)}) collective-permute-start(f32[2,32,1024]{2,1,0:T(8,128)S(1)} %get-tuple-element.171), channel_id=1, source_target_pairs={{1,0},{2,1},{3,2},{4,3},{5,4},{6,5},{7,6},{8,7},{9,8},{10,9},{11,1... | collective-permute-start | bytes 786440 | tf_op jit(solution)/shard_map/while/body/eval_jaxpr/ppermute | solution.py:20
  334.8 12.5 %collective-permute-start = (f32[2,32,1024]{2,1,0:T(8,128)S(1)}, f32[2,32,1024]{2,1,0:T(8,128)S(1)}, u32[]{:S(2)}, u32[]{:S(2)}) collective-permute-start(f32[2,32,1024]{2,1,0:T(8,128)S(1)} %get-tuple-element.169), channel_id=1, source_target_pairs={{1,0},{2,1},{3,2},{4,3},{5,4},{6,5},{7,6},{8,7},{9,8},{10,9},{11,1... | collective-permute-start | bytes 786440 | tf_op jit(solution)/shard_map/while/body/eval_jaxpr/ppermute | solution.py:20
  336.7 11.7 %collective-permute-start.1 = (f32[2,32,1024]{2,1,0:T(8,128)S(1)}, f32[2,32,1024]{2,1,0:T(8,128)S(1)}, u32[]{:S(2)}, u32[]{:S(2)}) collective-permute-start(f32[2,32,1024]{2,1,0:T(8,128)S(1)} %get-tuple-element.170), channel_id=1, source_target_pairs={{0,1},{1,2},{2,3},{3,4},{4,5},{5,6},{6,7},{7,8},{8,9},{9,10},{10,1... | collective-permute-start | bytes 786440 | tf_op jit(solution)/shard_map/while/body/eval_jaxpr/ppermute | solution.py:18
  349.7 11.5 %collective-permute-start.2 = (f32[2,32,1024]{2,1,0:T(8,128)S(1)}, f32[2,32,1024]{2,1,0:T(8,128)S(1)}, u32[]{:S(2)}, u32[]{:S(2)}) collective-permute-start(f32[2,32,1024]{2,1,0:T(8,128)S(1)} %get-tuple-element.171), channel_id=1, source_target_pairs={{1,0},{2,1},{3,2},{4,3},{5,4},{6,5},{7,6},{8,7},{9,8},{10,9},{11,1... | collective-permute-start | bytes 786440 | tf_op jit(solution)/shard_map/while/body/eval_jaxpr/ppermute | solution.py:20
  379.7 11.9 %collective-permute-start = (f32[2,32,1024]{2,1,0:T(8,128)S(1)}, f32[2,32,1024]{2,1,0:T(8,128)S(1)}, u32[]{:S(2)}, u32[]{:S(2)}) collective-permute-start(f32[2,32,1024]{2,1,0:T(8,128)S(1)} %get-tuple-element.169), channel_id=1, source_target_pairs={{1,0},{2,1},{3,2},{4,3},{5,4},{6,5},{7,6},{8,7},{9,8},{10,9},{11,1... | collective-permute-start | bytes 786440 | tf_op jit(solution)/shard_map/while/body/eval_jaxpr/ppermute | solution.py:20
  381.7 11.7 %collective-permute-start.1 = (f32[2,32,1024]{2,1,0:T(8,128)S(1)}, f32[2,32,1024]{2,1,0:T(8,128)S(1)}, u32[]{:S(2)}, u32[]{:S(2)}) collective-permute-start(f32[2,32,1024]{2,1,0:T(8,128)S(1)} %get-tuple-element.170), channel_id=1, source_target_pairs={{0,1},{1,2},{2,3},{3,4},{4,5},{5,6},{6,7},{7,8},{8,9},{9,10},{10,1... | collective-permute-start | bytes 786440 | tf_op jit(solution)/shard_map/while/body/eval_jaxpr/ppermute | solution.py:18
  394.6 13.1 %collective-permute-start.2 = (f32[2,32,1024]{2,1,0:T(8,128)S(1)}, f32[2,32,1024]{2,1,0:T(8,128)S(1)}, u32[]{:S(2)}, u32[]{:S(2)}) collective-permute-start(f32[2,32,1024]{2,1,0:T(8,128)S(1)} %get-tuple-element.171), channel_id=1, source_target_pairs={{1,0},{2,1},{3,2},{4,3},{5,4},{6,5},{7,6},{8,7},{9,8},{10,9},{11,1... | collective-permute-start | bytes 786440 | tf_op jit(solution)/shard_map/while/body/eval_jaxpr/ppermute | solution.py:20
  396.5 12.8 %collective-permute-start.3 = (f32[2,32,1024]{2,1,0:T(8,128)S(1)}, f32[2,32,1024]{2,1,0:T(8,128)S(1)}, u32[]{:S(2)}, u32[]{:S(2)}) collective-permute-start(f32[2,32,1024]{2,1,0:T(8,128)S(1)} %get-tuple-element.172), channel_id=1, source_target_pairs={{0,1},{1,2},{2,3},{3,4},{4,5},{5,6},{6,7},{7,8},{8,9},{9,10},{10,1... | collective-permute-start | bytes 786440 | tf_op jit(solution)/shard_map/while/body/eval_jaxpr/ppermute | solution.py:18
  426.7 11.6 %collective-permute-start = (f32[2,32,1024]{2,1,0:T(8,128)S(1)}, f32[2,32,1024]{2,1,0:T(8,128)S(1)}, u32[]{:S(2)}, u32[]{:S(2)}) collective-permute-start(f32[2,32,1024]{2,1,0:T(8,128)S(1)} %get-tuple-element.169), channel_id=1, source_target_pairs={{1,0},{2,1},{3,2},{4,3},{5,4},{6,5},{7,6},{8,7},{9,8},{10,9},{11,1... | collective-permute-start | bytes 786440 | tf_op jit(solution)/shard_map/while/body/eval_jaxpr/ppermute | solution.py:20
  470.3 11.6 %collective-permute-start = (f32[2,32,1024]{2,1,0:T(8,128)S(1)}, f32[2,32,1024]{2,1,0:T(8,128)S(1)}, u32[]{:S(2)}, u32[]{:S(2)}) collective-permute-start(f32[2,32,1024]{2,1,0:T(8,128)S(1)} %get-tuple-element.169), channel_id=1, source_target_pairs={{1,0},{2,1},{3,2},{4,3},{5,4},{6,5},{7,6},{8,7},{9,8},{10,9},{11,1... | collective-permute-start | bytes 786440 | tf_op jit(solution)/shard_map/while/body/eval_jaxpr/ppermute | solution.py:20
  472.2 10.9 %collective-permute-start.1 = (f32[2,32,1024]{2,1,0:T(8,128)S(1)}, f32[2,32,1024]{2,1,0:T(8,128)S(1)}, u32[]{:S(2)}, u32[]{:S(2)}) collective-permute-start(f32[2,32,1024]{2,1,0:T(8,128)S(1)} %get-tuple-element.170), channel_id=1, source_target_pairs={{0,1},{1,2},{2,3},{3,4},{4,5},{5,6},{6,7},{7,8},{8,9},{9,10},{10,1... | collective-permute-start | bytes 786440 | tf_op jit(solution)/shard_map/while/body/eval_jaxpr/ppermute | solution.py:18
  513.9 12.6 %collective-permute-start = (f32[2,32,1024]{2,1,0:T(8,128)S(1)}, f32[2,32,1024]{2,1,0:T(8,128)S(1)}, u32[]{:S(2)}, u32[]{:S(2)}) collective-permute-start(f32[2,32,1024]{2,1,0:T(8,128)S(1)} %get-tuple-element.169), channel_id=1, source_target_pairs={{1,0},{2,1},{3,2},{4,3},{5,4},{6,5},{7,6},{8,7},{9,8},{10,9},{11,1... | collective-permute-start | bytes 786440 | tf_op jit(solution)/shard_map/while/body/eval_jaxpr/ppermute | solution.py:20
  515.9 11.9 %collective-permute-start.1 = (f32[2,32,1024]{2,1,0:T(8,128)S(1)}, f32[2,32,1024]{2,1,0:T(8,128)S(1)}, u32[]{:S(2)}, u32[]{:S(2)}) collective-permute-start(f32[2,32,1024]{2,1,0:T(8,128)S(1)} %get-tuple-element.170), channel_id=1, source_target_pairs={{0,1},{1,2},{2,3},{3,4},{4,5},{5,6},{6,7},{7,8},{8,9},{9,10},{10,1... | collective-permute-start | bytes 786440 | tf_op jit(solution)/shard_map/while/body/eval_jaxpr/ppermute | solution.py:18
  528.9 11.7 %collective-permute-start.2 = (f32[2,32,1024]{2,1,0:T(8,128)S(1)}, f32[2,32,1024]{2,1,0:T(8,128)S(1)}, u32[]{:S(2)}, u32[]{:S(2)}) collective-permute-start(f32[2,32,1024]{2,1,0:T(8,128)S(1)} %get-tuple-element.171), channel_id=1, source_target_pairs={{1,0},{2,1},{3,2},{4,3},{5,4},{6,5},{7,6},{8,7},{9,8},{10,9},{11,1... | collective-permute-start | bytes 786440 | tf_op jit(solution)/shard_map/while/body/eval_jaxpr/ppermute | solution.py:20
  530.9 11.0 %collective-permute-start.3 = (f32[2,32,1024]{2,1,0:T(8,128)S(1)}, f32[2,32,1024]{2,1,0:T(8,128)S(1)}, u32[]{:S(2)}, u32[]{:S(2)}) collective-permute-start(f32[2,32,1024]{2,1,0:T(8,128)S(1)} %get-tuple-element.172), channel_id=1, source_target_pairs={{0,1},{1,2},{2,3},{3,4},{4,5},{5,6},{6,7},{7,8},{8,9},{9,10},{10,1... | collective-permute-start | bytes 786440 | tf_op jit(solution)/shard_map/while/body/eval_jaxpr/ppermute | solution.py:18
  559.2 11.5 %collective-permute-start = (f32[2,32,1024]{2,1,0:T(8,128)S(1)}, f32[2,32,1024]{2,1,0:T(8,128)S(1)}, u32[]{:S(2)}, u32[]{:S(2)}) collective-permute-start(f32[2,32,1024]{2,1,0:T(8,128)S(1)} %get-tuple-element.169), channel_id=1, source_target_pairs={{1,0},{2,1},{3,2},{4,3},{5,4},{6,5},{7,6},{8,7},{9,8},{10,9},{11,1... | collective-permute-start | bytes 786440 | tf_op jit(solution)/shard_map/while/body/eval_jaxpr/ppermute | solution.py:20
  573.0 10.8 %collective-permute-start.2 = (f32[2,32,1024]{2,1,0:T(8,128)S(1)}, f32[2,32,1024]{2,1,0:T(8,128)S(1)}, u32[]{:S(2)}, u32[]{:S(2)}) collective-permute-start(f32[2,32,1024]{2,1,0:T(8,128)S(1)} %get-tuple-element.171), channel_id=1, source_target_pairs={{1,0},{2,1},{3,2},{4,3},{5,4},{6,5},{7,6},{8,7},{9,8},{10,9},{11,1... | collective-permute-start | bytes 786440 | tf_op jit(solution)/shard_map/while/body/eval_jaxpr/ppermute | solution.py:20
  602.6 12.6 %collective-permute-start = (f32[2,32,1024]{2,1,0:T(8,128)S(1)}, f32[2,32,1024]{2,1,0:T(8,128)S(1)}, u32[]{:S(2)}, u32[]{:S(2)}) collective-permute-start(f32[2,32,1024]{2,1,0:T(8,128)S(1)} %get-tuple-element.169), channel_id=1, source_target_pairs={{1,0},{2,1},{3,2},{4,3},{5,4},{6,5},{7,6},{8,7},{9,8},{10,9},{11,1... | collective-permute-start | bytes 786440 | tf_op jit(solution)/shard_map/while/body/eval_jaxpr/ppermute | solution.py:20
  604.6 11.9 %collective-permute-start.1 = (f32[2,32,1024]{2,1,0:T(8,128)S(1)}, f32[2,32,1024]{2,1,0:T(8,128)S(1)}, u32[]{:S(2)}, u32[]{:S(2)}) collective-permute-start(f32[2,32,1024]{2,1,0:T(8,128)S(1)} %get-tuple-element.170), channel_id=1, source_target_pairs={{0,1},{1,2},{2,3},{3,4},{4,5},{5,6},{6,7},{7,8},{8,9},{9,10},{10,1... | collective-permute-start | bytes 786440 | tf_op jit(solution)/shard_map/while/body/eval_jaxpr/ppermute | solution.py:18
  617.7 11.7 %collective-permute-start.2 = (f32[2,32,1024]{2,1,0:T(8,128)S(1)}, f32[2,32,1024]{2,1,0:T(8,128)S(1)}, u32[]{:S(2)}, u32[]{:S(2)}) collective-permute-start(f32[2,32,1024]{2,1,0:T(8,128)S(1)} %get-tuple-element.171), channel_id=1, source_target_pairs={{1,0},{2,1},{3,2},{4,3},{5,4},{6,5},{7,6},{8,7},{9,8},{10,9},{11,1... | collective-permute-start | bytes 786440 | tf_op jit(solution)/shard_map/while/body/eval_jaxpr/ppermute | solution.py:20
  619.6 11.0 %collective-permute-start.3 = (f32[2,32,1024]{2,1,0:T(8,128)S(1)}, f32[2,32,1024]{2,1,0:T(8,128)S(1)}, u32[]{:S(2)}, u32[]{:S(2)}) collective-permute-start(f32[2,32,1024]{2,1,0:T(8,128)S(1)} %get-tuple-element.172), channel_id=1, source_target_pairs={{0,1},{1,2},{2,3},{3,4},{4,5},{5,6},{6,7},{7,8},{8,9},{9,10},{10,1... | collective-permute-start | bytes 786440 | tf_op jit(solution)/shard_map/while/body/eval_jaxpr/ppermute | solution.py:18
  647.9 11.5 %collective-permute-start = (f32[2,32,1024]{2,1,0:T(8,128)S(1)}, f32[2,32,1024]{2,1,0:T(8,128)S(1)}, u32[]{:S(2)}, u32[]{:S(2)}) collective-permute-start(f32[2,32,1024]{2,1,0:T(8,128)S(1)} %get-tuple-element.169), channel_id=1, source_target_pairs={{1,0},{2,1},{3,2},{4,3},{5,4},{6,5},{7,6},{8,7},{9,8},{10,9},{11,1... | collective-permute-start | bytes 786440 | tf_op jit(solution)/shard_map/while/body/eval_jaxpr/ppermute | solution.py:20
  691.4 12.6 %collective-permute-start = (f32[2,32,1024]{2,1,0:T(8,128)S(1)}, f32[2,32,1024]{2,1,0:T(8,128)S(1)}, u32[]{:S(2)}, u32[]{:S(2)}) collective-permute-start(f32[2,32,1024]{2,1,0:T(8,128)S(1)} %get-tuple-element.169), channel_id=1, source_target_pairs={{1,0},{2,1},{3,2},{4,3},{5,4},{6,5},{7,6},{8,7},{9,8},{10,9},{11,1... | collective-permute-start | bytes 786440 | tf_op jit(solution)/shard_map/while/body/eval_jaxpr/ppermute | solution.py:20
  693.3 11.9 %collective-permute-start.1 = (f32[2,32,1024]{2,1,0:T(8,128)S(1)}, f32[2,32,1024]{2,1,0:T(8,128)S(1)}, u32[]{:S(2)}, u32[]{:S(2)}) collective-permute-start(f32[2,32,1024]{2,1,0:T(8,128)S(1)} %get-tuple-element.170), channel_id=1, source_target_pairs={{0,1},{1,2},{2,3},{3,4},{4,5},{5,6},{6,7},{7,8},{8,9},{9,10},{10,1... | collective-permute-start | bytes 786440 | tf_op jit(solution)/shard_map/while/body/eval_jaxpr/ppermute | solution.py:18
  706.4 11.7 %collective-permute-start.2 = (f32[2,32,1024]{2,1,0:T(8,128)S(1)}, f32[2,32,1024]{2,1,0:T(8,128)S(1)}, u32[]{:S(2)}, u32[]{:S(2)}) collective-permute-start(f32[2,32,1024]{2,1,0:T(8,128)S(1)} %get-tuple-element.171), channel_id=1, source_target_pairs={{1,0},{2,1},{3,2},{4,3},{5,4},{6,5},{7,6},{8,7},{9,8},{10,9},{11,1... | collective-permute-start | bytes 786440 | tf_op jit(solution)/shard_map/while/body/eval_jaxpr/ppermute | solution.py:20
  708.3 11.0 %collective-permute-start.3 = (f32[2,32,1024]{2,1,0:T(8,128)S(1)}, f32[2,32,1024]{2,1,0:T(8,128)S(1)}, u32[]{:S(2)}, u32[]{:S(2)}) collective-permute-start(f32[2,32,1024]{2,1,0:T(8,128)S(1)} %get-tuple-element.172), channel_id=1, source_target_pairs={{0,1},{1,2},{2,3},{3,4},{4,5},{5,6},{6,7},{7,8},{8,9},{9,10},{10,1... | collective-permute-start | bytes 786440 | tf_op jit(solution)/shard_map/while/body/eval_jaxpr/ppermute | solution.py:18
  736.6 11.5 %collective-permute-start = (f32[2,32,1024]{2,1,0:T(8,128)S(1)}, f32[2,32,1024]{2,1,0:T(8,128)S(1)}, u32[]{:S(2)}, u32[]{:S(2)}) collective-permute-start(f32[2,32,1024]{2,1,0:T(8,128)S(1)} %get-tuple-element.169), channel_id=1, source_target_pairs={{1,0},{2,1},{3,2},{4,3},{5,4},{6,5},{7,6},{8,7},{9,8},{10,9},{11,1... | collective-permute-start | bytes 786440 | tf_op jit(solution)/shard_map/while/body/eval_jaxpr/ppermute | solution.py:20
  779.9 11.9 %collective-permute-start.25 = (f32[2,32,1024]{2,1,0:T(8,128)S(1)}, f32[2,32,1024]{2,1,0:T(8,128)S(1)}, u32[]{:S(2)}, u32[]{:S(2)}) collective-permute-start(f32[2,32,1024]{2,1,0:T(8,128)S(1)} %get-tuple-element.111), channel_id=1, source_target_pairs={{0,1},{1,2},{2,3},{3,4},{4,5},{5,6},{6,7},{7,8},{8,9},{9,10},{10,1... | collective-permute-start | bytes 786440 | tf_op jit(solution)/shard_map/ppermute | solution.py:18
  786.4 11.6 %collective-permute-start.26 = (f32[2,32,1024]{2,1,0:T(8,128)S(1)}, f32[2,32,1024]{2,1,0:T(8,128)S(1)}, u32[]{:S(2)}, u32[]{:S(2)}) collective-permute-start(f32[2,32,1024]{2,1,0:T(8,128)S(1)} %get-tuple-element.110), channel_id=1, source_target_pairs={{1,0},{2,1},{3,2},{4,3},{5,4},{6,5},{7,6},{8,7},{9,8},{10,9},{11,1... | collective-permute-start | bytes 786440 | tf_op jit(solution)/shard_map/ppermute | solution.py:20
  (70 other events, 644.4 us)
where the time goes:
time: 820 us; the launch traced here: 816 us
  waiting for transfers between devices  345 us (42%)
  starting transfers between devices  335 us (41%)
  other arithmetic  111 us (14%)
  local copies, waits for them, and re-layouts  21.4 us (3%)
    ppermute x39, starting transfers between devices, padded_2(): lax.ppermute(tail, axis, [(i, (i + 1) % count) for i in range(ends)])  212 us
    ppermute x16, waiting for transfers between devices, passed_along(): lax.ppermute(value, axis, [(source, source + steps) for source in range(i...  140 us
    ppermute x39, waiting for transfers between devices, padded_2(): lax.ppermute(head, axis, [((i + 1) % count, i) for i in range(ends)])  138 us
    ppermute x39, starting transfers between devices, padded_2(): lax.ppermute(head, axis, [((i + 1) % count, i) for i in range(ends)])  92 us
    ppermute x39, waiting for transfers between devices, padded_2(): lax.ppermute(tail, axis, [(i, (i + 1) % count) for i in range(ends)])  66.6 us
    div x60, other arithmetic, relax_sweep(): return (right_side[1:-1] + rate_in * neighbours) / (1.0 + 6.0 * rate_in)  36.6 us
    ppermute x16, starting transfers between devices, passed_along(): lax.ppermute(value, axis, [(source, source + steps) for source in range(i...  31.7 us
    select_n x14, other arithmetic, relay_turn(): return jnp.where(owner_index == 0, cpoint, received)  26.6 us
  transfers between devices with their start and end apart: 94, of which 93 were waited for; matrix products, arithmetic and copies ran while one was open for 0% of the time, Pallas kernels for 0%

commit v1 on v0

v1 whole, which is shorter than its diff:
```python
import functools

import jax
import jax.numpy as jnp
from jax import lax
from jax.experimental import pallas as pl
from jax.experimental.pallas import tpu as pltpu
from jax.sharding import Mesh, PartitionSpec as P

SWEEPS = 4
NT = 16
HALO = 16
CHUNK = 64
WIDE = CHUNK + 2 * HALO
PIECE = 8
STRIP = 4
NZD = 8
NSP = 16
LANES = 128
F32 = jnp.float32

VMEM = pl.BlockSpec(memory_space=pltpu.VMEM)
SMEM = pl.BlockSpec(memory_space=pltpu.SMEM)
LIMIT = 48 * 1024 * 1024


def call(kernel, out, specs, scratch=()):
    outs = [jax.ShapeDtypeStruct(s, F32) for s in out]
    return pl.pallas_call(
        kernel,
        out_shape=outs,
        in_specs=specs,
        out_specs=[VMEM] * len(out),
        scratch_shapes=[pltpu.VMEM(s, F32) for s in scratch],
        compiler_params=pltpu.CompilerParams(vmem_limit_bytes=LIMIT),
    )


SNAKE = [x * 4 + (y if x % 2 == 0 else 3 - y) for x in range(4) for y in range(4)]


def chunk_of_space(j):
    x, y = j // 4, j % 4
    return x * 4 + jnp.where(x % 2 == 0, y, 3 - y)


def flat(z, core, j):
    return (z * 2 + core) * NSP + j


def piece_pairs(first):
    path = [
        (z, SNAKE[k])
        for k in range(NSP)
        for z in (range(NZD) if k % 2 == 0 else range(NZD - 1, -1, -1))
    ]
    pairs = []
    for core in (0, 1):
        for q in range(first, len(path) - 1, 2):
            a = flat(path[q][0], core, path[q][1])
            b = flat(path[q + 1][0], core, path[q + 1][1])
            pairs += [(a, b), (b, a)]
    return pairs


def chunk_pairs(first):
    pairs = []
    for k in range(first, NSP - 1, 2):
        a, b = SNAKE[k], SNAKE[k + 1]
        pairs += [(a, b), (b, a)]
    return pairs


def lateral(v):
    n = v.shape[0]
    x = v.reshape(n * 16, LANES)
    lane = lax.broadcasted_iota(jnp.int32, x.shape, 1)
    row = lax.broadcasted_iota(jnp.int32, x.shape, 0) % 16
    zin = lane % 32
    total = jnp.where(zin < 31, pltpu.roll(x, LANES - 1, 1), 0.0)
    total = total + jnp.where(zin > 0, pltpu.roll(x, 1, 1), 0.0)
    rp = pltpu.roll(x, LANES - 32, 1)
    up = jnp.where(row < 15, pltpu.roll(rp, n * 16 - 1, 0), 0.0)
    total = total + jnp.where(lane >= 96, up, rp)
    rm = pltpu.roll(x, 32, 1)
    dn = jnp.where(row > 0, pltpu.roll(rm, 1, 0), 0.0)
    total = total + jnp.where(lane < 32, dn, rm)
    return total.reshape(v.shape)


def swept(v, bb, cc):
    return bb + cc * (lateral(v[1:-1]) + v[2:] + v[:-2])


def prep_kernel(core_ref, c_ref, s_ref, r_ref, o_ref):
    zero = jnp.zeros((HALO, LANES), F32)

    def spread(load, base):
        for m in range(8):
            tile = load(m).T
            for half in range(2):
                k = 2 * m + half
                part = tile[half * 64 : half * 64 + 64]
                o_ref[SNAKE[k], base + HALO : base + HALO + CHUNK] = part
                if k > 0:
                    o_ref[SNAKE[k - 1], base + HALO + CHUNK : base + WIDE] = part[:HALO]
                if k < NSP - 1:
                    o_ref[SNAKE[k + 1], base : base + HALO] = part[CHUNK - HALO :]
        o_ref[SNAKE[0], base : base + HALO] = zero
        o_ref[SNAKE[NSP - 1], base + HALO + CHUNK : base + WIDE] = zero

    spread(lambda m: c_ref[:, m * 128 : (m + 1) * 128], 0)

    @pl.when(core_ref[0] == 0)
    def _():
        spread(lambda m: s_ref[:, m * 128 : (m + 1) * 128], WIDE)

    @pl.when(core_ref[0] != 0)
    def _():
        spread(lambda m: r_ref[:, m * 128 : (m + 1) * 128], WIDE)


def unpack_kernel(a_ref, c_ref, q_ref):
    def one(y, _):
        c_ref[y] = a_ref[pl.ds(y, NSP, stride=2 * WIDE), :]
        q_ref[y] = a_ref[pl.ds(WIDE + y, NSP, stride=2 * WIDE), :]
        return 0

    lax.fori_loop(0, WIDE, one, 0, unroll=8)


def fine_kernel(
    info_ref, c_ref, own_ref, oth_ref, o_ref, inv2_ref, cc2_ref, inv_ref, cc_ref, sinv_ref,
    a_ref, b_ref, bb_ref, rate_ref,
):
    core = info_ref[0]
    odd = info_ref[1]
    sub = info_ref[2]
    step = 8

    def init(n, _):
        at = pl.ds(pl.multiple_of(n * step, step), step)
        own, oth = own_ref[at], oth_ref[at]
        source = jnp.where(core == 0, own, oth)
        rate = jnp.where(core == 0, oth, own)
        inv = 1.0 / (1.0 + 6.0 * rate)
        rate_ref[at] = rate
        inv_ref[at] = inv
        cc_ref[at] = rate * inv
        sinv_ref[at] = source * inv
        a_ref[pl.ds(n * step + 1, step)] = c_ref[at]
        return 0

    lax.fori_loop(0, WIDE // step, init, 0)

    refs = [a_ref, b_ref]
    for number in range(4):
        def right(n, _):
            at = pl.ds(pl.multiple_of(n * step, step), step)
            bb_ref[at] = a_ref[pl.ds(n * step + 1, step)] * inv_ref[at] + sinv_ref[at]
            return 0

        lax.fori_loop(0, WIDE // step, right, 0)
        for sweep in range(SWEEPS):
            src, dst = refs[sweep % 2], refs[(sweep + 1) % 2]
            low = number * SWEEPS + sweep + 1
            blocks = -(-(WIDE - 2 * low) // step)
            start = WIDE // 2 - blocks * step // 2

            def block(n, _, src=src, dst=dst, start=start):
                at = start + n * step
                v = src[pl.ds(at, step + 2)]
                dst[pl.ds(at + 1, step)] = swept(v, bb_ref[pl.ds(at, step)], cc_ref[pl.ds(at, step)])
                return 0

            lax.fori_loop(0, blocks, block, 0)
        if number % 2 == 1:
            for z in range(NZD):
                part = jnp.where(odd == 1, NZD - 1 - z, z)
                o_ref[z, number // 2] = a_ref[pl.ds(HALO + 1 + PIECE * part, PIECE)]

    rate = 2.0 * rate_ref[pl.ds(HALO - PIECE + PIECE * sub, 3 * PIECE)]
    inv = 1.0 / (1.0 + 6.0 * rate)
    inv2_ref[...] = inv
    cc2_ref[...] = rate * inv


def messages(odd, e, r_next, a_ref, b_ref):
    head, tail = r_next[:STRIP], r_next[STRIP:]
    a_ref[:PIECE] = e
    b_ref[:PIECE] = e
    a_ref[PIECE:] = jnp.where(odd == 0, tail, head)
    b_ref[PIECE:] = jnp.where(odd == 0, head, tail)


def residual_kernel(info_ref, own_ref, oth_ref, r_ref, cp_ref, mine_ref, a_ref, b_ref):
    core, odd = info_ref[0], info_ref[3]

    def uw(t, which):
        mine, other = own_ref[t // 2, which], oth_ref[t // 2, which]
        return jnp.where(core == t % 2, mine, other)

    r_ref[0] = jnp.zeros(r_ref.shape[1:], F32)
    r_ref[1] = uw(0, 0) - uw(0, 0)
    for t in range(2, NT):
        r_ref[t] = uw(t - 2, 1) - uw(t - 1, 0)
    for n in range(NT // 2):
        even_cp = oth_ref[max(n - 1, 0), 0]
        cp_ref[n] = jnp.where(core == 0, even_cp, oth_ref[n, 0])
        mine_ref[n] = jnp.where(core == 0, r_ref[2 * n], r_ref[2 * n + 1])
    messages(odd, r_ref[1], r_ref[2], a_ref, b_ref)


def coarse_step(v, inv, cc):
    bb = v * inv
    for sweep in range(SWEEPS):
        low = sweep + 1
        high = bb.shape[0] - low
        v = swept(v, bb[low:high], cc[low:high])
    return v


def chain_kernel(t, info_ref, ra_ref, rb_ref, e_ref, r_ref, inv_ref, cc_ref, e1_ref, e2_ref, *out):
    odd = info_ref[3]
    ra, rb = ra_ref[...], rb_ref[...]
    left = jnp.where(odd == 0, rb, ra)
    right = jnp.where(odd == 0, ra, rb)
    e = jnp.concatenate([left[:PIECE], e_ref[...], right[:PIECE]], 0)
    r1 = jnp.concatenate([left[PIECE:], r_ref[t + 1], right[PIECE:]], 0)
    inv, cc = inv_ref[...], cc_ref[...]
    e1 = coarse_step(e, inv, cc) + r1
    e2 = coarse_step(e1, inv[STRIP:-STRIP], cc[STRIP:-STRIP]) + r_ref[t + 2]
    e1_ref[...] = e1[STRIP:-STRIP]
    e2_ref[...] = e2
    if out:
        messages(odd, e2, r_ref[t + 3], *out)


def correct_kernel(info_ref, cp_ref, r_ref, *refs):
    core = info_ref[0]
    e_refs, o_ref = refs[:-1], refs[-1]
    for n in range(NT // 2):
        even = e_refs[2 * n - 1][...] if n > 0 else jnp.zeros(cp_ref.shape[1:], F32)
        o_ref[n, 0] = cp_ref[n] + jnp.where(core == 0, even, e_refs[2 * n][...])
        o_ref[n, 1] = r_ref[n]


def last_kernel(info_ref, g_ref, c_ref, ra_ref, rb_ref, inv_ref, cc_ref, sinv_ref, o_ref, a_ref, b_ref, bb_ref):
    odd, first = info_ref[1], info_ref[4]
    size = CHUNK + 2 * STRIP
    step = 8
    for n in range(NZD):
        z = jnp.where(odd == 1, NZD - 1 - n, n)
        c = c_ref[HALO + n * PIECE : HALO + n * PIECE + PIECE]
        a_ref[1 + STRIP + n * PIECE : 1 + STRIP + (n + 1) * PIECE] = jnp.where(first == 1, c, g_ref[z, 0])
        for y in range(PIECE):
            o_ref[pl.ds(2 * CHUNK + n * PIECE + y, NSP, stride=3 * CHUNK), :] = g_ref[z, 1, y]
    a_ref[1 : 1 + STRIP] = jnp.where(odd == 0, rb_ref[...], ra_ref[...])
    a_ref[1 + STRIP + CHUNK : 1 + size] = jnp.where(odd == 0, ra_ref[...], rb_ref[...])

    off = HALO - STRIP

    def right(n, _):
        at = n * step
        v = a_ref[pl.ds(at + 1, step)]
        bb_ref[pl.ds(at, step)] = v * inv_ref[pl.ds(off + at, step)] + sinv_ref[pl.ds(off + at, step)]
        return 0

    lax.fori_loop(0, size // step, right, 0)

    def keep(which):
        def one(y, _):
            o_ref[pl.ds(which * CHUNK + y, NSP, stride=3 * CHUNK), :] = a_ref[1 + STRIP + y]
            return 0

        lax.fori_loop(0, CHUNK, one, 0, unroll=8)

    keep(0)
    refs = [a_ref, b_ref]
    for sweep in range(SWEEPS):
        src, dst = refs[sweep % 2], refs[(sweep + 1) % 2]
        blocks = -(-(size - 2 * (sweep + 1)) // step)
        start = size // 2 - blocks * step // 2

        def block(n, _, src=src, dst=dst, start=start):
            at = start + n * step
            v = src[pl.ds(at, step + 2)]
            dst[pl.ds(at + 1, step)] = swept(
                v, bb_ref[pl.ds(at, step)], cc_ref[pl.ds(off + at, step)]
            )
            return 0

        lax.fori_loop(0, blocks, block, 0)
    keep(1)


def finish_kernel(a_ref, f_ref, r_ref):
    outs = [f_ref.at[0], f_ref.at[1], r_ref]
    for which in range(3):
        for m in range(8):
            low = a_ref[SNAKE[2 * m], which * CHUNK : (which + 1) * CHUNK]
            high = a_ref[SNAKE[2 * m + 1], which * CHUNK : (which + 1) * CHUNK]
            outs[which][:, m * 128 : (m + 1) * 128] = jnp.concatenate([low, high], 0).T


def body(c_guess, source, rate):
    z = lax.axis_index("z")
    core = lax.axis_index("core")
    k = chunk_of_space(lax.axis_index("space"))
    odd_chunk = k % 2
    sub = jnp.where(odd_chunk == 1, NZD - 1 - z, z)
    first = jnp.where((z == 0) & (core == 0), 1, 0)
    info = jnp.stack([core, odd_chunk, sub, sub % 2, first]).astype(jnp.int32)
    everyone = ("z", "core", "space")

    def swap(v):
        return lax.ppermute(v, "core", [(0, 1), (1, 0)])

    plane = (16, LANES)

    sent = call(prep_kernel, [(NSP, 2 * WIDE, LANES)], [SMEM] + [VMEM] * 3)(
        info, c_guess.reshape(LANES, -1), source.reshape(LANES, -1), rate.reshape(LANES, -1)
    )[0]
    got = lax.all_to_all(sent, "space", 0, 0)
    c, own = call(unpack_kernel, [(WIDE,) + plane] * 2, [VMEM])(got.reshape(-1, LANES))
    oth = swap(own)

    uw, inv2, cc2, inv, cc, sinv = call(
        fine_kernel,
        [(NZD, 2, PIECE) + plane] + [(3 * PIECE,) + plane] * 2 + [(WIDE,) + plane] * 3,
        [SMEM] + [VMEM] * 3,
        [(WIDE + 2,) + plane] * 2 + [(WIDE,) + plane] * 2,
    )(info, c, own, oth)

    mine = lax.all_to_all(uw, "z", 0, 0)
    other = swap(mine)
    piece = (PIECE,) + plane
    message = (PIECE + STRIP,) + plane
    res, cpoint, res_mine, ma, mb = call(
        residual_kernel,
        [(NT,) + piece, (NT // 2,) + piece, (NT // 2,) + piece, message, message],
        [SMEM] + [VMEM] * 2,
    )(info, mine, other)

    errors = [res[1]]
    pairs_a, pairs_b = piece_pairs(0), piece_pairs(1)
    for t in range(1, NT - 1, 2):
        ra = lax.ppermute(ma, everyone, pairs_a)
        rb = lax.ppermute(mb, everyone, pairs_b)
        last = t + 2 == NT - 1
        made = call(
            functools.partial(chain_kernel, t),
            [piece, piece] + ([] if last else [message, message]),
            [SMEM] + [VMEM] * 6,
        )(info, ra, rb, errors[-1], res, inv2, cc2)
        errors += made[:2]
        if not last:
            ma, mb = made[2:]

    corrected = call(
        correct_kernel, [(NZD, 2) + piece], [SMEM] + [VMEM] * (2 + len(errors))
    )(info, cpoint, res_mine, *errors)[0]
    chunk = lax.all_to_all(corrected, "z", 0, 0)
    head = jnp.where(odd_chunk == 0, chunk[0, 0, :STRIP], chunk[NZD - 1, 0, :STRIP])
    tail = jnp.where(odd_chunk == 0, chunk[NZD - 1, 0, STRIP:], chunk[0, 0, STRIP:])
    head = jnp.where(first == 1, c[HALO : HALO + STRIP], head)
    tail = jnp.where(first == 1, c[HALO + CHUNK - STRIP : HALO + CHUNK], tail)
    ra = lax.ppermute(jnp.where(odd_chunk == 0, tail, head), "space", chunk_pairs(0))
    rb = lax.ppermute(jnp.where(odd_chunk == 0, head, tail), "space", chunk_pairs(1))
    size = CHUNK + 2 * STRIP
    sent = call(
        last_kernel,
        [(NSP * 3 * CHUNK, LANES)],
        [SMEM] + [VMEM] * 7,
        [(size + 2,) + plane] * 2 + [(size,) + plane],
    )(info, chunk, c, ra, rb, inv, cc, sinv)[0]
    got = lax.all_to_all(sent.reshape(NSP, 3 * CHUNK, LANES), "space", 0, 0)
    fine, residual = call(finish_kernel, [(2, LANES, 1024), (LANES, 1024)], [VMEM])(got)
    return fine.reshape(1, 2, 4, 32, 1024), residual.reshape(1, 4, 32, 1024)


def solution(mesh):
    inner = Mesh(mesh.devices.reshape(NZD, 2, NSP), ("z", "core", "space"))
    tm = ("z", "core")
    return jax.shard_map(
        body,
        mesh=inner,
        in_specs=(P(tm, "space", None, None), P("space", None, None), P("space", None, None)),
        out_specs=(P(tm, None, "space", None, None), P(tm, "space", None, None)),
        check_vma=False,
    )
```

time: 820 us -> 239 us (0.29)
  the two profiles are of different devices: /device:TPU:88 before, /device:TPU:8 now
where the time goes in v1:
time: 239 us; the launch traced here: 235 us
  blocking collectives  84.3 us (35%)
  Pallas kernels  52.7 us (22%)
  waiting for transfers between devices  52.4 us (22%)
  starting transfers between devices  39.9 us (17%)
  local copies, waits for them, and re-layouts  5.23 us (2%)
    all_to_all x1, blocking collectives, body(): mine = lax.all_to_all(uw, 'z', 0, 0)  37.3 us
    all_to_all x1, blocking collectives, body(): got = lax.all_to_all(sent, 'space', 0, 0)  28.3 us
    pallas_call x1, Pallas kernels, body(): call(fine_kernel, [(NZD, 2, PIECE) + plane] + [(3 * PIECE,) + plane] * 2...  25.4 us
    ppermute x7, waiting for transfers between devices, body(): rb = lax.ppermute(mb, everyone, pairs_b)  20.9 us
    ppermute x7, starting transfers between devices, body(): rb = lax.ppermute(mb, everyone, pairs_b)  20.5 us
    all_to_all x1, waiting for transfers between devices, body(): chunk = lax.all_to_all(corrected, 'z', 0, 0)  19 us
    all_to_all x1, blocking collectives, body(): got = lax.all_to_all(sent.reshape(NSP, 3 * CHUNK, LANES), 'space', 0, 0)  18.8 us
    pallas_call x7, Pallas kernels, body(): call(functools.partial(chain_kernel, t), [piece, piece] + ([] if last els...  14.4 us
  transfers between devices with their start and end apart: 19, of which 17 were waited for; matrix products, arithmetic and copies ran while one was open for 0% of the time, Pallas kernels for 0%

profile of v1, /device:TPU:8, one launch (start us, length us, event | category | flops | bytes accessed | tf_op | source)
XLA Modules:
  0.0 235.4 jit_solution(9741870248117473876)
XLA Ops:
  0.8 1.0 copy-done.2
  1.8 1.0 copy-done.3
  2.9 1.0 copy-done.4
  4.8 28.3 %all_to_all.20 = f32[16,192,128]{2,1,0:T(8,128)S(1)} all-to-all(f32[16,192,128]{2,1,0:T(8,128)S(1)} %shard_map.50), channel_id=1, replica_groups=mesh['z'=8,'core'=2,'space'=16] {'space'}, dimensions={0} | all-to-all | bytes 3145728 | tf_op jit(solution)/shard_map/all_to_all | solution.py:324
  33.1 1.0 shard_map.51
  34.1 2.3 collective-permute-done.oth_ref
  36.4 25.4 %shard_map.52 = (f32[8,2,8,16,128]{4,3,2,1,0:T(8,128)S(1)}, f32[24,16,128]{2,1,0:T(8,128)S(1)}, f32[24,16,128]{2,1,0:T(8,128)S(1)}, f32[96,16,128]{2,1,0:T(8,128...) custom-call(s32[5]{0:T(128)S(1)} %stack.23.core_ref.info_ref, f32[96,16,128]{2,1,0:T(8,128)S(1)} %get-tuple-element.43.c_ref, ...), custom_call_target="tpu_custom_call" | custom-call | tf_op jit(solution)/shard_map/pallas_call | solution.py:328
  61.9 0.9 copy-done
  62.7 37.3 %all_to_all.21.own_ref = f32[8,2,8,16,128]{4,3,2,1,0:T(8,128)S(1)} all-to-all(f32[8,2,8,16,128]{4,3,2,1,0:T(8,128)S(1)} %get-tuple-element.45), channel_id=1, replica_groups=mesh['z'=8,'core'=2,'space'=16] {'z'}, dimensions={0} | all-to-all | bytes 2097152 | tf_op jit(solution)/shard_map/all_to_all | solution.py:335
  100.0 2.7 %collective-permute-done.1.oth_ref = f32[8,2,8,16,128]{4,3,2,1,0:T(8,128)S(1)} collective-permute-done((f32[8,2,8,16,128]{4,3,2,1,0:T(8,128)S(1)}, f32[8,2,8,16,128]{4,3,2,1,0:T(8,128)S(1)}, u32[]{:S(2)}, u32[]{:S(2)}) %collective-permute-start.1) | collective-permute-done | bytes 1048608 | tf_op jit(solution)/shard_map/ppermute | solution.py:317
  104.2 2.9 %collective-permute-start.3 = (f32[12,16,128]{2,1,0:T(8,128)S(1)}, f32[12,16,128]{2,1,0:T(8,128)S(1)}, u32[]{:S(2)}, u32[]{:S(2)}) collective-permute-start(f32[12,16,128]{2,1,0:T(8,128)S(1)} %get-tuple-element.50), channel_id=1, source_target_pairs={{32,64},{64,32},{96,128},{128,96},{160,192},{192,160},{224,225},{2... | collective-permute-start | bytes 294920 | tf_op jit(solution)/shard_map/ppermute | solution.py:349
  107.1 1.3 collective-permute-done.2.ra_ref
  108.4 2.2 collective-permute-done.3.rb_ref
  110.7 2.1 shard_map.54
  112.7 1.5 collective-permute-start.4
  114.3 2.9 %collective-permute-start.5 = (f32[12,16,128]{2,1,0:T(8,128)S(1)}, f32[12,16,128]{2,1,0:T(8,128)S(1)}, u32[]{:S(2)}, u32[]{:S(2)}) collective-permute-start(f32[12,16,128]{2,1,0:T(8,128)S(1)} %get-tuple-element.56), channel_id=1, source_target_pairs={{32,64},{64,32},{96,128},{128,96},{160,192},{192,160},{224,225},{2... | collective-permute-start | bytes 294920 | tf_op jit(solution)/shard_map/ppermute | solution.py:349
  117.4 3.3 %collective-permute-done.5.rb_ref = f32[12,16,128]{2,1,0:T(8,128)S(1)} collective-permute-done((f32[12,16,128]{2,1,0:T(8,128)S(1)}, f32[12,16,128]{2,1,0:T(8,128)S(1)}, u32[]{:S(2)}, u32[]{:S(2)}) %collective-permute-start.5) | collective-permute-done | bytes 98336 | tf_op jit(solution)/shard_map/ppermute | solution.py:349
  120.8 2.1 shard_map.55
  123.5 2.9 %collective-permute-start.7 = (f32[12,16,128]{2,1,0:T(8,128)S(1)}, f32[12,16,128]{2,1,0:T(8,128)S(1)}, u32[]{:S(2)}, u32[]{:S(2)}) collective-permute-start(f32[12,16,128]{2,1,0:T(8,128)S(1)} %get-tuple-element.60), channel_id=1, source_target_pairs={{32,64},{64,32},{96,128},{128,96},{160,192},{192,160},{224,225},{2... | collective-permute-start | bytes 294920 | tf_op jit(solution)/shard_map/ppermute | solution.py:349
  126.4 1.1 collective-permute-done.6.ra_ref
  127.5 2.4 %collective-permute-done.7.rb_ref = f32[12,16,128]{2,1,0:T(8,128)S(1)} collective-permute-done((f32[12,16,128]{2,1,0:T(8,128)S(1)}, f32[12,16,128]{2,1,0:T(8,128)S(1)}, u32[]{:S(2)}, u32[]{:S(2)}) %collective-permute-start.7) | collective-permute-done | bytes 98336 | tf_op jit(solution)/shard_map/ppermute | solution.py:349
  130.0 2.1 shard_map.56
  132.0 1.5 collective-permute-start.8
  133.6 2.9 %collective-permute-start.9 = (f32[12,16,128]{2,1,0:T(8,128)S(1)}, f32[12,16,128]{2,1,0:T(8,128)S(1)}, u32[]{:S(2)}, u32[]{:S(2)}) collective-permute-start(f32[12,16,128]{2,1,0:T(8,128)S(1)} %get-tuple-element.64), channel_id=1, source_target_pairs={{32,64},{64,32},{96,128},{128,96},{160,192},{192,160},{224,225},{2... | collective-permute-start | bytes 294920 | tf_op jit(solution)/shard_map/ppermute | solution.py:349
  136.7 3.3 %collective-permute-done.9.rb_ref = f32[12,16,128]{2,1,0:T(8,128)S(1)} collective-permute-done((f32[12,16,128]{2,1,0:T(8,128)S(1)}, f32[12,16,128]{2,1,0:T(8,128)S(1)}, u32[]{:S(2)}, u32[]{:S(2)}) %collective-permute-start.9) | collective-permute-done | bytes 98336 | tf_op jit(solution)/shard_map/ppermute | solution.py:349
  140.1 2.1 shard_map.57
  142.1 1.1 collective-permute-start.10
  143.2 2.9 %collective-permute-start.11 = (f32[12,16,128]{2,1,0:T(8,128)S(1)}, f32[12,16,128]{2,1,0:T(8,128)S(1)}, u32[]{:S(2)}, u32[]{:S(2)}) collective-permute-start(f32[12,16,128]{2,1,0:T(8,128)S(1)} %get-tuple-element.68), channel_id=1, source_target_pairs={{32,64},{64,32},{96,128},{128,96},{160,192},{192,160},{224,225},{2... | collective-permute-start | bytes 294920 | tf_op jit(solution)/shard_map/ppermute | solution.py:349
  147.0 2.7 %collective-permute-done.11.rb_ref = f32[12,16,128]{2,1,0:T(8,128)S(1)} collective-permute-done((f32[12,16,128]{2,1,0:T(8,128)S(1)}, f32[12,16,128]{2,1,0:T(8,128)S(1)}, u32[]{:S(2)}, u32[]{:S(2)}) %collective-permute-start.11) | collective-permute-done | bytes 98336 | tf_op jit(solution)/shard_map/ppermute | solution.py:349
  149.7 2.1 shard_map.58
  151.8 1.9 collective-permute-start.12
  153.7 2.9 %collective-permute-start.13 = (f32[12,16,128]{2,1,0:T(8,128)S(1)}, f32[12,16,128]{2,1,0:T(8,128)S(1)}, u32[]{:S(2)}, u32[]{:S(2)}) collective-permute-start(f32[12,16,128]{2,1,0:T(8,128)S(1)} %get-tuple-element.72), channel_id=1, source_target_pairs={{32,64},{64,32},{96,128},{128,96},{160,192},{192,160},{224,225},{2... | collective-permute-start | bytes 294920 | tf_op jit(solution)/shard_map/ppermute | solution.py:349
  156.7 3.6 %collective-permute-done.13.rb_ref = f32[12,16,128]{2,1,0:T(8,128)S(1)} collective-permute-done((f32[12,16,128]{2,1,0:T(8,128)S(1)}, f32[12,16,128]{2,1,0:T(8,128)S(1)}, u32[]{:S(2)}, u32[]{:S(2)}) %collective-permute-start.13) | collective-permute-done | bytes 98336 | tf_op jit(solution)/shard_map/ppermute | solution.py:349
  160.2 2.1 shard_map.59
  162.3 1.5 collective-permute-start.14
  163.8 2.9 %collective-permute-start.15 = (f32[12,16,128]{2,1,0:T(8,128)S(1)}, f32[12,16,128]{2,1,0:T(8,128)S(1)}, u32[]{:S(2)}, u32[]{:S(2)}) collective-permute-start(f32[12,16,128]{2,1,0:T(8,128)S(1)} %get-tuple-element.76), channel_id=1, source_target_pairs={{32,64},{64,32},{96,128},{128,96},{160,192},{192,160},{224,225},{2... | collective-permute-start | bytes 294920 | tf_op jit(solution)/shard_map/ppermute | solution.py:349
  167.0 3.3 %collective-permute-done.15.rb_ref = f32[12,16,128]{2,1,0:T(8,128)S(1)} collective-permute-done((f32[12,16,128]{2,1,0:T(8,128)S(1)}, f32[12,16,128]{2,1,0:T(8,128)S(1)}, u32[]{:S(2)}, u32[]{:S(2)}) %collective-permute-start.15) | collective-permute-done | bytes 98336 | tf_op jit(solution)/shard_map/ppermute | solution.py:349
  170.3 2.0 shard_map.60
  172.3 1.6 shard_map.61
  174.0 6.4 %all-to-all-start.2 = ((f32[8,2,8,16,128]{4,3,2,1,0:T(8,128)}), f32[8,2,8,16,128]{4,3,2,1,0:T(8,128)S(1)}, u32[]{:S(2)}, u32[]{:S(2)}) async-start(f32[8,2,8,16,128]{4,3,2,1,0:T(8,128)} %shard_map.61), calls=%async_computation.2 | async-start | bytes 2097152 | tf_op jit(solution)/shard_map/all_to_all | solution.py:363
  180.4 19.0 %all-to-all-done.2.g_ref = f32[8,2,8,16,128]{4,3,2,1,0:T(8,128)S(1)} async-done(((f32[8,2,8,16,128]{4,3,2,1,0:T(8,128)}), f32[8,2,8,16,128]{4,3,2,1,0:T(8,128)S(1)}, u32[]{:S(2)}, u32[]{:S(2)}) %all-to-all-start.2) | async-done | bytes 1048608 | tf_op jit(solution)/shard_map/all_to_all | solution.py:363
  199.4 1.7 collective-permute-start.16
  201.2 2.3 collective-permute-start.17
  203.4 3.5 %collective-permute-done.17.rb_ref = f32[4,16,128]{2,1,0:T(8,128)S(1)} collective-permute-done((f32[4,16,128]{2,1,0:T(8,128)S(1)}, f32[4,16,128]{2,1,0:T(8,128)S(1)}, u32[]{:S(2)}, u32[]{:S(2)}) %collective-permute-start.17) | collective-permute-done | bytes 32800 | tf_op jit(solution)/shard_map/ppermute | solution.py:369
  207.0 1.1 copy-done.1
  208.1 7.1 %shard_map.62 = f32[3072,128]{1,0:T(8,128)S(1)} custom-call(s32[5]{0:T(128)S(1)} %stack.23.core_ref.info_ref, f32[8,2,8,16,128]{4,3,2,1,0:T(8,128)S(1)} %all-to-all-done.2.g_ref, f32[96,16,128]{2,1,0:T(8,128)S(1)} %get-tuple-element.43.c_ref, f32[4,16,128]{2,1,0:T(8,128)S(1)} %collective-permute-done.16.ra_ref, ...), custom_call_target="tpu_custom_call" | custom-call | tf_op jit(solution)/shard_map/pallas_call | solution.py:371
  215.2 18.8 %all_to_all.22.a_ref = f32[16,192,128]{2,1,0:T(8,128)S(1)} all-to-all(f32[16,192,128]{2,1,0:T(8,128)S(1)} %bitcast.25), channel_id=1, replica_groups=mesh['z'=8,'core'=2,'space'=16] {'space'}, dimensions={0} | all-to-all | bytes 3145728 | tf_op jit(solution)/shard_map/all_to_all | solution.py:377
  234.0 1.5 shard_map.63
  (21 shorter events, 4.8 us)
Async XLA Ops:
  0.8 1.0 copy-start.2
  1.8 1.0 copy-start.3
  2.9 1.0 copy-start.4
  34.0 2.4 %collective-permute-start = (f32[96,16,128]{2,1,0:T(8,128)S(1)}, f32[96,16,128]{2,1,0:T(8,128)S(1)}, u32[]{:S(2)}, u32[]{:S(2)}) collective-permute-start(f32[96,16,128]{2,1,0:T(8,128)S(1)} %get-tuple-element.44.own_ref), channel_id=1, source_target_pairs={{0,16},{16,0},{1,17},{17,1},{2,18},{18,2},{3,19},{19,3},{4,20},{20... | collective-permute-start | bytes 2359304 | tf_op jit(solution)/shard_map/ppermute | solution.py:317
  61.8 0.9 copy-start
  100.0 2.7 %collective-permute-start.1 = (f32[8,2,8,16,128]{4,3,2,1,0:T(8,128)S(1)}, f32[8,2,8,16,128]{4,3,2,1,0:T(8,128)S(1)}, u32[]{:S(2)}, u32[]{:S(2)}) collective-permute-start(f32[8,2,8,16,128]{4,3,2,1,0:T(8,128)S(1)} %all_to_all.21.own_ref), channel_id=1, source_target_pairs={{0,16},{16,0},{1,17},{17,1},{2,18},{18,2},{3,19},{19,3},{4,20},{20... | collective-permute-start | bytes 3145736 | tf_op jit(solution)/shard_map/ppermute | solution.py:317
  103.5 4.9 %collective-permute-start.2 = (f32[12,16,128]{2,1,0:T(8,128)S(1)}, f32[12,16,128]{2,1,0:T(8,128)S(1)}, u32[]{:S(2)}, u32[]{:S(2)}) collective-permute-start(f32[12,16,128]{2,1,0:T(8,128)S(1)} %get-tuple-element.49), channel_id=1, source_target_pairs={{0,32},{32,0},{64,96},{96,64},{128,160},{160,128},{192,224},{224,1... | collective-permute-start | bytes 294920 | tf_op jit(solution)/shard_map/ppermute | solution.py:348
  104.2 6.5 %collective-permute-start.3 = (f32[12,16,128]{2,1,0:T(8,128)S(1)}, f32[12,16,128]{2,1,0:T(8,128)S(1)}, u32[]{:S(2)}, u32[]{:S(2)}) collective-permute-start(f32[12,16,128]{2,1,0:T(8,128)S(1)} %get-tuple-element.50), channel_id=1, source_target_pairs={{32,64},{64,32},{96,128},{128,96},{160,192},{192,160},{224,225},{2... | collective-permute-start | bytes 294920 | tf_op jit(solution)/shard_map/ppermute | solution.py:349
  112.7 4.7 %collective-permute-start.4 = (f32[12,16,128]{2,1,0:T(8,128)S(1)}, f32[12,16,128]{2,1,0:T(8,128)S(1)}, u32[]{:S(2)}, u32[]{:S(2)}) collective-permute-start(f32[12,16,128]{2,1,0:T(8,128)S(1)} %get-tuple-element.55), channel_id=1, source_target_pairs={{0,32},{32,0},{64,96},{96,64},{128,160},{160,128},{192,224},{224,1... | collective-permute-start | bytes 294920 | tf_op jit(solution)/shard_map/ppermute | solution.py:348
  114.3 6.5 %collective-permute-start.5 = (f32[12,16,128]{2,1,0:T(8,128)S(1)}, f32[12,16,128]{2,1,0:T(8,128)S(1)}, u32[]{:S(2)}, u32[]{:S(2)}) collective-permute-start(f32[12,16,128]{2,1,0:T(8,128)S(1)} %get-tuple-element.56), channel_id=1, source_target_pairs={{32,64},{64,32},{96,128},{128,96},{160,192},{192,160},{224,225},{2... | collective-permute-start | bytes 294920 | tf_op jit(solution)/shard_map/ppermute | solution.py:349
  122.8 4.7 %collective-permute-start.6 = (f32[12,16,128]{2,1,0:T(8,128)S(1)}, f32[12,16,128]{2,1,0:T(8,128)S(1)}, u32[]{:S(2)}, u32[]{:S(2)}) collective-permute-start(f32[12,16,128]{2,1,0:T(8,128)S(1)} %get-tuple-element.59), channel_id=1, source_target_pairs={{0,32},{32,0},{64,96},{96,64},{128,160},{160,128},{192,224},{224,1... | collective-permute-start | bytes 294920 | tf_op jit(solution)/shard_map/ppermute | solution.py:348
  123.5 6.5 %collective-permute-start.7 = (f32[12,16,128]{2,1,0:T(8,128)S(1)}, f32[12,16,128]{2,1,0:T(8,128)S(1)}, u32[]{:S(2)}, u32[]{:S(2)}) collective-permute-start(f32[12,16,128]{2,1,0:T(8,128)S(1)} %get-tuple-element.60), channel_id=1, source_target_pairs={{32,64},{64,32},{96,128},{128,96},{160,192},{192,160},{224,225},{2... | collective-permute-start | bytes 294920 | tf_op jit(solution)/shard_map/ppermute | solution.py:349
  132.0 4.7 %collective-permute-start.8 = (f32[12,16,128]{2,1,0:T(8,128)S(1)}, f32[12,16,128]{2,1,0:T(8,128)S(1)}, u32[]{:S(2)}, u32[]{:S(2)}) collective-permute-start(f32[12,16,128]{2,1,0:T(8,128)S(1)} %get-tuple-element.63), channel_id=1, source_target_pairs={{0,32},{32,0},{64,96},{96,64},{128,160},{160,128},{192,224},{224,1... | collective-permute-start | bytes 294920 | tf_op jit(solution)/shard_map/ppermute | solution.py:348
  133.6 6.5 %collective-permute-start.9 = (f32[12,16,128]{2,1,0:T(8,128)S(1)}, f32[12,16,128]{2,1,0:T(8,128)S(1)}, u32[]{:S(2)}, u32[]{:S(2)}) collective-permute-start(f32[12,16,128]{2,1,0:T(8,128)S(1)} %get-tuple-element.64), channel_id=1, source_target_pairs={{32,64},{64,32},{96,128},{128,96},{160,192},{192,160},{224,225},{2... | collective-permute-start | bytes 294920 | tf_op jit(solution)/shard_map/ppermute | solution.py:349
  142.1 4.9 %collective-permute-start.10 = (f32[12,16,128]{2,1,0:T(8,128)S(1)}, f32[12,16,128]{2,1,0:T(8,128)S(1)}, u32[]{:S(2)}, u32[]{:S(2)}) collective-permute-start(f32[12,16,128]{2,1,0:T(8,128)S(1)} %get-tuple-element.67), channel_id=1, source_target_pairs={{0,32},{32,0},{64,96},{96,64},{128,160},{160,128},{192,224},{224,1... | collective-permute-start | bytes 294920 | tf_op jit(solution)/shard_map/ppermute | solution.py:348
  143.2 6.5 %collective-permute-start.11 = (f32[12,16,128]{2,1,0:T(8,128)S(1)}, f32[12,16,128]{2,1,0:T(8,128)S(1)}, u32[]{:S(2)}, u32[]{:S(2)}) collective-permute-start(f32[12,16,128]{2,1,0:T(8,128)S(1)} %get-tuple-element.68), channel_id=1, source_target_pairs={{32,64},{64,32},{96,128},{128,96},{160,192},{192,160},{224,225},{2... | collective-permute-start | bytes 294920 | tf_op jit(solution)/shard_map/ppermute | solution.py:349
  151.8 4.9 %collective-permute-start.12 = (f32[12,16,128]{2,1,0:T(8,128)S(1)}, f32[12,16,128]{2,1,0:T(8,128)S(1)}, u32[]{:S(2)}, u32[]{:S(2)}) collective-permute-start(f32[12,16,128]{2,1,0:T(8,128)S(1)} %get-tuple-element.71), channel_id=1, source_target_pairs={{0,32},{32,0},{64,96},{96,64},{128,160},{160,128},{192,224},{224,1... | collective-permute-start | bytes 294920 | tf_op jit(solution)/shard_map/ppermute | solution.py:348
  153.7 6.5 %collective-permute-start.13 = (f32[12,16,128]{2,1,0:T(8,128)S(1)}, f32[12,16,128]{2,1,0:T(8,128)S(1)}, u32[]{:S(2)}, u32[]{:S(2)}) collective-permute-start(f32[12,16,128]{2,1,0:T(8,128)S(1)} %get-tuple-element.72), channel_id=1, source_target_pairs={{32,64},{64,32},{96,128},{128,96},{160,192},{192,160},{224,225},{2... | collective-permute-start | bytes 294920 | tf_op jit(solution)/shard_map/ppermute | solution.py:349
  162.3 4.7 %collective-permute-start.14 = (f32[12,16,128]{2,1,0:T(8,128)S(1)}, f32[12,16,128]{2,1,0:T(8,128)S(1)}, u32[]{:S(2)}, u32[]{:S(2)}) collective-permute-start(f32[12,16,128]{2,1,0:T(8,128)S(1)} %get-tuple-element.75), channel_id=1, source_target_pairs={{0,32},{32,0},{64,96},{96,64},{128,160},{160,128},{192,224},{224,1... | collective-permute-start | bytes 294920 | tf_op jit(solution)/shard_map/ppermute | solution.py:348
  163.8 6.5 %collective-permute-start.15 = (f32[12,16,128]{2,1,0:T(8,128)S(1)}, f32[12,16,128]{2,1,0:T(8,128)S(1)}, u32[]{:S(2)}, u32[]{:S(2)}) collective-permute-start(f32[12,16,128]{2,1,0:T(8,128)S(1)} %get-tuple-element.76), channel_id=1, source_target_pairs={{32,64},{64,32},{96,128},{128,96},{160,192},{192,160},{224,225},{2... | collective-permute-start | bytes 294920 | tf_op jit(solution)/shard_map/ppermute | solution.py:349
  174.0 25.4 %all-to-all-start.2 = ((f32[8,2,8,16,128]{4,3,2,1,0:T(8,128)}), f32[8,2,8,16,128]{4,3,2,1,0:T(8,128)S(1)}, u32[]{:S(2)}, u32[]{:S(2)}) async-start(f32[8,2,8,16,128]{4,3,2,1,0:T(8,128)} %shard_map.61), calls=%async_computation.2 | async-start | bytes 2097152 | tf_op jit(solution)/shard_map/all_to_all | solution.py:363
  199.4 4.0 %collective-permute-start.16 = (f32[4,16,128]{2,1,0:T(8,128)S(1)}, f32[4,16,128]{2,1,0:T(8,128)S(1)}, u32[]{:S(2)}, u32[]{:S(2)}) collective-permute-start(f32[4,16,128]{2,1,0:T(8,128)S(1)} %broadcast_select_fusion.1), channel_id=1, source_target_pairs={{0,1},{1,0},{2,3},{3,2},{7,6},{6,7},{5,4},{4,5},{8,9},{9,8},{10,11... | collective-permute-start | bytes 98312 | tf_op jit(solution)/shard_map/ppermute | solution.py:368
  201.2 5.8 %collective-permute-start.17 = (f32[4,16,128]{2,1,0:T(8,128)S(1)}, f32[4,16,128]{2,1,0:T(8,128)S(1)}, u32[]{:S(2)}, u32[]{:S(2)}) collective-permute-start(f32[4,16,128]{2,1,0:T(8,128)S(1)} %get-tuple-element.84), channel_id=1, source_target_pairs={{1,2},{2,1},{3,7},{7,3},{6,5},{5,6},{4,8},{8,4},{9,10},{10,9},{11,... | collective-permute-start | bytes 98312 | tf_op jit(solution)/shard_map/ppermute | solution.py:369
  207.0 1.1 copy-start.1

commit v2 on v1

v2 whole, which is shorter than its diff:
```python
import functools

import jax
import jax.numpy as jnp
from jax import lax
from jax.experimental import pallas as pl
from jax.experimental.pallas import tpu as pltpu
from jax.sharding import Mesh, PartitionSpec as P

SWEEPS = 4
NT = 16
HALO = 16
CHUNK = 64
WIDE = CHUNK + 2 * HALO
PIECE = 8
STRIP = 4
NZD = 8
NSP = 16
LANES = 128
F32 = jnp.float32

VMEM = pl.BlockSpec(memory_space=pltpu.VMEM)
LIMIT = 16 * 1024 * 1024
MOST = 60 * 1024 * 1024
BF16 = jnp.bfloat16


def call(kernel, out, specs, scratch=(), mixer=False, sems=0, limit=LIMIT):
    outs = [jax.ShapeDtypeStruct(s, F32) for s in out]
    scratch = [pltpu.VMEM(s, F32) for s in scratch]
    if mixer:
        scratch.append(pltpu.VMEM((2 * LANES, 2 * LANES), BF16))
    if sems:
        scratch.append(pltpu.SemaphoreType.DMA((sems,)))
    return pl.pallas_call(
        kernel,
        out_shape=outs,
        in_specs=specs,
        out_specs=[VMEM] * len(out),
        scratch_shapes=scratch,
        compiler_params=pltpu.CompilerParams(vmem_limit_bytes=limit),
    )


SNAKE = [x * 4 + (y if x % 2 == 0 else 3 - y) for x in range(4) for y in range(4)]


def position():
    z, core = lax.axis_index("z"), lax.axis_index("core")
    j = lax.axis_index("space")
    x = j // 4
    odd = x % 2
    y = j % 4
    odd_chunk = (y + odd) % 2
    sub = z + odd_chunk * (NZD - 1 - 2 * z)
    return z, core, odd_chunk, sub


def flat(z, core, j):
    return (z * 2 + core) * NSP + j


def piece_pairs(first):
    path = [
        (z, SNAKE[k])
        for k in range(NSP)
        for z in (range(NZD) if k % 2 == 0 else range(NZD - 1, -1, -1))
    ]
    pairs = []
    for core in (0, 1):
        for q in range(first, len(path) - 1, 2):
            a = flat(path[q][0], core, path[q][1])
            b = flat(path[q + 1][0], core, path[q + 1][1])
            pairs += [(a, b), (b, a)]
    return pairs


def chunk_pairs(first):
    pairs = []
    for z in range(NZD):
        for core in (0, 1):
            for k in range(first, NSP - 1, 2):
                a, b = flat(z, core, SNAKE[k]), flat(z, core, SNAKE[k + 1])
                pairs += [(a, b), (b, a)]
    return pairs


def edges(rows):
    shape = (1, rows, LANES)
    lane = lax.broadcasted_iota(jnp.int32, shape, 2)
    row = lax.broadcasted_iota(jnp.int32, shape, 1)
    top, bottom = (lane >= 96) & (row < 15), (lane < 32) & (row > 0)
    return (lane & 31) < 31, (lane & 31) > 0, lane >= 96, lane < 32, top, bottom


def rolled(v):
    z_top, z_bottom, x_top, x_bottom, top, bottom = edges(16)
    total = jnp.where(z_top, pltpu.roll(v, LANES - 1, 2), 0.0)
    total = total + jnp.where(z_bottom, pltpu.roll(v, 1, 2), 0.0)
    up = pltpu.roll(v, LANES - 32, 2)
    down = pltpu.roll(v, 32, 2)
    far_up = jnp.where(top, pltpu.roll(up, 15, 1), 0.0)
    far_down = jnp.where(bottom, pltpu.roll(down, 1, 1), 0.0)
    return total + jnp.where(x_top, far_up, up) + jnp.where(x_bottom, far_down, down)


def fill_mixer(m_ref):
    shape = (2 * LANES, 2 * LANES)
    source = lax.broadcasted_iota(jnp.int32, shape, 0) & (LANES - 1)
    column = lax.broadcasted_iota(jnp.int32, shape, 1)
    lane = column & (LANES - 1)
    apart = jnp.abs(source - lane)
    near = ((apart == 1) & ((source >> 5) == (lane >> 5))) | (apart == 32)
    far = apart == 96
    picked = jnp.where(column < LANES, jnp.where(near, 1.0, 0.0), jnp.where(far, 1.0, 0.0))
    m_ref[...] = picked.astype(BF16)


def mixed(v, m_ref):
    n = v.shape[0]
    _, _, _, _, top, bottom = edges(16)
    x = v.reshape(n * 16, LANES)
    high = x.astype(BF16)
    rest = x - high.astype(F32)
    middle = rest.astype(BF16)
    low = (rest - middle.astype(F32)).astype(BF16)
    both = jnp.concatenate([high, middle], 1)
    p = jnp.dot(both, m_ref[...], preferred_element_type=F32)
    p = p + jnp.dot(low, m_ref[:LANES], preferred_element_type=F32)
    near = p[:, :LANES].reshape(v.shape)
    far = p[:, LANES:].reshape(v.shape)
    across = jnp.where(bottom, pltpu.roll(far, 1, 1), 0.0)
    return near + jnp.where(top, pltpu.roll(far, 15, 1), across)


def lateral(v, m_ref):
    if m_ref is None:
        return rolled(v)
    cut = v.shape[0] // 3
    return jnp.concatenate([rolled(v[:cut]), mixed(v[cut:], m_ref)], 0)


def swept(v, bb, cc, m_ref=None):
    return bb + cc * (lateral(v[1:-1], m_ref) + v[2:] + v[:-2])


def prep_kernel(c_ref, s_ref, r_ref, o_ref, v_ref, q_ref, sems):
    core = lax.axis_index("core")
    zero = jnp.zeros((HALO, LANES), F32)

    def copies(ref, to, first):
        return [
            pltpu.make_async_copy(
                ref.at[:, pl.ds(m * LANES, LANES)], to.at[:, pl.ds(m * LANES, LANES)], sems.at[first + m]
            )
            for m in range(8)
        ]

    def spread(arriving, ref, base):
        for m in range(8):
            arriving[m].wait()
            tile = ref[:, m * LANES : (m + 1) * LANES].T
            for half in range(2):
                k = 2 * m + half
                part = tile[half * 64 : half * 64 + 64]
                o_ref[SNAKE[k], base + HALO : base + HALO + CHUNK] = part
                if k > 0:
                    o_ref[SNAKE[k - 1], base + HALO + CHUNK : base + WIDE] = part[:HALO]
                if k < NSP - 1:
                    o_ref[SNAKE[k + 1], base : base + HALO] = part[CHUNK - HALO :]
        o_ref[SNAKE[0], base : base + HALO] = zero
        o_ref[SNAKE[NSP - 1], base + HALO + CHUNK : base + WIDE] = zero

    states = copies(c_ref, v_ref, 0)
    for copy in states:
        copy.start()

    @pl.when(core == 0)
    def _():
        fields = copies(s_ref, q_ref, 8)
        for copy in fields:
            copy.start()
        spread(fields, q_ref, WIDE)

    @pl.when(core != 0)
    def _():
        fields = copies(r_ref, q_ref, 8)
        for copy in fields:
            copy.start()
        spread(fields, q_ref, WIDE)

    spread(states, v_ref, 0)


def unpack_kernel(a_ref, q_ref):
    def one(y, _):
        q_ref[y] = a_ref[pl.ds(WIDE + y, NSP, stride=2 * WIDE), :]
        return 0

    lax.fori_loop(0, WIDE, one, 0, unroll=8)


def fine_kernel(
    g_ref, own_ref, oth_ref, o_ref, inv2_ref, cc2_ref, inv_ref, cc_ref, sinv_ref, c_ref,
    a_ref, b_ref, bb_ref, rate_ref, m_ref,
):
    _, core, odd, sub = position()
    step = 8
    fill_mixer(m_ref)

    def gather(y, _):
        a_ref[y] = g_ref[pl.ds(y, NSP, stride=2 * WIDE), :]
        return 0

    lax.fori_loop(0, WIDE, gather, 0, unroll=8)
    c_ref[...] = a_ref[HALO : HALO + CHUNK]

    def init(n, _):
        at = pl.ds(pl.multiple_of(n * step, step), step)
        own, oth = own_ref[at], oth_ref[at]
        source = jnp.where(core == 0, own, oth)
        rate = jnp.where(core == 0, oth, own)
        inv = 1.0 / (1.0 + 6.0 * rate)
        rate_ref[at] = rate
        inv_ref[at] = inv
        cc_ref[at] = rate * inv
        sinv_ref[at] = source * inv
        return 0

    lax.fori_loop(0, WIDE // step, init, 0)

    refs = [a_ref, b_ref]
    for number in range(4):
        def right(n, _):
            at = pl.ds(pl.multiple_of(n * step, step), step)
            bb_ref[at] = a_ref[at] * inv_ref[at] + sinv_ref[at]
            return 0

        lax.fori_loop(0, WIDE // step, right, 0)
        for sweep in range(SWEEPS):
            src, dst = refs[sweep % 2], refs[(sweep + 1) % 2]
            low = number * SWEEPS + sweep + 1
            high = WIDE - low
            dst[low:high] = swept(src[low - 1 : high + 1], bb_ref[low:high], cc_ref[low:high], m_ref)
        if number % 2 == 1:
            for z in range(NZD):
                part = jnp.where(odd == 1, NZD - 1 - z, z)
                o_ref[z, number // 2] = a_ref[pl.ds(HALO + PIECE * part, PIECE)]

    rate = 2.0 * rate_ref[pl.ds(HALO - PIECE + PIECE * sub, 3 * PIECE)]
    inv = 1.0 / (1.0 + 6.0 * rate)
    inv2_ref[...] = inv
    cc2_ref[...] = rate * inv


def messages(odd, e, r_next, a_ref, b_ref):
    head, tail = r_next[:STRIP], r_next[STRIP:]
    a_ref[:PIECE] = e
    b_ref[:PIECE] = e
    a_ref[PIECE:] = jnp.where(odd == 0, tail, head)
    b_ref[PIECE:] = jnp.where(odd == 0, head, tail)


def residual_kernel(own_ref, oth_ref, r_ref, cp_ref, mine_ref, a_ref, b_ref):
    _, core, _, sub = position()
    odd = sub % 2

    def uw(t, which):
        mine, other = own_ref[t // 2, which], oth_ref[t // 2, which]
        return jnp.where(core == t % 2, mine, other)

    r_ref[0] = jnp.zeros(r_ref.shape[1:], F32)
    r_ref[1] = uw(0, 0) - uw(0, 0)
    for t in range(2, NT):
        r_ref[t] = uw(t - 2, 1) - uw(t - 1, 0)
    for n in range(NT // 2):
        even_cp = oth_ref[max(n - 1, 0), 0]
        cp_ref[n] = jnp.where(core == 0, even_cp, oth_ref[n, 0])
        mine_ref[n] = jnp.where(core == 0, r_ref[2 * n], r_ref[2 * n + 1])
    messages(odd, r_ref[1], r_ref[2], a_ref, b_ref)


def coarse_step(v, inv, cc):
    bb = v * inv
    for sweep in range(SWEEPS):
        low = sweep + 1
        high = bb.shape[0] - low
        v = swept(v, bb[low:high], cc[low:high])
    return v


def chain_step(t, ra_ref, rb_ref, e_ref, r_ref, inv_ref, cc_ref):
    sub = position()[3]
    odd = sub % 2
    ra, rb = ra_ref[...], rb_ref[...]
    left = jnp.where(odd == 0, rb, ra)
    right = jnp.where(odd == 0, ra, rb)
    e = jnp.concatenate([left[:PIECE], e_ref[...], right[:PIECE]], 0)
    r1 = jnp.concatenate([left[PIECE:], r_ref[t + 1], right[PIECE:]], 0)
    inv, cc = inv_ref[...], cc_ref[...]
    e1 = coarse_step(e, inv, cc) + r1
    e2 = coarse_step(e1, inv[STRIP:-STRIP], cc[STRIP:-STRIP]) + r_ref[t + 2]
    return e1[STRIP:-STRIP], e2


def chain_kernel(t, ra_ref, rb_ref, e_ref, r_ref, inv_ref, cc_ref, e1_ref, e2_ref, a_ref, b_ref):
    sub = position()[3]
    e1, e2 = chain_step(t, ra_ref, rb_ref, e_ref, r_ref, inv_ref, cc_ref)
    e1_ref[...] = e1
    e2_ref[...] = e2
    messages(sub % 2, e2, r_ref[t + 3], a_ref, b_ref)


def chain_end_kernel(t, ra_ref, rb_ref, r_ref, inv_ref, cc_ref, cp_ref, mine_ref, *refs):
    core = lax.axis_index("core")
    e_refs, o_ref = refs[:-1], refs[-1]
    e1, e2 = chain_step(t, ra_ref, rb_ref, e_refs[-1], r_ref, inv_ref, cc_ref)
    errors = [jnp.zeros(e1.shape, F32)] + [ref[...] for ref in e_refs] + [e1, e2]
    for n in range(NT // 2):
        o_ref[n, 0] = cp_ref[n] + jnp.where(core == 0, errors[2 * n], errors[2 * n + 1])
        o_ref[n, 1] = mine_ref[n]


def last_kernel(
    g_ref, c_ref, ra_ref, rb_ref, inv_ref, cc_ref, sinv_ref, o_ref, a_ref, b_ref, bb_ref, m_ref, sems
):
    device_z, core, odd, _ = position()
    size = CHUNK + 2 * STRIP
    fill_mixer(m_ref)
    for n in range(NZD):
        z = jnp.where(odd == 1, NZD - 1 - n, n)
        a_ref[STRIP + n * PIECE : STRIP + (n + 1) * PIECE] = g_ref[z, 0]
        for y in range(PIECE):
            o_ref[pl.ds(2 * CHUNK + n * PIECE + y, NSP, stride=3 * CHUNK), :] = g_ref[z, 1, y]
    a_ref[:STRIP] = jnp.where(odd == 0, rb_ref[...], ra_ref[...])
    a_ref[STRIP + CHUNK : size] = jnp.where(odd == 0, ra_ref[...], rb_ref[...])

    @pl.when((device_z == 0) & (core == 0))
    def _():
        copy = pltpu.make_async_copy(c_ref, a_ref.at[pl.ds(STRIP, CHUNK)], sems.at[0])
        copy.start()
        copy.wait()

    off = HALO - STRIP
    bb_ref[...] = a_ref[...] * inv_ref[off : off + size] + sinv_ref[off : off + size]

    def keep(which):
        def one(y, _):
            o_ref[pl.ds(which * CHUNK + y, NSP, stride=3 * CHUNK), :] = a_ref[STRIP + y]
            return 0

        lax.fori_loop(0, CHUNK, one, 0, unroll=8)

    keep(0)
    refs = [a_ref, b_ref]
    for sweep in range(SWEEPS):
        src, dst = refs[sweep % 2], refs[(sweep + 1) % 2]
        low = sweep + 1
        high = size - low
        dst[low:high] = swept(
            src[low - 1 : high + 1], bb_ref[low:high], cc_ref[off + low : off + high], m_ref
        )
    keep(1)


def finish_kernel(a_ref, f_ref, r_ref):
    outs = [f_ref.at[0], f_ref.at[1], r_ref]
    for which in range(3):
        for m in range(8):
            low = a_ref[SNAKE[2 * m], which * CHUNK : (which + 1) * CHUNK]
            high = a_ref[SNAKE[2 * m + 1], which * CHUNK : (which + 1) * CHUNK]
            outs[which][:, m * 128 : (m + 1) * 128] = jnp.concatenate([low, high], 0).T


def strips_kernel(g_ref, c_ref, a_ref, b_ref, head_ref, tail_ref, sems):
    z, core, odd, _ = position()
    low, high = odd * (NZD - 1), (1 - odd) * (NZD - 1)
    head_ref[...] = g_ref[low, 0, :STRIP]
    tail_ref[...] = g_ref[high, 0, STRIP:]

    @pl.when((z == 0) & (core == 0))
    def _():
        copies = [
            pltpu.make_async_copy(c_ref.at[pl.ds(0, STRIP)], head_ref, sems.at[0]),
            pltpu.make_async_copy(c_ref.at[pl.ds(CHUNK - STRIP, STRIP)], tail_ref, sems.at[1]),
        ]
        for copy in copies:
            copy.start()
        for copy in copies:
            copy.wait()

    head, tail = head_ref[...], tail_ref[...]
    a_ref[...] = jnp.where(odd == 0, tail, head)
    b_ref[...] = jnp.where(odd == 0, head, tail)


def body(c_guess, source, rate):
    everyone = ("z", "core", "space")
    anywhere = pl.BlockSpec(memory_space=pltpu.HBM)
    plane = (16, LANES)
    piece = (PIECE,) + plane
    message = (PIECE + STRIP,) + plane

    def swap(v):
        return lax.ppermute(v, "core", [(0, 1), (1, 0)])

    sent = call(
        prep_kernel, [(NSP, 2 * WIDE, LANES)], [anywhere] * 3, [(LANES, 1024)] * 2, sems=16, limit=MOST
    )(c_guess.reshape(LANES, -1), source.reshape(LANES, -1), rate.reshape(LANES, -1))[0]
    got = lax.all_to_all(sent, "space", 0, 0).reshape(-1, LANES)
    own = call(unpack_kernel, [(WIDE,) + plane], [VMEM])(got)[0]
    oth = swap(own)

    uw, inv2, cc2, inv, cc, sinv, c = call(
        fine_kernel,
        [(NZD, 2) + piece]
        + [(3 * PIECE,) + plane] * 2
        + [(WIDE,) + plane] * 3
        + [(CHUNK,) + plane],
        [VMEM] * 3,
        [(WIDE,) + plane] * 4,
        mixer=True,
    )(got, own, oth)

    mine = lax.all_to_all(uw, "z", 0, 0)
    other = swap(mine)
    res, cpoint, res_mine, ma, mb = call(
        residual_kernel,
        [(NT,) + piece, (NT // 2,) + piece, (NT // 2,) + piece, message, message],
        [VMEM] * 2,
    )(mine, other)

    pairs_a, pairs_b = piece_pairs(0), piece_pairs(1)
    errors = [res[1]]
    for t in range(1, NT - 3, 2):
        ra = lax.ppermute(ma, everyone, pairs_a)
        rb = lax.ppermute(mb, everyone, pairs_b)
        e1, e2, ma, mb = call(
            functools.partial(chain_kernel, t), [piece, piece, message, message], [VMEM] * 6
        )(ra, rb, errors[-1], res, inv2, cc2)
        errors += [e1, e2]
    ra = lax.ppermute(ma, everyone, pairs_a)
    rb = lax.ppermute(mb, everyone, pairs_b)
    corrected = call(
        functools.partial(chain_end_kernel, NT - 3),
        [(NZD, 2) + piece],
        [VMEM] * (7 + len(errors)),
    )(ra, rb, res, inv2, cc2, cpoint, res_mine, *errors)[0]

    chunk = lax.all_to_all(corrected, "z", 0, 0)
    edge = (STRIP,) + plane
    ma, mb = call(strips_kernel, [edge] * 2, [VMEM, anywhere], [edge] * 2, sems=2)(chunk, c)
    ra = lax.ppermute(ma, everyone, chunk_pairs(0))
    rb = lax.ppermute(mb, everyone, chunk_pairs(1))
    size = CHUNK + 2 * STRIP
    sent = call(
        last_kernel,
        [(NSP * 3 * CHUNK, LANES)],
        [VMEM, anywhere] + [VMEM] * 5,
        [(size,) + plane] * 3,
        mixer=True,
        sems=1,
    )(chunk, c, ra, rb, inv, cc, sinv)[0]
    got = lax.all_to_all(sent.reshape(NSP, 3 * CHUNK, LANES), "space", 0, 0)
    fine, residual = call(finish_kernel, [(2, LANES, 1024), (LANES, 1024)], [VMEM])(got)
    return fine.reshape(1, 2, 4, 32, 1024), residual.reshape(1, 4, 32, 1024)


def solution(mesh):
    inner = Mesh(mesh.devices.reshape(NZD, 2, NSP), ("z", "core", "space"))
    tm = ("z", "core")
    return jax.shard_map(
        body,
        mesh=inner,
        in_specs=(P(tm, "space", None, None), P("space", None, None), P("space", None, None)),
        out_specs=(P(tm, None, "space", None, None), P(tm, "space", None, None)),
        check_vma=False,
    )
```

time: 239 us -> 214 us (0.90)
  blocking collectives: 84.3 us -> 114 us
  Pallas kernels: 52.7 us -> 29.7 us
  waiting for transfers between devices: 52.4 us -> 34 us
  starting transfers between devices: 39.9 us -> 33.4 us
  local copies, waits for them, and re-layouts: 5.23 us -> 0.01 us
    all_to_all x1 -> x2, blocking collectives: 28.3 us -> 56.5 us  [the longest x1 28.4 us: body(): got = lax.all_to_all(sent, 'space', 0, 0).reshape(-1, LANES)]
    pallas_call x12, Pallas kernels: 50.3 us -> 28 us  [the longest x1 9.76 us: body(): call(fine_kernel, [(NZD, 2) + piece] + [(3 * PIECE,) + plane] * 2 + [(WID...]
    all_to_all x1 -> x0, waiting for transfers between devices: 19 us -> none  [body(): chunk = lax.all_to_all(corrected, 'z', 0, 0)]
    all_to_all x1 -> x0, starting transfers between devices: 6.42 us -> none  [body(): chunk = lax.all_to_all(corrected, 'z', 0, 0)]
    unnamed x10 -> x0, local copies, waits for them, and re-layouts: 5.14 us -> none
  transfers between devices with their start and end apart: 19 -> 18, of which waited for: 17 -> 17; matrix products, arithmetic and copies ran while one was open for 0% -> 0% of each run, Pallas kernels for 0% -> 0%
where the time goes in v2:
time: 214 us; the launch traced here: 212 us
  blocking collectives  114 us (53%)
  waiting for transfers between devices  34 us (16%)
  starting transfers between devices  33.4 us (16%)
  Pallas kernels  29.7 us (14%)
    all_to_all x1, blocking collectives, body(): mine = lax.all_to_all(uw, 'z', 0, 0)  37.3 us
    all_to_all x1, blocking collectives, body(): got = lax.all_to_all(sent, 'space', 0, 0).reshape(-1, LANES)  28.4 us
    all_to_all x1, blocking collectives, body(): chunk = lax.all_to_all(corrected, 'z', 0, 0)  28.1 us
    ppermute x7, starting transfers between devices, body(): rb = lax.ppermute(mb, everyone, pairs_b)  20.9 us
    ppermute x7, waiting for transfers between devices, body(): rb = lax.ppermute(mb, everyone, pairs_b)  20.9 us
    all_to_all x1, blocking collectives, body(): got = lax.all_to_all(sent.reshape(NSP, 3 * CHUNK, LANES), 'space', 0, 0)  19.9 us
    pallas_call x1, Pallas kernels, body(): call(fine_kernel, [(NZD, 2) + piece] + [(3 * PIECE,) + plane] * 2 + [(WID...  9.76 us
    pallas_call x6, Pallas kernels, body(): call(functools.partial(chain_kernel, t), [piece, piece, message, message]...  8.78 us
  transfers between devices with their start and end apart: 18, of which 17 were waited for; matrix products, arithmetic and copies ran while one was open for 0% of the time, Pallas kernels for 0%

profile of v2, /device:TPU:8, one launch (start us, length us, event | category | flops | bytes accessed | tf_op | source)
XLA Modules:
  0.0 211.8 jit_solution(10310339392885070375)
XLA Ops:
  0.6 4.0 %shard_map.50 = f32[16,192,128]{2,1,0:T(8,128)} custom-call(f32[128,1024]{1,0:T(8,128)} %bitcast.12, f32[128,1024]{1,0:T(8,128)} %bitcast.13, f32[128,1024]{1,0:T(8,128)} %bitcast.14), custom_call_target="tpu_custom_call" | custom-call | tf_op jit(solution)/shard_map/pallas_call | solution.py:407
  4.7 28.4 %all_to_all.20 = f32[16,192,128]{2,1,0:T(8,128)S(1)} all-to-all(f32[16,192,128]{2,1,0:T(8,128)} %shard_map.50), channel_id=1, replica_groups=mesh['z'=8,'core'=2,'space'=16] {'space'}, dimensions={0} | all-to-all | bytes 3145728 | tf_op jit(solution)/shard_map/all_to_all | solution.py:410
  33.1 0.5 shard_map.51.own_ref
  33.7 2.3 %collective-permute-done.oth_ref = f32[96,16,128]{2,1,0:T(8,128)S(1)} collective-permute-done((f32[96,16,128]{2,1,0:T(8,128)S(1)}, f32[96,16,128]{2,1,0:T(8,128)S(1)}, u32[]{:S(2)}, u32[]{:S(2)}) %collective-permute-start) | collective-permute-done | bytes 786464 | tf_op jit(solution)/shard_map/ppermute | solution.py:405
  36.0 9.8 %shard_map.52 = (f32[8,2,8,16,128]{4,3,2,1,0:T(8,128)S(1)}, f32[24,16,128]{2,1,0:T(8,128)S(1)}, f32[24,16,128]{2,1,0:T(8,128)S(1)}, f32[96,16,128]{2,1,0:T(8,128...) custom-call(f32[3072,128]{1,0:T(8,128)S(1)} %bitcast.10, ...), custom_call_target="tpu_custom_call" | custom-call | tf_op jit(solution)/shard_map/pallas_call | solution.py:414
  45.7 37.3 %all_to_all.21.own_ref = f32[8,2,8,16,128]{4,3,2,1,0:T(8,128)S(1)} all-to-all(f32[8,2,8,16,128]{4,3,2,1,0:T(8,128)S(1)} %get-tuple-element.42), channel_id=1, replica_groups=mesh['z'=8,'core'=2,'space'=16] {'z'}, dimensions={0} | all-to-all | bytes 2097152 | tf_op jit(solution)/shard_map/all_to_all | solution.py:425
  83.0 2.7 %collective-permute-done.1.oth_ref = f32[8,2,8,16,128]{4,3,2,1,0:T(8,128)S(1)} collective-permute-done((f32[8,2,8,16,128]{4,3,2,1,0:T(8,128)S(1)}, f32[8,2,8,16,128]{4,3,2,1,0:T(8,128)S(1)}, u32[]{:S(2)}, u32[]{:S(2)}) %collective-permute-start.1) | collective-permute-done | bytes 1048608 | tf_op jit(solution)/shard_map/ppermute | solution.py:405
  85.7 0.3 shard_map.53
  86.0 0.7 collective-permute-start.2
  86.6 3.1 %collective-permute-start.3 = (f32[12,16,128]{2,1,0:T(8,128)S(1)}, f32[12,16,128]{2,1,0:T(8,128)S(1)}, u32[]{:S(2)}, u32[]{:S(2)}) collective-permute-start(f32[12,16,128]{2,1,0:T(8,128)S(1)} %get-tuple-element.44), channel_id=1, source_target_pairs={{32,64},{64,32},{96,128},{128,96},{160,192},{192,160},{224,225},{2... | collective-permute-start | bytes 294920 | tf_op jit(solution)/shard_map/ppermute | solution.py:437
  89.8 1.1 collective-permute-done.2.ra_ref
  90.9 2.2 %collective-permute-done.3.rb_ref = f32[12,16,128]{2,1,0:T(8,128)S(1)} collective-permute-done((f32[12,16,128]{2,1,0:T(8,128)S(1)}, f32[12,16,128]{2,1,0:T(8,128)S(1)}, u32[]{:S(2)}, u32[]{:S(2)}) %collective-permute-start.3) | collective-permute-done | bytes 98336 | tf_op jit(solution)/shard_map/ppermute | solution.py:437
  93.1 1.5 shard_map.54
  94.6 1.5 collective-permute-start.4
  96.2 2.9 %collective-permute-start.5 = (f32[12,16,128]{2,1,0:T(8,128)S(1)}, f32[12,16,128]{2,1,0:T(8,128)S(1)}, u32[]{:S(2)}, u32[]{:S(2)}) collective-permute-start(f32[12,16,128]{2,1,0:T(8,128)S(1)} %get-tuple-element.49), channel_id=1, source_target_pairs={{32,64},{64,32},{96,128},{128,96},{160,192},{192,160},{224,225},{2... | collective-permute-start | bytes 294920 | tf_op jit(solution)/shard_map/ppermute | solution.py:437
  99.3 3.3 %collective-permute-done.5.rb_ref = f32[12,16,128]{2,1,0:T(8,128)S(1)} collective-permute-done((f32[12,16,128]{2,1,0:T(8,128)S(1)}, f32[12,16,128]{2,1,0:T(8,128)S(1)}, u32[]{:S(2)}, u32[]{:S(2)}) %collective-permute-start.5) | collective-permute-done | bytes 98336 | tf_op jit(solution)/shard_map/ppermute | solution.py:437
  102.7 1.5 shard_map.55
  104.1 0.7 collective-permute-start.6
  104.8 2.9 %collective-permute-start.7 = (f32[12,16,128]{2,1,0:T(8,128)S(1)}, f32[12,16,128]{2,1,0:T(8,128)S(1)}, u32[]{:S(2)}, u32[]{:S(2)}) collective-permute-start(f32[12,16,128]{2,1,0:T(8,128)S(1)} %get-tuple-element.52), channel_id=1, source_target_pairs={{32,64},{64,32},{96,128},{128,96},{160,192},{192,160},{224,225},{2... | collective-permute-start | bytes 294920 | tf_op jit(solution)/shard_map/ppermute | solution.py:437
  107.7 1.1 collective-permute-done.6.ra_ref
  108.8 2.4 %collective-permute-done.7.rb_ref = f32[12,16,128]{2,1,0:T(8,128)S(1)} collective-permute-done((f32[12,16,128]{2,1,0:T(8,128)S(1)}, f32[12,16,128]{2,1,0:T(8,128)S(1)}, u32[]{:S(2)}, u32[]{:S(2)}) %collective-permute-start.7) | collective-permute-done | bytes 98336 | tf_op jit(solution)/shard_map/ppermute | solution.py:437
  111.3 1.5 shard_map.56
  112.7 1.5 collective-permute-start.8
  114.3 2.9 %collective-permute-start.9 = (f32[12,16,128]{2,1,0:T(8,128)S(1)}, f32[12,16,128]{2,1,0:T(8,128)S(1)}, u32[]{:S(2)}, u32[]{:S(2)}) collective-permute-start(f32[12,16,128]{2,1,0:T(8,128)S(1)} %get-tuple-element.55), channel_id=1, source_target_pairs={{32,64},{64,32},{96,128},{128,96},{160,192},{192,160},{224,225},{2... | collective-permute-start | bytes 294920 | tf_op jit(solution)/shard_map/ppermute | solution.py:437
  117.5 3.3 %collective-permute-done.9.rb_ref = f32[12,16,128]{2,1,0:T(8,128)S(1)} collective-permute-done((f32[12,16,128]{2,1,0:T(8,128)S(1)}, f32[12,16,128]{2,1,0:T(8,128)S(1)}, u32[]{:S(2)}, u32[]{:S(2)}) %collective-permute-start.9) | collective-permute-done | bytes 98336 | tf_op jit(solution)/shard_map/ppermute | solution.py:437
  120.8 1.5 shard_map.57
  122.3 0.9 collective-permute-start.10
  123.2 2.9 %collective-permute-start.11 = (f32[12,16,128]{2,1,0:T(8,128)S(1)}, f32[12,16,128]{2,1,0:T(8,128)S(1)}, u32[]{:S(2)}, u32[]{:S(2)}) collective-permute-start(f32[12,16,128]{2,1,0:T(8,128)S(1)} %get-tuple-element.58), channel_id=1, source_target_pairs={{32,64},{64,32},{96,128},{128,96},{160,192},{192,160},{224,225},{2... | collective-permute-start | bytes 294920 | tf_op jit(solution)/shard_map/ppermute | solution.py:437
  126.1 0.8 collective-permute-done.10.ra_ref
  127.0 2.7 %collective-permute-done.11.rb_ref = f32[12,16,128]{2,1,0:T(8,128)S(1)} collective-permute-done((f32[12,16,128]{2,1,0:T(8,128)S(1)}, f32[12,16,128]{2,1,0:T(8,128)S(1)}, u32[]{:S(2)}, u32[]{:S(2)}) %collective-permute-start.11) | collective-permute-done | bytes 98336 | tf_op jit(solution)/shard_map/ppermute | solution.py:437
  129.7 1.5 shard_map.58
  131.2 1.9 collective-permute-start.12
  133.1 2.9 %collective-permute-start.13 = (f32[12,16,128]{2,1,0:T(8,128)S(1)}, f32[12,16,128]{2,1,0:T(8,128)S(1)}, u32[]{:S(2)}, u32[]{:S(2)}) collective-permute-start(f32[12,16,128]{2,1,0:T(8,128)S(1)} %get-tuple-element.61), channel_id=1, source_target_pairs={{32,64},{64,32},{96,128},{128,96},{160,192},{192,160},{224,225},{2... | collective-permute-start | bytes 294920 | tf_op jit(solution)/shard_map/ppermute | solution.py:437
  136.0 3.9 %collective-permute-done.13.rb_ref = f32[12,16,128]{2,1,0:T(8,128)S(1)} collective-permute-done((f32[12,16,128]{2,1,0:T(8,128)S(1)}, f32[12,16,128]{2,1,0:T(8,128)S(1)}, u32[]{:S(2)}, u32[]{:S(2)}) %collective-permute-start.13) | collective-permute-done | bytes 98336 | tf_op jit(solution)/shard_map/ppermute | solution.py:437
  139.9 1.5 shard_map.59
  141.4 1.2 collective-permute-start.14
  142.5 3.2 %collective-permute-start.15 = (f32[12,16,128]{2,1,0:T(8,128)S(1)}, f32[12,16,128]{2,1,0:T(8,128)S(1)}, u32[]{:S(2)}, u32[]{:S(2)}) collective-permute-start(f32[12,16,128]{2,1,0:T(8,128)S(1)} %get-tuple-element.64), channel_id=1, source_target_pairs={{32,64},{64,32},{96,128},{128,96},{160,192},{192,160},{224,225},{2... | collective-permute-start | bytes 294920 | tf_op jit(solution)/shard_map/ppermute | solution.py:443
  145.7 0.4 collective-permute-done.14.ra_ref
  146.1 3.0 %collective-permute-done.15.rb_ref = f32[12,16,128]{2,1,0:T(8,128)S(1)} collective-permute-done((f32[12,16,128]{2,1,0:T(8,128)S(1)}, f32[12,16,128]{2,1,0:T(8,128)S(1)}, u32[]{:S(2)}, u32[]{:S(2)}) %collective-permute-start.15) | collective-permute-done | bytes 98336 | tf_op jit(solution)/shard_map/ppermute | solution.py:443
  149.0 1.5 shard_map.60
  150.6 28.1 %all_to_all.22.g_ref = f32[8,2,8,16,128]{4,3,2,1,0:T(8,128)S(1)} all-to-all(f32[8,2,8,16,128]{4,3,2,1,0:T(8,128)S(1)} %shard_map.60), channel_id=1, replica_groups=mesh['z'=8,'core'=2,'space'=16] {'z'}, dimensions={0} | all-to-all | bytes 2097152 | tf_op jit(solution)/shard_map/all_to_all | solution.py:450
  178.8 1.7 collective-permute-start.16
  180.5 2.2 %collective-permute-start.17 = (f32[4,16,128]{2,1,0:T(8,128)S(1)}, f32[4,16,128]{2,1,0:T(8,128)S(1)}, u32[]{:S(2)}, u32[]{:S(2)}) collective-permute-start(f32[4,16,128]{2,1,0:T(8,128)S(1)} %get-tuple-element.76), channel_id=1, source_target_pairs={{1,2},{2,1},{3,7},{7,3},{6,5},{5,6},{4,8},{8,4},{9,10},{10,9},{11,... | collective-permute-start | bytes 98312 | tf_op jit(solution)/shard_map/ppermute | solution.py:454
  182.8 0.7 collective-permute-done.16.ra_ref
  183.5 3.6 %collective-permute-done.17.rb_ref = f32[4,16,128]{2,1,0:T(8,128)S(1)} collective-permute-done((f32[4,16,128]{2,1,0:T(8,128)S(1)}, f32[4,16,128]{2,1,0:T(8,128)S(1)}, u32[]{:S(2)}, u32[]{:S(2)}) %collective-permute-start.17) | collective-permute-done | bytes 32800 | tf_op jit(solution)/shard_map/ppermute | solution.py:454
  187.1 3.3 %shard_map.62 = f32[3072,128]{1,0:T(8,128)S(1)} custom-call(f32[8,2,8,16,128]{4,3,2,1,0:T(8,128)S(1)} %all_to_all.22.g_ref, f32[64,16,128]{2,1,0:T(8,128)S(1)} %get-tuple-element.74.c_ref, f32[4,16,128]{2,1,0:T(8,128)S(1)} %collective-permute-done.16.ra_ref, f32[4,16,128]{2,1,0:T(8,128)S(1)} %collective-permute-done.17.rb_ref, ...), custom_call_target="tpu_custom_call" | custom-call | tf_op jit(solution)/shard_map/pallas_call | solution.py:456
  190.4 19.9 %all_to_all.23.a_ref = f32[16,192,128]{2,1,0:T(8,128)S(1)} all-to-all(f32[16,192,128]{2,1,0:T(8,128)S(1)} %bitcast.11), channel_id=1, replica_groups=mesh['z'=8,'core'=2,'space'=16] {'space'}, dimensions={0} | all-to-all | bytes 3145728 | tf_op jit(solution)/shard_map/all_to_all | solution.py:464
  210.3 1.5 shard_map.63
  (7 shorter events, 0.6 us)
Async XLA Ops:
  33.6 2.4 %collective-permute-start = (f32[96,16,128]{2,1,0:T(8,128)S(1)}, f32[96,16,128]{2,1,0:T(8,128)S(1)}, u32[]{:S(2)}, u32[]{:S(2)}) collective-permute-start(f32[96,16,128]{2,1,0:T(8,128)S(1)} %shard_map.51.own_ref), channel_id=1, source_target_pairs={{0,16},{16,0},{1,17},{17,1},{2,18},{18,2},{3,19},{19,3},{4,20},{20... | collective-permute-start | bytes 2359304 | tf_op jit(solution)/shard_map/ppermute | solution.py:405
  83.0 2.7 %collective-permute-start.1 = (f32[8,2,8,16,128]{4,3,2,1,0:T(8,128)S(1)}, f32[8,2,8,16,128]{4,3,2,1,0:T(8,128)S(1)}, u32[]{:S(2)}, u32[]{:S(2)}) collective-permute-start(f32[8,2,8,16,128]{4,3,2,1,0:T(8,128)S(1)} %all_to_all.21.own_ref), channel_id=1, source_target_pairs={{0,16},{16,0},{1,17},{17,1},{2,18},{18,2},{3,19},{19,3},{4,20},{20... | collective-permute-start | bytes 3145736 | tf_op jit(solution)/shard_map/ppermute | solution.py:405
  86.0 4.9 %collective-permute-start.2 = (f32[12,16,128]{2,1,0:T(8,128)S(1)}, f32[12,16,128]{2,1,0:T(8,128)S(1)}, u32[]{:S(2)}, u32[]{:S(2)}) collective-permute-start(f32[12,16,128]{2,1,0:T(8,128)S(1)} %get-tuple-element.43), channel_id=1, source_target_pairs={{0,32},{32,0},{64,96},{96,64},{128,160},{160,128},{192,224},{224,1... | collective-permute-start | bytes 294920 | tf_op jit(solution)/shard_map/ppermute | solution.py:436
  86.6 6.5 %collective-permute-start.3 = (f32[12,16,128]{2,1,0:T(8,128)S(1)}, f32[12,16,128]{2,1,0:T(8,128)S(1)}, u32[]{:S(2)}, u32[]{:S(2)}) collective-permute-start(f32[12,16,128]{2,1,0:T(8,128)S(1)} %get-tuple-element.44), channel_id=1, source_target_pairs={{32,64},{64,32},{96,128},{128,96},{160,192},{192,160},{224,225},{2... | collective-permute-start | bytes 294920 | tf_op jit(solution)/shard_map/ppermute | solution.py:437
  94.6 4.7 %collective-permute-start.4 = (f32[12,16,128]{2,1,0:T(8,128)S(1)}, f32[12,16,128]{2,1,0:T(8,128)S(1)}, u32[]{:S(2)}, u32[]{:S(2)}) collective-permute-start(f32[12,16,128]{2,1,0:T(8,128)S(1)} %get-tuple-element.48), channel_id=1, source_target_pairs={{0,32},{32,0},{64,96},{96,64},{128,160},{160,128},{192,224},{224,1... | collective-permute-start | bytes 294920 | tf_op jit(solution)/shard_map/ppermute | solution.py:436
  96.2 6.5 %collective-permute-start.5 = (f32[12,16,128]{2,1,0:T(8,128)S(1)}, f32[12,16,128]{2,1,0:T(8,128)S(1)}, u32[]{:S(2)}, u32[]{:S(2)}) collective-permute-start(f32[12,16,128]{2,1,0:T(8,128)S(1)} %get-tuple-element.49), channel_id=1, source_target_pairs={{32,64},{64,32},{96,128},{128,96},{160,192},{192,160},{224,225},{2... | collective-permute-start | bytes 294920 | tf_op jit(solution)/shard_map/ppermute | solution.py:437
  104.1 4.7 %collective-permute-start.6 = (f32[12,16,128]{2,1,0:T(8,128)S(1)}, f32[12,16,128]{2,1,0:T(8,128)S(1)}, u32[]{:S(2)}, u32[]{:S(2)}) collective-permute-start(f32[12,16,128]{2,1,0:T(8,128)S(1)} %get-tuple-element.51), channel_id=1, source_target_pairs={{0,32},{32,0},{64,96},{96,64},{128,160},{160,128},{192,224},{224,1... | collective-permute-start | bytes 294920 | tf_op jit(solution)/shard_map/ppermute | solution.py:436
  104.8 6.5 %collective-permute-start.7 = (f32[12,16,128]{2,1,0:T(8,128)S(1)}, f32[12,16,128]{2,1,0:T(8,128)S(1)}, u32[]{:S(2)}, u32[]{:S(2)}) collective-permute-start(f32[12,16,128]{2,1,0:T(8,128)S(1)} %get-tuple-element.52), channel_id=1, source_target_pairs={{32,64},{64,32},{96,128},{128,96},{160,192},{192,160},{224,225},{2... | collective-permute-start | bytes 294920 | tf_op jit(solution)/shard_map/ppermute | solution.py:437
  112.7 4.7 %collective-permute-start.8 = (f32[12,16,128]{2,1,0:T(8,128)S(1)}, f32[12,16,128]{2,1,0:T(8,128)S(1)}, u32[]{:S(2)}, u32[]{:S(2)}) collective-permute-start(f32[12,16,128]{2,1,0:T(8,128)S(1)} %get-tuple-element.54), channel_id=1, source_target_pairs={{0,32},{32,0},{64,96},{96,64},{128,160},{160,128},{192,224},{224,1... | collective-permute-start | bytes 294920 | tf_op jit(solution)/shard_map/ppermute | solution.py:436
  114.3 6.5 %collective-permute-start.9 = (f32[12,16,128]{2,1,0:T(8,128)S(1)}, f32[12,16,128]{2,1,0:T(8,128)S(1)}, u32[]{:S(2)}, u32[]{:S(2)}) collective-permute-start(f32[12,16,128]{2,1,0:T(8,128)S(1)} %get-tuple-element.55), channel_id=1, source_target_pairs={{32,64},{64,32},{96,128},{128,96},{160,192},{192,160},{224,225},{2... | collective-permute-start | bytes 294920 | tf_op jit(solution)/shard_map/ppermute | solution.py:437
  122.3 4.7 %collective-permute-start.10 = (f32[12,16,128]{2,1,0:T(8,128)S(1)}, f32[12,16,128]{2,1,0:T(8,128)S(1)}, u32[]{:S(2)}, u32[]{:S(2)}) collective-permute-start(f32[12,16,128]{2,1,0:T(8,128)S(1)} %get-tuple-element.57), channel_id=1, source_target_pairs={{0,32},{32,0},{64,96},{96,64},{128,160},{160,128},{192,224},{224,1... | collective-permute-start | bytes 294920 | tf_op jit(solution)/shard_map/ppermute | solution.py:436
  123.2 6.5 %collective-permute-start.11 = (f32[12,16,128]{2,1,0:T(8,128)S(1)}, f32[12,16,128]{2,1,0:T(8,128)S(1)}, u32[]{:S(2)}, u32[]{:S(2)}) collective-permute-start(f32[12,16,128]{2,1,0:T(8,128)S(1)} %get-tuple-element.58), channel_id=1, source_target_pairs={{32,64},{64,32},{96,128},{128,96},{160,192},{192,160},{224,225},{2... | collective-permute-start | bytes 294920 | tf_op jit(solution)/shard_map/ppermute | solution.py:437
  131.2 4.9 %collective-permute-start.12 = (f32[12,16,128]{2,1,0:T(8,128)S(1)}, f32[12,16,128]{2,1,0:T(8,128)S(1)}, u32[]{:S(2)}, u32[]{:S(2)}) collective-permute-start(f32[12,16,128]{2,1,0:T(8,128)S(1)} %get-tuple-element.60), channel_id=1, source_target_pairs={{0,32},{32,0},{64,96},{96,64},{128,160},{160,128},{192,224},{224,1... | collective-permute-start | bytes 294920 | tf_op jit(solution)/shard_map/ppermute | solution.py:436
  133.1 6.8 %collective-permute-start.13 = (f32[12,16,128]{2,1,0:T(8,128)S(1)}, f32[12,16,128]{2,1,0:T(8,128)S(1)}, u32[]{:S(2)}, u32[]{:S(2)}) collective-permute-start(f32[12,16,128]{2,1,0:T(8,128)S(1)} %get-tuple-element.61), channel_id=1, source_target_pairs={{32,64},{64,32},{96,128},{128,96},{160,192},{192,160},{224,225},{2... | collective-permute-start | bytes 294920 | tf_op jit(solution)/shard_map/ppermute | solution.py:437
  141.4 4.7 %collective-permute-start.14 = (f32[12,16,128]{2,1,0:T(8,128)S(1)}, f32[12,16,128]{2,1,0:T(8,128)S(1)}, u32[]{:S(2)}, u32[]{:S(2)}) collective-permute-start(f32[12,16,128]{2,1,0:T(8,128)S(1)} %get-tuple-element.63), channel_id=1, source_target_pairs={{0,32},{32,0},{64,96},{96,64},{128,160},{160,128},{192,224},{224,1... | collective-permute-start | bytes 294920 | tf_op jit(solution)/shard_map/ppermute | solution.py:442
  142.5 6.5 %collective-permute-start.15 = (f32[12,16,128]{2,1,0:T(8,128)S(1)}, f32[12,16,128]{2,1,0:T(8,128)S(1)}, u32[]{:S(2)}, u32[]{:S(2)}) collective-permute-start(f32[12,16,128]{2,1,0:T(8,128)S(1)} %get-tuple-element.64), channel_id=1, source_target_pairs={{32,64},{64,32},{96,128},{128,96},{160,192},{192,160},{224,225},{2... | collective-permute-start | bytes 294920 | tf_op jit(solution)/shard_map/ppermute | solution.py:443
  178.8 4.7 %collective-permute-start.16 = (f32[4,16,128]{2,1,0:T(8,128)S(1)}, f32[4,16,128]{2,1,0:T(8,128)S(1)}, u32[]{:S(2)}, u32[]{:S(2)}) collective-permute-start(f32[4,16,128]{2,1,0:T(8,128)S(1)} %get-tuple-element.75), channel_id=1, source_target_pairs={{0,1},{1,0},{2,3},{3,2},{7,6},{6,7},{5,4},{4,5},{8,9},{9,8},{10,11... | collective-permute-start | bytes 98312 | tf_op jit(solution)/shard_map/ppermute | solution.py:453
  180.5 6.5 %collective-permute-start.17 = (f32[4,16,128]{2,1,0:T(8,128)S(1)}, f32[4,16,128]{2,1,0:T(8,128)S(1)}, u32[]{:S(2)}, u32[]{:S(2)}) collective-permute-start(f32[4,16,128]{2,1,0:T(8,128)S(1)} %get-tuple-element.76), channel_id=1, source_target_pairs={{1,2},{2,1},{3,7},{7,3},{6,5},{5,6},{4,8},{8,4},{9,10},{10,9},{11,... | collective-permute-start | bytes 98312 | tf_op jit(solution)/shard_map/ppermute | solution.py:454

commit v3 on v2

--- a/solution.py
+++ b/solution.py
@@ -56,6 +56,11 @@
     return z, core, odd_chunk, sub
 
 
+def at_ends():
+    j = lax.axis_index("space")
+    return j == SNAKE[0], j == SNAKE[-1]
+
+
 def flat(z, core, j):
     return (z * 2 + core) * NSP + j
 
@@ -68,21 +73,27 @@
     ]
     pairs = []
     for core in (0, 1):
-        for q in range(first, len(path) - 1, 2):
-            a = flat(path[q][0], core, path[q][1])
-            b = flat(path[q + 1][0], core, path[q + 1][1])
+        for q in range(first, len(path), 2):
+            (z, j), (other_z, other_j) = path[q], path[(q + 1) % len(path)]
+            a, b = flat(z, core, j), flat(other_z, core, other_j)
             pairs += [(a, b), (b, a)]
     return pairs
 
 
 def chunk_pairs(first):
     pairs = []
-    for z in range(NZD):
-        for core in (0, 1):
-            for k in range(first, NSP - 1, 2):
-                a, b = flat(z, core, SNAKE[k]), flat(z, core, SNAKE[k + 1])
-                pairs += [(a, b), (b, a)]
+    for k in range(first, NSP, 2):
+        a, b = SNAKE[k], SNAKE[(k + 1) % NSP]
+        pairs += [(a, b), (b, a)]
     return pairs
+
+
+def interval_shift(step):
+    moves = []
+    for t in range(NT):
+        to = (t + step) % NT
+        moves += [(flat(t // 2, t % 2, j), flat(to // 2, to % 2, j)) for j in range(NSP)]
+    return moves
 
 
 def edges(rows):
@@ -200,11 +211,25 @@
     lax.fori_loop(0, WIDE, one, 0, unroll=8)
 
 
-def fine_kernel(
-    g_ref, own_ref, oth_ref, o_ref, inv2_ref, cc2_ref, inv_ref, cc_ref, sinv_ref, c_ref,
-    a_ref, b_ref, bb_ref, rate_ref, m_ref,
+def double_step(number, a_ref, b_ref, bb_ref, inv_ref, cc_ref, sinv_ref, m_ref):
+    refs = [a_ref, b_ref]
+    for step in (number, number + 1):
+        edge = step * SWEEPS
+        bb_ref[edge : WIDE - edge] = (
+            a_ref[edge : WIDE - edge] * inv_ref[edge : WIDE - edge] + sinv_ref[edge : WIDE - edge]
+        )
+        for sweep in range(SWEEPS):
+            src, dst = refs[sweep % 2], refs[(sweep + 1) % 2]
+            low = edge + sweep + 1
+            high = WIDE - low
+            dst[low:high] = swept(src[low - 1 : high + 1], bb_ref[low:high], cc_ref[low:high], m_ref)
+
+
+def first_kernel(
+    g_ref, own_ref, oth_ref, a_ref, u_ref, inv2_ref, cc2_ref, inv_ref, cc_ref, sinv_ref, c_ref,
+    b_ref, bb_ref, rate_ref, m_ref,
 ):
-    _, core, odd, sub = position()
+    _, core, _, sub = position()
     step = 8
     fill_mixer(m_ref)
 
@@ -228,29 +253,31 @@
         return 0
 
     lax.fori_loop(0, WIDE // step, init, 0)
-
-    refs = [a_ref, b_ref]
-    for number in range(4):
-        def right(n, _):
-            at = pl.ds(pl.multiple_of(n * step, step), step)
-            bb_ref[at] = a_ref[at] * inv_ref[at] + sinv_ref[at]
-            return 0
-
-        lax.fori_loop(0, WIDE // step, right, 0)
-        for sweep in range(SWEEPS):
-            src, dst = refs[sweep % 2], refs[(sweep + 1) % 2]
-            low = number * SWEEPS + sweep + 1
-            high = WIDE - low
-            dst[low:high] = swept(src[low - 1 : high + 1], bb_ref[low:high], cc_ref[low:high], m_ref)
-        if number % 2 == 1:
-            for z in range(NZD):
-                part = jnp.where(odd == 1, NZD - 1 - z, z)
-                o_ref[z, number // 2] = a_ref[pl.ds(HALO + PIECE * part, PIECE)]
-
+    double_step(0, a_ref, b_ref, bb_ref, inv_ref, cc_ref, sinv_ref, m_ref)
+    u_ref[...] = a_ref[HALO : HALO + CHUNK]
     rate = 2.0 * rate_ref[pl.ds(HALO - PIECE + PIECE * sub, 3 * PIECE)]
     inv = 1.0 / (1.0 + 6.0 * rate)
     inv2_ref[...] = inv
     cc2_ref[...] = rate * inv
+
+
+def second_kernel(u_ref, inv_ref, cc_ref, sinv_ref, w_ref, a_ref, b_ref, bb_ref, m_ref):
+    fill_mixer(m_ref)
+    a_ref[...] = u_ref[...]
+    double_step(2, a_ref, b_ref, bb_ref, inv_ref, cc_ref, sinv_ref, m_ref)
+    w_ref[...] = a_ref[HALO : HALO + CHUNK]
+
+
+def difference_kernel(w_ref, next_ref, r_ref, low_ref, high_ref):
+    z, core, odd, _ = position()
+    last = (z == NZD - 1) & (core == 1)
+    for n in range(NZD):
+        part = jnp.where(odd == 1, NZD - 1 - n, n)
+        after = next_ref[pl.ds(PIECE * part, PIECE)]
+        r = jnp.where(last, after, w_ref[pl.ds(PIECE * part, PIECE)]) - after
+        r_ref[n] = r
+        half = low_ref if n < NZD // 2 else high_ref
+        half[n % (NZD // 2)] = r
 
 
 def messages(odd, e, r_next, a_ref, b_ref):
@@ -261,23 +288,12 @@
     b_ref[PIECE:] = jnp.where(odd == 0, head, tail)
 
 
-def residual_kernel(own_ref, oth_ref, r_ref, cp_ref, mine_ref, a_ref, b_ref):
+def residual_kernel(own_ref, oth_ref, r_ref, a_ref, b_ref):
     _, core, _, sub = position()
-    odd = sub % 2
-
-    def uw(t, which):
-        mine, other = own_ref[t // 2, which], oth_ref[t // 2, which]
-        return jnp.where(core == t % 2, mine, other)
-
-    r_ref[0] = jnp.zeros(r_ref.shape[1:], F32)
-    r_ref[1] = uw(0, 0) - uw(0, 0)
-    for t in range(2, NT):
-        r_ref[t] = uw(t - 2, 1) - uw(t - 1, 0)
-    for n in range(NT // 2):
-        even_cp = oth_ref[max(n - 1, 0), 0]
-        cp_ref[n] = jnp.where(core == 0, even_cp, oth_ref[n, 0])
-        mine_ref[n] = jnp.where(core == 0, r_ref[2 * n], r_ref[2 * n + 1])
-    messages(odd, r_ref[1], r_ref[2], a_ref, b_ref)
+    for t in range(1, NT):
+        n = (t // 2 - 1) % NZD
+        r_ref[t] = jnp.where(core == t % 2, own_ref[n], oth_ref[n])
+    messages(sub % 2, r_ref[1], r_ref[2], a_ref, b_ref)
 
 
 def coarse_step(v, inv, cc):
@@ -292,9 +308,10 @@
 def chain_step(t, ra_ref, rb_ref, e_ref, r_ref, inv_ref, cc_ref):
     sub = position()[3]
     odd = sub % 2
+    bottom, top = at_ends()
     ra, rb = ra_ref[...], rb_ref[...]
-    left = jnp.where(odd == 0, rb, ra)
-    right = jnp.where(odd == 0, ra, rb)
+    left = jnp.where(bottom & (sub == 0), 0.0, jnp.where(odd == 0, rb, ra))
+    right = jnp.where(top & (sub == NZD - 1), 0.0, jnp.where(odd == 0, ra, rb))
     e = jnp.concatenate([left[:PIECE], e_ref[...], right[:PIECE]], 0)
     r1 = jnp.concatenate([left[PIECE:], r_ref[t + 1], right[PIECE:]], 0)
     inv, cc = inv_ref[...], cc_ref[...]
@@ -311,31 +328,39 @@
     messages(sub % 2, e2, r_ref[t + 3], a_ref, b_ref)
 
 
-def chain_end_kernel(t, ra_ref, rb_ref, r_ref, inv_ref, cc_ref, cp_ref, mine_ref, *refs):
+def chain_end_kernel(t, ra_ref, rb_ref, r_ref, inv_ref, cc_ref, *refs):
     core = lax.axis_index("core")
     e_refs, o_ref = refs[:-1], refs[-1]
     e1, e2 = chain_step(t, ra_ref, rb_ref, e_refs[-1], r_ref, inv_ref, cc_ref)
     errors = [jnp.zeros(e1.shape, F32)] + [ref[...] for ref in e_refs] + [e1, e2]
     for n in range(NT // 2):
-        o_ref[n, 0] = cp_ref[n] + jnp.where(core == 0, errors[2 * n], errors[2 * n + 1])
-        o_ref[n, 1] = mine_ref[n]
+        o_ref[n] = jnp.where(core == 0, errors[2 * n], errors[2 * n + 1])
 
 
 def last_kernel(
-    g_ref, c_ref, ra_ref, rb_ref, inv_ref, cc_ref, sinv_ref, o_ref, a_ref, b_ref, bb_ref, m_ref, sems
+    e_ref, cp_ref, low_ref, high_ref, c_ref, ra_ref, rb_ref, inv_ref, cc_ref, sinv_ref, o_ref,
+    a_ref, b_ref, bb_ref, m_ref, sems
 ):
     device_z, core, odd, _ = position()
+    first = (device_z == 0) & (core == 0)
     size = CHUNK + 2 * STRIP
     fill_mixer(m_ref)
     for n in range(NZD):
         z = jnp.where(odd == 1, NZD - 1 - n, n)
-        a_ref[STRIP + n * PIECE : STRIP + (n + 1) * PIECE] = g_ref[z, 0]
+        at = n * PIECE
+        a_ref[STRIP + at : STRIP + at + PIECE] = cp_ref[at : at + PIECE] + e_ref[z]
+    for n in range(NZD):
+        at = n * PIECE
         for y in range(PIECE):
-            o_ref[pl.ds(2 * CHUNK + n * PIECE + y, NSP, stride=3 * CHUNK), :] = g_ref[z, 1, y]
-    a_ref[:STRIP] = jnp.where(odd == 0, rb_ref[...], ra_ref[...])
-    a_ref[STRIP + CHUNK : size] = jnp.where(odd == 0, ra_ref[...], rb_ref[...])
-
-    @pl.when((device_z == 0) & (core == 0))
+            half = low_ref if n < NZD // 2 else high_ref
+            part = jnp.where(odd == 1, NZD - 1 - n, n)
+            row = 2 * CHUNK + part * PIECE + y
+            o_ref[pl.ds(row, NSP, stride=3 * CHUNK), :] = jnp.where(first, 0.0, half[n % (NZD // 2), y])
+    bottom, top = at_ends()
+    a_ref[:STRIP] = jnp.where(bottom, 0.0, jnp.where(odd == 0, rb_ref[...], ra_ref[...]))
+    a_ref[STRIP + CHUNK : size] = jnp.where(top, 0.0, jnp.where(odd == 0, ra_ref[...], rb_ref[...]))
+
+    @pl.when(first)
     def _():
         copy = pltpu.make_async_copy(c_ref, a_ref.at[pl.ds(STRIP, CHUNK)], sems.at[0])
         copy.start()
@@ -372,11 +397,11 @@
             outs[which][:, m * 128 : (m + 1) * 128] = jnp.concatenate([low, high], 0).T
 
 
-def strips_kernel(g_ref, c_ref, a_ref, b_ref, head_ref, tail_ref, sems):
+def strips_kernel(e_ref, cp_ref, c_ref, a_ref, b_ref, head_ref, tail_ref, sems):
     z, core, odd, _ = position()
     low, high = odd * (NZD - 1), (1 - odd) * (NZD - 1)
-    head_ref[...] = g_ref[low, 0, :STRIP]
-    tail_ref[...] = g_ref[high, 0, STRIP:]
+    head_ref[...] = cp_ref[:STRIP] + e_ref[low, :STRIP]
+    tail_ref[...] = cp_ref[CHUNK - STRIP :] + e_ref[high, STRIP:]
 
     @pl.when((z == 0) & (core == 0))
     def _():
@@ -411,56 +436,66 @@
     own = call(unpack_kernel, [(WIDE,) + plane], [VMEM])(got)[0]
     oth = swap(own)
 
-    uw, inv2, cc2, inv, cc, sinv, c = call(
-        fine_kernel,
-        [(NZD, 2) + piece]
-        + [(3 * PIECE,) + plane] * 2
-        + [(WIDE,) + plane] * 3
-        + [(CHUNK,) + plane],
+    wide, whole = (WIDE,) + plane, (CHUNK,) + plane
+    ahead, u, inv2, cc2, inv, cc, sinv, c = call(
+        first_kernel,
+        [wide, whole] + [(3 * PIECE,) + plane] * 2 + [wide] * 3 + [whole],
         [VMEM] * 3,
-        [(WIDE,) + plane] * 4,
+        [wide] * 3,
         mixer=True,
     )(got, own, oth)
-
-    mine = lax.all_to_all(uw, "z", 0, 0)
+    after = lax.ppermute(u, everyone, interval_shift(-1))
+    w = call(second_kernel, [whole], [VMEM] * 4, [wide] * 3, mixer=True)(ahead, inv, cc, sinv)[0]
+    half = (NZD // 2,) + piece
+    r, r_low, r_high = call(difference_kernel, [(NZD,) + piece, half, half], [VMEM] * 2)(w, after)
+
+    mine = lax.all_to_all(r, "z", 0, 0)
     other = swap(mine)
-    res, cpoint, res_mine, ma, mb = call(
-        residual_kernel,
-        [(NT,) + piece, (NT // 2,) + piece, (NT // 2,) + piece, message, message],
-        [VMEM] * 2,
+    res, ma, mb = call(
+        residual_kernel, [(NT,) + piece, message, message], [VMEM] * 2
     )(mine, other)
-
     pairs_a, pairs_b = piece_pairs(0), piece_pairs(1)
+    beside = {0: (u, 1), 2: (r_low, 2), 4: (r_high, 2)}
+    moved = []
     errors = [res[1]]
-    for t in range(1, NT - 3, 2):
+    for turn in range(7):
+        t = 2 * turn + 1
         ra = lax.ppermute(ma, everyone, pairs_a)
         rb = lax.ppermute(mb, everyone, pairs_b)
+        if turn in beside:
+            part, step = beside[turn]
+            ra, rb, part = lax.optimization_barrier((ra, rb, part))
+            moved.append(lax.ppermute(part, everyone, interval_shift(step)))
+        if turn == 6:
+            break
         e1, e2, ma, mb = call(
             functools.partial(chain_kernel, t), [piece, piece, message, message], [VMEM] * 6
         )(ra, rb, errors[-1], res, inv2, cc2)
         errors += [e1, e2]
-    ra = lax.ppermute(ma, everyone, pairs_a)
-    rb = lax.ppermute(mb, everyone, pairs_b)
-    corrected = call(
+        if turn - 1 in beside:
+            ma, moved[-1] = lax.optimization_barrier((ma, moved[-1]))
+    cpoint, low, high = moved
+    errors = call(
         functools.partial(chain_end_kernel, NT - 3),
-        [(NZD, 2) + piece],
-        [VMEM] * (7 + len(errors)),
-    )(ra, rb, res, inv2, cc2, cpoint, res_mine, *errors)[0]
-
-    chunk = lax.all_to_all(corrected, "z", 0, 0)
+        [(NZD,) + piece],
+        [VMEM] * (5 + len(errors)),
+    )(ra, rb, res, inv2, cc2, *errors)[0]
+
+    chunk = lax.all_to_all(errors, "z", 0, 0)
     edge = (STRIP,) + plane
-    ma, mb = call(strips_kernel, [edge] * 2, [VMEM, anywhere], [edge] * 2, sems=2)(chunk, c)
-    ra = lax.ppermute(ma, everyone, chunk_pairs(0))
-    rb = lax.ppermute(mb, everyone, chunk_pairs(1))
-    size = CHUNK + 2 * STRIP
+    ma, mb = call(strips_kernel, [edge] * 2, [VMEM] * 2 + [anywhere], [edge] * 2, sems=2)(
+        chunk, cpoint, c
+    )
+    ra = lax.ppermute(ma, "space", chunk_pairs(0))
+    rb = lax.ppermute(mb, "space", chunk_pairs(1))
     sent = call(
         last_kernel,
         [(NSP * 3 * CHUNK, LANES)],
-        [VMEM, anywhere] + [VMEM] * 5,
-        [(size,) + plane] * 3,
+        [VMEM] * 4 + [anywhere] + [VMEM] * 5,
+        [(CHUNK + 2 * STRIP,) + plane] * 3,
         mixer=True,
         sems=1,
-    )(chunk, c, ra, rb, inv, cc, sinv)[0]
+    )(chunk, cpoint, low, high, c, ra, rb, inv, cc, sinv)[0]
     got = lax.all_to_all(sent.reshape(NSP, 3 * CHUNK, LANES), "space", 0, 0)
     fine, residual = call(finish_kernel, [(2, LANES, 1024), (LANES, 1024)], [VMEM])(got)
     return fine.reshape(1, 2, 4, 32, 1024), residual.reshape(1, 4, 32, 1024)

time: 214 us -> 186 us (0.87)
  blocking collectives: 114 us -> 89.6 us
  starting transfers between devices: 33.4 us -> 30.4 us
    all_to_all x2, blocking collectives: 65.4 us -> 42 us  [the longest x1 21.7 us: body(): mine = lax.all_to_all(r, 'z', 0, 0)]
    ppermute x7, starting transfers between devices: 20.9 us -> 7.7 us  [body(): rb = lax.ppermute(mb, everyone, pairs_b)]
    ppermute x7, waiting for transfers between devices: 3.91 us -> 16.7 us  [body(): ra = lax.ppermute(ma, everyone, pairs_a)]
    ppermute x7, waiting for transfers between devices: 20.9 us -> 8.8 us  [body(): rb = lax.ppermute(mb, everyone, pairs_b)]
    ppermute x2 -> x6, starting transfers between devices: 3.97 us -> 11.3 us  [the longest x1 5.61 us: body(): after = lax.ppermute(u, everyone, interval_shift(-1))]
    ppermute x7, starting transfers between devices: 8.41 us -> 11.2 us  [body(): ra = lax.ppermute(ma, everyone, pairs_a)]
    ppermute x2 -> x6, waiting for transfers between devices: 4.28 us -> 6.43 us  [the longest x1 2.86 us: body(): after = lax.ppermute(u, everyone, interval_shift(-1))]
    pallas_call x5 -> x7, Pallas kernels: 14.9 us -> 14.2 us  [the longest x1 5.34 us: body(): call(first_kernel, [wide, whole] + [(3 * PIECE,) + plane] * 2 + [wide] *...]
  transfers between devices with their start and end apart: 18 -> 22, of which waited for: 17 -> 18; matrix products, arithmetic and copies ran while one was open for 0% -> 0% of each run, Pallas kernels for 0% -> 7%
where the time goes in v3:
time: 186 us
  blocking collectives  89.6 us (48%)
  waiting for transfers between devices  36 us (19%)
  starting transfers between devices  30.4 us (16%)
  Pallas kernels  29 us (16%)
    all_to_all x1, blocking collectives, body(): got = lax.all_to_all(sent, 'space', 0, 0).reshape(-1, LANES)  28.4 us
    all_to_all x1, blocking collectives, body(): mine = lax.all_to_all(r, 'z', 0, 0)  21.7 us
    all_to_all x1, blocking collectives, body(): chunk = lax.all_to_all(errors, 'z', 0, 0)  20.3 us
    all_to_all x1, blocking collectives, body(): got = lax.all_to_all(sent.reshape(NSP, 3 * CHUNK, LANES), 'space', 0, 0)  19.2 us
    ppermute x7, waiting for transfers between devices, body(): ra = lax.ppermute(ma, everyone, pairs_a)  16.7 us
    ppermute x7, starting transfers between devices, body(): ra = lax.ppermute(ma, everyone, pairs_a)  11.2 us
    ppermute x7, waiting for transfers between devices, body(): rb = lax.ppermute(mb, everyone, pairs_b)  8.8 us
    pallas_call x6, Pallas kernels, body(): call(functools.partial(chain_kernel, t), [piece, piece, message, message]...  8.76 us
  transfers between devices with their start and end apart: 22, of which 18 were waited for; matrix products, arithmetic and copies ran while one was open for 0% of the time, Pallas kernels for 7%

profile of v3, /device:TPU:8, one launch (start us, length us, event | category | flops | bytes accessed | tf_op | source)
XLA Modules:
  0.0 185.9 jit_solution(17009697563142573487)
XLA Ops:
  0.6 4.1 %shard_map.50 = f32[16,192,128]{2,1,0:T(8,128)} custom-call(f32[128,1024]{1,0:T(8,128)} %bitcast.12, f32[128,1024]{1,0:T(8,128)} %bitcast.13, f32[128,1024]{1,0:T(8,128)} %bitcast.14), custom_call_target="tpu_custom_call" | custom-call | tf_op jit(solution)/shard_map/pallas_call | solution.py:432
  4.7 28.4 %all_to_all.20 = f32[16,192,128]{2,1,0:T(8,128)S(1)} all-to-all(f32[16,192,128]{2,1,0:T(8,128)} %shard_map.50), channel_id=1, replica_groups=mesh['z'=8,'core'=2,'space'=16] {'space'}, dimensions={0} | all-to-all | bytes 3145728 | tf_op jit(solution)/shard_map/all_to_all | solution.py:435
  33.7 2.3 %collective-permute-done.oth_ref = f32[96,16,128]{2,1,0:T(8,128)S(1)} collective-permute-done((f32[96,16,128]{2,1,0:T(8,128)S(1)}, f32[96,16,128]{2,1,0:T(8,128)S(1)}, u32[]{:S(2)}, u32[]{:S(2)}) %collective-permute-start) | collective-permute-done | bytes 786464 | tf_op jit(solution)/shard_map/ppermute | solution.py:430
  36.0 5.3 %shard_map.52 = (f32[96,16,128]{2,1,0:T(8,128)S(1)}, f32[64,16,128]{2,1,0:T(8,128)S(1)}, f32[24,16,128]{2,1,0:T(8,128)S(1)}, f32[24,16,128]{2,1,0:T(8,128)S(1)},...) custom-call(f32[3072,128]{1,0:T(8,128)S(1)} %bitcast.10, ...), custom_call_target="tpu_custom_call" | custom-call | tf_op jit(solution)/shard_map/pallas_call | solution.py:440
  41.3 5.6 %collective-permute-start.1 = (f32[64,16,128]{2,1,0:T(8,128)S(1)}, f32[64,16,128]{2,1,0:T(8,128)S(1)}, u32[]{:S(2)}, u32[]{:S(2)}) collective-permute-start(f32[64,16,128]{2,1,0:T(8,128)S(1)} %get-tuple-element.76), channel_id=1, source_target_pairs={{0,240},{1,241},{2,242},{3,243},{4,244},{5,245},{6,246},{7,247},{8... | collective-permute-start | bytes 1572872 | tf_op jit(solution)/shard_map/ppermute | solution.py:447
  46.9 3.8 %shard_map.53.w_ref = f32[64,16,128]{2,1,0:T(8,128)S(1)} custom-call(f32[96,16,128]{2,1,0:T(8,128)S(1)} %get-tuple-element.59.u_ref, f32[96,16,128]{2,1,0:T(8,128)S(1)} %get-tuple-element.60.inv_ref, f32[96,16,128]{2,1,0:T(8,128)S(1)} %get-tuple-element.61.cc_ref, f32[96,16,128]{2,1,0:T(8,128)S(1)} %get-tuple-element.62.sinv_ref), custom_call_target="tpu_custom_call" | custom-call | tf_op jit(solution)/shard_map/pallas_call | solution.py:448
  50.8 2.9 %collective-permute-done.1.next_ref = f32[64,16,128]{2,1,0:T(8,128)S(1)} collective-permute-done((f32[64,16,128]{2,1,0:T(8,128)S(1)}, f32[64,16,128]{2,1,0:T(8,128)S(1)}, u32[]{:S(2)}, u32[]{:S(2)}) %collective-permute-start.1) | collective-permute-done | bytes 524320 | tf_op jit(solution)/shard_map/ppermute | solution.py:447
  53.7 21.7 %all_to_all.21.own_ref = f32[8,8,16,128]{3,2,1,0:T(8,128)S(1)} all-to-all(f32[8,8,16,128]{3,2,1,0:T(8,128)S(1)} %get-tuple-element.64), channel_id=1, replica_groups=mesh['z'=8,'core'=2,'space'=16] {'z'}, dimensions={0} | all-to-all | bytes 1048576 | tf_op jit(solution)/shard_map/all_to_all | solution.py:452
  75.6 1.8 collective-permute-done.2.oth_ref
  77.7 1.1 collective-permute-start.4
  78.9 3.5 %collective-permute-done.3.ra_ref = f32[12,16,128]{2,1,0:T(8,128)S(1)} collective-permute-done((f32[12,16,128]{2,1,0:T(8,128)S(1)}, f32[12,16,128]{2,1,0:T(8,128)S(1)}, u32[]{:S(2)}, u32[]{:S(2)}) %collective-permute-start.3) | collective-permute-done | bytes 98336 | tf_op jit(solution)/shard_map/ppermute | solution.py:463
  82.7 1.5 shard_map.56
  84.2 1.6 collective-permute-start.5
  85.8 1.0 collective-permute-start.6
  86.8 2.5 %collective-permute-done.5.ra_ref = f32[12,16,128]{2,1,0:T(8,128)S(1)} collective-permute-done((f32[12,16,128]{2,1,0:T(8,128)S(1)}, f32[12,16,128]{2,1,0:T(8,128)S(1)}, u32[]{:S(2)}, u32[]{:S(2)}) %collective-permute-start.5) | collective-permute-done | bytes 98336 | tf_op jit(solution)/shard_map/ppermute | solution.py:463
  89.3 1.4 collective-permute-done.6.rb_ref
  90.7 1.5 shard_map.57
  92.1 1.1 collective-permute-start.9
  93.3 1.5 collective-permute-start.8
  94.8 2.2 %collective-permute-done.9.rb_ref = f32[12,16,128]{2,1,0:T(8,128)S(1)} collective-permute-done((f32[12,16,128]{2,1,0:T(8,128)S(1)}, f32[12,16,128]{2,1,0:T(8,128)S(1)}, u32[]{:S(2)}, u32[]{:S(2)}) %collective-permute-start.9) | collective-permute-done | bytes 98336 | tf_op jit(solution)/shard_map/ppermute | solution.py:464
  97.0 1.4 collective-permute-done.8.ra_ref
  98.4 1.6 collective-permute-start.12
  100.0 1.5 shard_map.58
  101.5 1.1 collective-permute-start.11
  102.6 5.5 %collective-permute-done.10.ra_ref = f32[12,16,128]{2,1,0:T(8,128)S(1)} collective-permute-done((f32[12,16,128]{2,1,0:T(8,128)S(1)}, f32[12,16,128]{2,1,0:T(8,128)S(1)}, u32[]{:S(2)}, u32[]{:S(2)}) %collective-permute-start.10) | collective-permute-done | bytes 98336 | tf_op jit(solution)/shard_map/ppermute | solution.py:463
  108.2 1.5 shard_map.59
  109.6 1.1 collective-permute-start.14
  110.7 2.0 %collective-permute-start.13 = (f32[12,16,128]{2,1,0:T(8,128)S(1)}, f32[12,16,128]{2,1,0:T(8,128)S(1)}, u32[]{:S(2)}, u32[]{:S(2)}) collective-permute-start(f32[12,16,128]{2,1,0:T(8,128)S(1)} %get-tuple-element.88), channel_id=1, source_target_pairs={{0,32},{32,0},{64,96},{96,64},{128,160},{160,128},{192,224},{224,1... | collective-permute-start | bytes 294920 | tf_op jit(solution)/shard_map/ppermute | solution.py:463
  112.8 1.5 collective-permute-done.14.rb_ref
  114.3 1.0 collective-permute-done.13.ra_ref
  115.4 2.0 %collective-permute-start.17 = (f32[4,8,16,128]{3,2,1,0:T(8,128)S(1)}, f32[4,8,16,128]{3,2,1,0:T(8,128)S(1)}, u32[]{:S(2)}, u32[]{:S(2)}) collective-permute-start(f32[4,8,16,128]{3,2,1,0:T(8,128)S(1)} %get-tuple-element.98), channel_id=1, source_target_pairs={{0,32},{1,33},{2,34},{3,35},{4,36},{5,37},{6,38},{7,39},{8,40},{9,... | collective-permute-start | bytes 786440 | tf_op jit(solution)/shard_map/ppermute | solution.py:468
  117.4 1.5 shard_map.60
  118.9 3.5 %collective-permute-start.15 = (f32[12,16,128]{2,1,0:T(8,128)S(1)}, f32[12,16,128]{2,1,0:T(8,128)S(1)}, u32[]{:S(2)}, u32[]{:S(2)}) collective-permute-start(f32[12,16,128]{2,1,0:T(8,128)S(1)} %get-tuple-element.94), channel_id=1, source_target_pairs={{0,32},{32,0},{64,96},{96,64},{128,160},{160,128},{192,224},{224,1... | collective-permute-start | bytes 294920 | tf_op jit(solution)/shard_map/ppermute | solution.py:463
  123.4 1.6 collective-permute-done.15.ra_ref
  125.0 2.0 %collective-permute-done.16.rb_ref = f32[12,16,128]{2,1,0:T(8,128)S(1)} collective-permute-done((f32[12,16,128]{2,1,0:T(8,128)S(1)}, f32[12,16,128]{2,1,0:T(8,128)S(1)}, u32[]{:S(2)}, u32[]{:S(2)}) %collective-permute-start.16) | collective-permute-done | bytes 98336 | tf_op jit(solution)/shard_map/ppermute | solution.py:464
  127.0 1.5 shard_map.61
  128.4 1.1 collective-permute-start.19
  129.6 2.2 %collective-permute-start.18 = (f32[12,16,128]{2,1,0:T(8,128)S(1)}, f32[12,16,128]{2,1,0:T(8,128)S(1)}, u32[]{:S(2)}, u32[]{:S(2)}) collective-permute-start(f32[12,16,128]{2,1,0:T(8,128)S(1)} %get-tuple-element.99), channel_id=1, source_target_pairs={{0,32},{32,0},{64,96},{96,64},{128,160},{160,128},{192,224},{224,1... | collective-permute-start | bytes 294920 | tf_op jit(solution)/shard_map/ppermute | solution.py:463
  131.8 1.4 collective-permute-done.19.rb_ref
  133.1 1.2 collective-permute-done.18.ra_ref
  134.4 1.5 shard_map.62
  135.9 20.3 %all_to_all.22.e_ref = f32[8,8,16,128]{3,2,1,0:T(8,128)S(1)} all-to-all(f32[8,8,16,128]{3,2,1,0:T(8,128)S(1)} %shard_map.62), channel_id=1, replica_groups=mesh['z'=8,'core'=2,'space'=16] {'z'}, dimensions={0} | all-to-all | bytes 1048576 | tf_op jit(solution)/shard_map/all_to_all | solution.py:484
  156.3 1.7 collective-permute-start.20
  158.4 1.9 %collective-permute-done.20.ra_ref = f32[4,16,128]{2,1,0:T(8,128)S(1)} collective-permute-done((f32[4,16,128]{2,1,0:T(8,128)S(1)}, f32[4,16,128]{2,1,0:T(8,128)S(1)}, u32[]{:S(2)}, u32[]{:S(2)}) %collective-permute-start.20) | collective-permute-done | bytes 32800 | tf_op jit(solution)/shard_map/ppermute | solution.py:489
  160.3 1.6 collective-permute-done.21.rb_ref
  161.9 3.3 %shard_map.64 = f32[3072,128]{1,0:T(8,128)S(1)} custom-call(f32[8,8,16,128]{3,2,1,0:T(8,128)S(1)} %all_to_all.22.e_ref, f32[64,16,128]{2,1,0:T(8,128)S(1)} %collective-permute-done.7.cp_ref, f32[4,8,16,128]{3,2,1,0:T(8,128)S(1)} %collective-permute-done.12.low_ref, f32[4,8,16,128]{3,2,1,0:T(8,128)S(1)} %collective-permute-done.17.high_ref, ...), custom_call_target="tpu_custom_call" | custom-call | tf_op jit(solution)/shard_map/pallas_call | solution.py:491
  165.2 19.2 %all_to_all.23.a_ref = f32[16,192,128]{2,1,0:T(8,128)S(1)} all-to-all(f32[16,192,128]{2,1,0:T(8,128)S(1)} %bitcast.11), channel_id=1, replica_groups=mesh['z'=8,'core'=2,'space'=16] {'space'}, dimensions={0} | all-to-all | bytes 3145728 | tf_op jit(solution)/shard_map/all_to_all | solution.py:499
  184.4 1.5 shard_map.65
  (17 shorter events, 3.0 us)
Async XLA Ops:
  33.6 2.4 %collective-permute-start = (f32[96,16,128]{2,1,0:T(8,128)S(1)}, f32[96,16,128]{2,1,0:T(8,128)S(1)}, u32[]{:S(2)}, u32[]{:S(2)}) collective-permute-start(f32[96,16,128]{2,1,0:T(8,128)S(1)} %shard_map.51.own_ref), channel_id=1, source_target_pairs={{0,16},{16,0},{1,17},{17,1},{2,18},{18,2},{3,19},{19,3},{4,20},{20... | collective-permute-start | bytes 2359304 | tf_op jit(solution)/shard_map/ppermute | solution.py:430
  41.3 12.3 %collective-permute-start.1 = (f32[64,16,128]{2,1,0:T(8,128)S(1)}, f32[64,16,128]{2,1,0:T(8,128)S(1)}, u32[]{:S(2)}, u32[]{:S(2)}) collective-permute-start(f32[64,16,128]{2,1,0:T(8,128)S(1)} %get-tuple-element.76), channel_id=1, source_target_pairs={{0,240},{1,241},{2,242},{3,243},{4,244},{5,245},{6,246},{7,247},{8... | collective-permute-start | bytes 1572872 | tf_op jit(solution)/shard_map/ppermute | solution.py:447
  75.5 1.9 %collective-permute-start.2 = (f32[8,8,16,128]{3,2,1,0:T(8,128)S(1)}, f32[8,8,16,128]{3,2,1,0:T(8,128)S(1)}, u32[]{:S(2)}, u32[]{:S(2)}) collective-permute-start(f32[8,8,16,128]{3,2,1,0:T(8,128)S(1)} %all_to_all.21.own_ref), channel_id=1, source_target_pairs={{0,16},{16,0},{1,17},{17,1},{2,18},{18,2},{3,19},{19,3},{4,20},{20... | collective-permute-start | bytes 1572872 | tf_op jit(solution)/shard_map/ppermute | solution.py:430
  77.5 4.9 %collective-permute-start.3 = (f32[12,16,128]{2,1,0:T(8,128)S(1)}, f32[12,16,128]{2,1,0:T(8,128)S(1)}, u32[]{:S(2)}, u32[]{:S(2)}) collective-permute-start(f32[12,16,128]{2,1,0:T(8,128)S(1)} %get-tuple-element.65), channel_id=1, source_target_pairs={{0,32},{32,0},{64,96},{96,64},{128,160},{160,128},{192,224},{224,1... | collective-permute-start | bytes 294920 | tf_op jit(solution)/shard_map/ppermute | solution.py:463
  77.7 4.9 %collective-permute-start.4 = (f32[12,16,128]{2,1,0:T(8,128)S(1)}, f32[12,16,128]{2,1,0:T(8,128)S(1)}, u32[]{:S(2)}, u32[]{:S(2)}) collective-permute-start(f32[12,16,128]{2,1,0:T(8,128)S(1)} %get-tuple-element.66), channel_id=1, source_target_pairs={{32,64},{64,32},{96,128},{128,96},{160,192},{192,160},{224,225},{2... | collective-permute-start | bytes 294920 | tf_op jit(solution)/shard_map/ppermute | solution.py:464
  82.7 10.6 %collective-permute-start.7 = (f32[64,16,128]{2,1,0:T(8,128)S(1)}, f32[64,16,128]{2,1,0:T(8,128)S(1)}, u32[]{:S(2)}, u32[]{:S(2)}) collective-permute-start(f32[64,16,128]{2,1,0:T(8,128)S(1)} %get-tuple-element.76), channel_id=1, source_target_pairs={{0,16},{1,17},{2,18},{3,19},{4,20},{5,21},{6,22},{7,23},{8,24},{9,... | collective-permute-start | bytes 1572872 | tf_op jit(solution)/shard_map/ppermute | solution.py:468
  84.2 5.1 %collective-permute-start.5 = (f32[12,16,128]{2,1,0:T(8,128)S(1)}, f32[12,16,128]{2,1,0:T(8,128)S(1)}, u32[]{:S(2)}, u32[]{:S(2)}) collective-permute-start(f32[12,16,128]{2,1,0:T(8,128)S(1)} %get-tuple-element.72), channel_id=1, source_target_pairs={{0,32},{32,0},{64,96},{96,64},{128,160},{160,128},{192,224},{224,1... | collective-permute-start | bytes 294920 | tf_op jit(solution)/shard_map/ppermute | solution.py:463
  85.8 4.9 %collective-permute-start.6 = (f32[12,16,128]{2,1,0:T(8,128)S(1)}, f32[12,16,128]{2,1,0:T(8,128)S(1)}, u32[]{:S(2)}, u32[]{:S(2)}) collective-permute-start(f32[12,16,128]{2,1,0:T(8,128)S(1)} %get-tuple-element.73), channel_id=1, source_target_pairs={{32,64},{64,32},{96,128},{128,96},{160,192},{192,160},{224,225},{2... | collective-permute-start | bytes 294920 | tf_op jit(solution)/shard_map/ppermute | solution.py:464
  92.1 4.9 %collective-permute-start.9 = (f32[12,16,128]{2,1,0:T(8,128)S(1)}, f32[12,16,128]{2,1,0:T(8,128)S(1)}, u32[]{:S(2)}, u32[]{:S(2)}) collective-permute-start(f32[12,16,128]{2,1,0:T(8,128)S(1)} %get-tuple-element.78), channel_id=1, source_target_pairs={{32,64},{64,32},{96,128},{128,96},{160,192},{192,160},{224,225},{2... | collective-permute-start | bytes 294920 | tf_op jit(solution)/shard_map/ppermute | solution.py:464
  93.3 5.1 %collective-permute-start.8 = (f32[12,16,128]{2,1,0:T(8,128)S(1)}, f32[12,16,128]{2,1,0:T(8,128)S(1)}, u32[]{:S(2)}, u32[]{:S(2)}) collective-permute-start(f32[12,16,128]{2,1,0:T(8,128)S(1)} %get-tuple-element.77), channel_id=1, source_target_pairs={{0,32},{32,0},{64,96},{96,64},{128,160},{160,128},{192,224},{224,1... | collective-permute-start | bytes 294920 | tf_op jit(solution)/shard_map/ppermute | solution.py:463
  98.4 12.4 %collective-permute-start.12 = (f32[4,8,16,128]{3,2,1,0:T(8,128)S(1)}, f32[4,8,16,128]{3,2,1,0:T(8,128)S(1)}, u32[]{:S(2)}, u32[]{:S(2)}) collective-permute-start(f32[4,8,16,128]{3,2,1,0:T(8,128)S(1)} %get-tuple-element.87), channel_id=1, source_target_pairs={{0,32},{1,33},{2,34},{3,35},{4,36},{5,37},{6,38},{7,39},{8,40},{9,... | collective-permute-start | bytes 786440 | tf_op jit(solution)/shard_map/ppermute | solution.py:468
  101.4 6.7 %collective-permute-start.10 = (f32[12,16,128]{2,1,0:T(8,128)S(1)}, f32[12,16,128]{2,1,0:T(8,128)S(1)}, u32[]{:S(2)}, u32[]{:S(2)}) collective-permute-start(f32[12,16,128]{2,1,0:T(8,128)S(1)} %get-tuple-element.83), channel_id=1, source_target_pairs={{0,32},{32,0},{64,96},{96,64},{128,160},{160,128},{192,224},{224,1... | collective-permute-start | bytes 294920 | tf_op jit(solution)/shard_map/ppermute | solution.py:463
  101.5 6.6 %collective-permute-start.11 = (f32[12,16,128]{2,1,0:T(8,128)S(1)}, f32[12,16,128]{2,1,0:T(8,128)S(1)}, u32[]{:S(2)}, u32[]{:S(2)}) collective-permute-start(f32[12,16,128]{2,1,0:T(8,128)S(1)} %get-tuple-element.84), channel_id=1, source_target_pairs={{32,64},{64,32},{96,128},{128,96},{160,192},{192,160},{224,225},{2... | collective-permute-start | bytes 294920 | tf_op jit(solution)/shard_map/ppermute | solution.py:464
  109.6 4.7 %collective-permute-start.14 = (f32[12,16,128]{2,1,0:T(8,128)S(1)}, f32[12,16,128]{2,1,0:T(8,128)S(1)}, u32[]{:S(2)}, u32[]{:S(2)}) collective-permute-start(f32[12,16,128]{2,1,0:T(8,128)S(1)} %get-tuple-element.89), channel_id=1, source_target_pairs={{32,64},{64,32},{96,128},{128,96},{160,192},{192,160},{224,225},{2... | collective-permute-start | bytes 294920 | tf_op jit(solution)/shard_map/ppermute | solution.py:464
  110.7 4.6 %collective-permute-start.13 = (f32[12,16,128]{2,1,0:T(8,128)S(1)}, f32[12,16,128]{2,1,0:T(8,128)S(1)}, u32[]{:S(2)}, u32[]{:S(2)}) collective-permute-start(f32[12,16,128]{2,1,0:T(8,128)S(1)} %get-tuple-element.88), channel_id=1, source_target_pairs={{0,32},{32,0},{64,96},{96,64},{128,160},{160,128},{192,224},{224,1... | collective-permute-start | bytes 294920 | tf_op jit(solution)/shard_map/ppermute | solution.py:463
  115.4 14.2 %collective-permute-start.17 = (f32[4,8,16,128]{3,2,1,0:T(8,128)S(1)}, f32[4,8,16,128]{3,2,1,0:T(8,128)S(1)}, u32[]{:S(2)}, u32[]{:S(2)}) collective-permute-start(f32[4,8,16,128]{3,2,1,0:T(8,128)S(1)} %get-tuple-element.98), channel_id=1, source_target_pairs={{0,32},{1,33},{2,34},{3,35},{4,36},{5,37},{6,38},{7,39},{8,40},{9,... | collective-permute-start | bytes 786440 | tf_op jit(solution)/shard_map/ppermute | solution.py:468
  118.9 6.1 %collective-permute-start.15 = (f32[12,16,128]{2,1,0:T(8,128)S(1)}, f32[12,16,128]{2,1,0:T(8,128)S(1)}, u32[]{:S(2)}, u32[]{:S(2)}) collective-permute-start(f32[12,16,128]{2,1,0:T(8,128)S(1)} %get-tuple-element.94), channel_id=1, source_target_pairs={{0,32},{32,0},{64,96},{96,64},{128,160},{160,128},{192,224},{224,1... | collective-permute-start | bytes 294920 | tf_op jit(solution)/shard_map/ppermute | solution.py:463
  122.4 4.6 %collective-permute-start.16 = (f32[12,16,128]{2,1,0:T(8,128)S(1)}, f32[12,16,128]{2,1,0:T(8,128)S(1)}, u32[]{:S(2)}, u32[]{:S(2)}) collective-permute-start(f32[12,16,128]{2,1,0:T(8,128)S(1)} %get-tuple-element.95), channel_id=1, source_target_pairs={{32,64},{64,32},{96,128},{128,96},{160,192},{192,160},{224,225},{2... | collective-permute-start | bytes 294920 | tf_op jit(solution)/shard_map/ppermute | solution.py:464
  128.4 4.7 %collective-permute-start.19 = (f32[12,16,128]{2,1,0:T(8,128)S(1)}, f32[12,16,128]{2,1,0:T(8,128)S(1)}, u32[]{:S(2)}, u32[]{:S(2)}) collective-permute-start(f32[12,16,128]{2,1,0:T(8,128)S(1)} %get-tuple-element.100), channel_id=1, source_target_pairs={{32,64},{64,32},{96,128},{128,96},{160,192},{192,160},{224,225},{2... | collective-permute-start | bytes 294920 | tf_op jit(solution)/shard_map/ppermute | solution.py:464
  129.6 4.8 %collective-permute-start.18 = (f32[12,16,128]{2,1,0:T(8,128)S(1)}, f32[12,16,128]{2,1,0:T(8,128)S(1)}, u32[]{:S(2)}, u32[]{:S(2)}) collective-permute-start(f32[12,16,128]{2,1,0:T(8,128)S(1)} %get-tuple-element.99), channel_id=1, source_target_pairs={{0,32},{32,0},{64,96},{96,64},{128,160},{160,128},{192,224},{224,1... | collective-permute-start | bytes 294920 | tf_op jit(solution)/shard_map/ppermute | solution.py:463
  156.3 4.0 %collective-permute-start.20 = (f32[4,16,128]{2,1,0:T(8,128)S(1)}, f32[4,16,128]{2,1,0:T(8,128)S(1)}, u32[]{:S(2)}, u32[]{:S(2)}) collective-permute-start(f32[4,16,128]{2,1,0:T(8,128)S(1)} %get-tuple-element.112), channel_id=1, source_target_pairs={{0,1},{1,0},{2,3},{3,2},{7,6},{6,7},{5,4},{4,5},{8,9},{9,8},{10,11... | collective-permute-start | bytes 98312 | tf_op jit(solution)/shard_map/ppermute | solution.py:489
  158.0 3.9 %collective-permute-start.21 = (f32[4,16,128]{2,1,0:T(8,128)S(1)}, f32[4,16,128]{2,1,0:T(8,128)S(1)}, u32[]{:S(2)}, u32[]{:S(2)}) collective-permute-start(f32[4,16,128]{2,1,0:T(8,128)S(1)} %get-tuple-element.113), channel_id=1, source_target_pairs={{1,2},{2,1},{3,7},{7,3},{6,5},{5,6},{4,8},{8,4},{9,10},{10,9},{11,... | collective-permute-start | bytes 98312 | tf_op jit(solution)/shard_map/ppermute | solution.py:490

commit v4 on v3

--- a/solution.py
+++ b/solution.py
@@ -17,6 +17,7 @@
 NZD = 8
 NSP = 16
 LANES = 128
+BLOCK = 32
 F32 = jnp.float32
 
 VMEM = pl.BlockSpec(memory_space=pltpu.VMEM)
@@ -25,18 +26,19 @@
 BF16 = jnp.bfloat16
 
 
-def call(kernel, out, specs, scratch=(), mixer=False, sems=0, limit=LIMIT):
+def call(kernel, out, specs, scratch=(), mixer=False, sems=(), limit=LIMIT, aliases=None, to=VMEM):
     outs = [jax.ShapeDtypeStruct(s, F32) for s in out]
     scratch = [pltpu.VMEM(s, F32) for s in scratch]
     if mixer:
         scratch.append(pltpu.VMEM((2 * LANES, 2 * LANES), BF16))
-    if sems:
-        scratch.append(pltpu.SemaphoreType.DMA((sems,)))
+    for count in sems:
+        scratch.append(pltpu.SemaphoreType.DMA(count))
     return pl.pallas_call(
         kernel,
         out_shape=outs,
         in_specs=specs,
-        out_specs=[VMEM] * len(out),
+        out_specs=[to] * len(out),
+        input_output_aliases=aliases or {},
         scratch_shapes=scratch,
         compiler_params=pltpu.CompilerParams(vmem_limit_bytes=limit),
     )
@@ -147,16 +149,21 @@
 def lateral(v, m_ref):
     if m_ref is None:
         return rolled(v)
-    cut = v.shape[0] // 3
-    return jnp.concatenate([rolled(v[:cut]), mixed(v[cut:], m_ref)], 0)
+    sums = []
+    for first in range(0, v.shape[0], BLOCK):
+        block = v[first : first + BLOCK]
+        cut = block.shape[0] // 4
+        if cut > 0:
+            sums.append(rolled(block[:cut]))
+        sums.append(mixed(block[cut:], m_ref))
+    return jnp.concatenate(sums, 0)
 
 
 def swept(v, bb, cc, m_ref=None):
     return bb + cc * (lateral(v[1:-1], m_ref) + v[2:] + v[:-2])
 
 
-def prep_kernel(c_ref, s_ref, r_ref, o_ref, v_ref, q_ref, sems):
-    core = lax.axis_index("core")
+def prep_kernel(c_ref, s_ref, r_ref, out_ref, v_ref, q_ref, o_ref, sems, out_sems):
     zero = jnp.zeros((HALO, LANES), F32)
 
     def copies(ref, to, first):
@@ -168,6 +175,19 @@
         ]
 
     def spread(arriving, ref, base):
+        leaving = []
+
+        def send(k):
+            rows = pl.ds(base, WIDE)
+            leaving.append(
+                pltpu.make_async_copy(
+                    o_ref.at[SNAKE[k], rows], out_ref.at[SNAKE[k], rows], out_sems.at[base // WIDE, k]
+                )
+            )
+            leaving[-1].start()
+
+        o_ref[SNAKE[0], base : base + HALO] = zero
+        o_ref[SNAKE[NSP - 1], base + HALO + CHUNK : base + WIDE] = zero
         for m in range(8):
             arriving[m].wait()
             tile = ref[:, m * LANES : (m + 1) * LANES].T
@@ -177,30 +197,29 @@
                 o_ref[SNAKE[k], base + HALO : base + HALO + CHUNK] = part
                 if k > 0:
                     o_ref[SNAKE[k - 1], base + HALO + CHUNK : base + WIDE] = part[:HALO]
+                    send(k - 1)
                 if k < NSP - 1:
                     o_ref[SNAKE[k + 1], base : base + HALO] = part[CHUNK - HALO :]
-        o_ref[SNAKE[0], base : base + HALO] = zero
-        o_ref[SNAKE[NSP - 1], base + HALO + CHUNK : base + WIDE] = zero
-
-    states = copies(c_ref, v_ref, 0)
-    for copy in states:
-        copy.start()
+        send(NSP - 1)
+        return leaving
+
+    def work(ref):
+        states, fields = copies(c_ref, v_ref, 0), copies(ref, q_ref, 8)
+        for copy in states + fields:
+            copy.start()
+        leaving = spread(states, v_ref, 0) + spread(fields, q_ref, WIDE)
+        for copy in leaving:
+            copy.wait()
+
+    core = lax.axis_index("core")
 
     @pl.when(core == 0)
     def _():
-        fields = copies(s_ref, q_ref, 8)
-        for copy in fields:
-            copy.start()
-        spread(fields, q_ref, WIDE)
+        work(s_ref)
 
     @pl.when(core != 0)
     def _():
-        fields = copies(r_ref, q_ref, 8)
-        for copy in fields:
-            copy.start()
-        spread(fields, q_ref, WIDE)
-
-    spread(states, v_ref, 0)
+        work(r_ref)
 
 
 def unpack_kernel(a_ref, q_ref):
@@ -337,64 +356,85 @@
         o_ref[n] = jnp.where(core == 0, errors[2 * n], errors[2 * n + 1])
 
 
-def last_kernel(
-    e_ref, cp_ref, low_ref, high_ref, c_ref, ra_ref, rb_ref, inv_ref, cc_ref, sinv_ref, o_ref,
+def keep(o_ref, which, values_ref, low, high):
+    def one(y, _):
+        o_ref[pl.ds(which * CHUNK + y, NSP, stride=3 * CHUNK), :] = values_ref[y]
+        return 0
+
+    lax.fori_loop(low, high, one, 0, unroll=8)
+
+
+def inner_kernel(
+    e_ref, cp_ref, low_ref, high_ref, c_ref, inv_ref, cc_ref, sinv_ref, o_ref, edge_ref,
     a_ref, b_ref, bb_ref, m_ref, sems
 ):
-    device_z, core, odd, _ = position()
-    first = (device_z == 0) & (core == 0)
-    size = CHUNK + 2 * STRIP
+    z, core, odd, _ = position()
+    first = (z == 0) & (core == 0)
     fill_mixer(m_ref)
     for n in range(NZD):
-        z = jnp.where(odd == 1, NZD - 1 - n, n)
         at = n * PIECE
-        a_ref[STRIP + at : STRIP + at + PIECE] = cp_ref[at : at + PIECE] + e_ref[z]
-    for n in range(NZD):
-        at = n * PIECE
-        for y in range(PIECE):
-            half = low_ref if n < NZD // 2 else high_ref
-            part = jnp.where(odd == 1, NZD - 1 - n, n)
-            row = 2 * CHUNK + part * PIECE + y
-            o_ref[pl.ds(row, NSP, stride=3 * CHUNK), :] = jnp.where(first, 0.0, half[n % (NZD // 2), y])
-    bottom, top = at_ends()
-    a_ref[:STRIP] = jnp.where(bottom, 0.0, jnp.where(odd == 0, rb_ref[...], ra_ref[...]))
-    a_ref[STRIP + CHUNK : size] = jnp.where(top, 0.0, jnp.where(odd == 0, ra_ref[...], rb_ref[...]))
+        a_ref[at : at + PIECE] = cp_ref[at : at + PIECE] + e_ref[jnp.where(odd == 1, NZD - 1 - n, n)]
 
     @pl.when(first)
     def _():
-        copy = pltpu.make_async_copy(c_ref, a_ref.at[pl.ds(STRIP, CHUNK)], sems.at[0])
+        copy = pltpu.make_async_copy(c_ref, a_ref, sems.at[0])
         copy.start()
         copy.wait()
 
-    off = HALO - STRIP
-    bb_ref[...] = a_ref[...] * inv_ref[off : off + size] + sinv_ref[off : off + size]
-
-    def keep(which):
-        def one(y, _):
-            o_ref[pl.ds(which * CHUNK + y, NSP, stride=3 * CHUNK), :] = a_ref[STRIP + y]
-            return 0
-
-        lax.fori_loop(0, CHUNK, one, 0, unroll=8)
-
-    keep(0)
+    bb_ref[...] = a_ref[...] * inv_ref[HALO : HALO + CHUNK] + sinv_ref[HALO : HALO + CHUNK]
+    edge_ref[0] = a_ref[: 2 * STRIP]
+    edge_ref[1] = a_ref[CHUNK - 2 * STRIP :]
+    keep(o_ref, 0, a_ref, 0, CHUNK)
     refs = [a_ref, b_ref]
     for sweep in range(SWEEPS):
         src, dst = refs[sweep % 2], refs[(sweep + 1) % 2]
         low = sweep + 1
-        high = size - low
+        high = CHUNK - low
         dst[low:high] = swept(
-            src[low - 1 : high + 1], bb_ref[low:high], cc_ref[off + low : off + high], m_ref
+            src[low - 1 : high + 1], bb_ref[low:high], cc_ref[HALO + low : HALO + high], m_ref
         )
-    keep(1)
-
-
-def finish_kernel(a_ref, f_ref, r_ref):
-    outs = [f_ref.at[0], f_ref.at[1], r_ref]
-    for which in range(3):
+    keep(o_ref, 1, a_ref, STRIP, CHUNK - STRIP)
+    for n in range(NZD):
+        half = low_ref if n < NZD // 2 else high_ref
+        part = jnp.where(odd == 1, NZD - 1 - n, n)
+        for y in range(PIECE):
+            row = 2 * CHUNK + part * PIECE + y
+            o_ref[pl.ds(row, NSP, stride=3 * CHUNK), :] = jnp.where(first, 0.0, half[n % (NZD // 2), y])
+
+
+def outer_kernel(s_ref, edge_ref, ra_ref, rb_ref, inv_ref, cc_ref, sinv_ref, o_ref):
+    odd = position()[2]
+    bottom, top = at_ends()
+    before = jnp.where(bottom, 0.0, jnp.where(odd == 0, rb_ref[...], ra_ref[...]))
+    behind = jnp.where(top, 0.0, jnp.where(odd == 0, ra_ref[...], rb_ref[...]))
+    v = jnp.concatenate([before, edge_ref[0], edge_ref[1], behind], 0)
+
+    def both(ref):
+        start, end = HALO - STRIP, HALO + CHUNK + STRIP
+        return jnp.concatenate([ref[start : start + 3 * STRIP], ref[end - 3 * STRIP : end]], 0)
+
+    bb, cc = v * both(inv_ref) + both(sinv_ref), both(cc_ref)
+    size = v.shape[0]
+    for sweep in range(SWEEPS):
+        low = sweep + 1
+        v = swept(v, bb[low : size - low], cc[low : size - low])
+    for y in range(STRIP):
+        o_ref[pl.ds(CHUNK + y, NSP, stride=3 * CHUNK), :] = v[y]
+        row = 2 * CHUNK - STRIP + y
+        o_ref[pl.ds(row, NSP, stride=3 * CHUNK), :] = v[v.shape[0] - STRIP + y]
+
+
+def finish_kernel(a_ref, f_ref, r_ref, v_ref, sems):
+    copies = []
+    for which, to in enumerate((f_ref.at[0], f_ref.at[1], r_ref)):
         for m in range(8):
             low = a_ref[SNAKE[2 * m], which * CHUNK : (which + 1) * CHUNK]
             high = a_ref[SNAKE[2 * m + 1], which * CHUNK : (which + 1) * CHUNK]
-            outs[which][:, m * 128 : (m + 1) * 128] = jnp.concatenate([low, high], 0).T
+            v_ref[which, :, m * LANES : (m + 1) * LANES] = jnp.concatenate([low, high], 0).T
+        copies.append(pltpu.make_async_copy(v_ref.at[which], to, sems.at[which]))
+        copies[-1].start()
+    for copy in copies:
+        copy.wait()
 
 
 def strips_kernel(e_ref, cp_ref, c_ref, a_ref, b_ref, head_ref, tail_ref, sems):
@@ -430,7 +470,7 @@
         return lax.ppermute(v, "core", [(0, 1), (1, 0)])
 
     sent = call(
-        prep_kernel, [(NSP, 2 * WIDE, LANES)], [anywhere] * 3, [(LANES, 1024)] * 2, sems=16, limit=MOST
+        prep_kernel, [(NSP, 2 * WIDE, LANES)], [anywhere] * 3, [(LANES, 1024)] * 2 + [(NSP, 2 * WIDE, LANES)], sems=((16,), (2, NSP)), limit=MOST, to=anywhere
     )(c_guess.reshape(LANES, -1), source.reshape(LANES, -1), rate.reshape(LANES, -1))[0]
     got = lax.all_to_all(sent, "space", 0, 0).reshape(-1, LANES)
     own = call(unpack_kernel, [(WIDE,) + plane], [VMEM])(got)[0]
@@ -483,21 +523,31 @@
 
     chunk = lax.all_to_all(errors, "z", 0, 0)
     edge = (STRIP,) + plane
-    ma, mb = call(strips_kernel, [edge] * 2, [VMEM] * 2 + [anywhere], [edge] * 2, sems=2)(
+    ma, mb = call(strips_kernel, [edge] * 2, [VMEM] * 2 + [anywhere], [edge] * 2, sems=((2,),))(
         chunk, cpoint, c
     )
     ra = lax.ppermute(ma, "space", chunk_pairs(0))
     rb = lax.ppermute(mb, "space", chunk_pairs(1))
-    sent = call(
-        last_kernel,
-        [(NSP * 3 * CHUNK, LANES)],
-        [VMEM] * 4 + [anywhere] + [VMEM] * 5,
-        [(CHUNK + 2 * STRIP,) + plane] * 3,
+    sent, edges_in = call(
+        inner_kernel,
+        [(NSP * 3 * CHUNK, LANES), (2, 2 * STRIP) + plane],
+        [VMEM] * 4 + [anywhere] + [VMEM] * 3,
+        [whole] * 3,
         mixer=True,
-        sems=1,
-    )(chunk, cpoint, low, high, c, ra, rb, inv, cc, sinv)[0]
+        sems=((1,),),
+    )(chunk, cpoint, low, high, c, inv, cc, sinv)
+    sent = call(outer_kernel, [(NSP * 3 * CHUNK, LANES)], [VMEM] * 7, aliases={0: 0})(
+        sent, edges_in, ra, rb, inv, cc, sinv
+    )[0]
     got = lax.all_to_all(sent.reshape(NSP, 3 * CHUNK, LANES), "space", 0, 0)
-    fine, residual = call(finish_kernel, [(2, LANES, 1024), (LANES, 1024)], [VMEM])(got)
+    fine, residual = call(
+        finish_kernel,
+        [(2, LANES, 1024), (LANES, 1024)],
+        [VMEM],
+        [(3, LANES, 1024)],
+        sems=((3,),),
+        to=anywhere,
+    )(got)
     return fine.reshape(1, 2, 4, 32, 1024), residual.reshape(1, 4, 32, 1024)
 
 

time: 186 us -> 184 us (0.989)
  waiting for transfers between devices: 36 us -> 33.6 us
    ppermute x1, waiting for transfers between devices: 1.92 us -> 0.01 us  [body(): ra = lax.ppermute(ma, 'space', chunk_pairs(0))]
    pallas_call x3 -> x4, Pallas kernels: 4.87 us -> 5.14 us  [the longest x1 2.91 us: body(): call(inner_kernel, [(NSP * 3 * CHUNK, LANES), (2, 2 * STRIP) + plane], [V...]
  transfers between devices with their start and end apart: 22 -> 22, of which waited for: 18 -> 17; matrix products, arithmetic and copies ran while one was open for 0% -> 0% of each run, Pallas kernels for 7% -> 8%
where the time goes in v4:
time: 184 us; the launch traced here: 183 us
  blocking collectives  90.9 us (49%)
  waiting for transfers between devices  33.6 us (18%)
  starting transfers between devices  30.5 us (17%)
  Pallas kernels  27.5 us (15%)
    all_to_all x1, blocking collectives, body(): got = lax.all_to_all(sent, 'space', 0, 0).reshape(-1, LANES)  28.4 us
    all_to_all x1, blocking collectives, body(): mine = lax.all_to_all(r, 'z', 0, 0)  21.7 us
    all_to_all x1, blocking collectives, body(): got = lax.all_to_all(sent.reshape(NSP, 3 * CHUNK, LANES), 'space', 0, 0)  20.4 us
    all_to_all x1, blocking collectives, body(): chunk = lax.all_to_all(errors, 'z', 0, 0)  20.3 us
    ppermute x7, waiting for transfers between devices, body(): ra = lax.ppermute(ma, everyone, pairs_a)  16.7 us
    ppermute x7, starting transfers between devices, body(): ra = lax.ppermute(ma, everyone, pairs_a)  11.2 us
    ppermute x7, waiting for transfers between devices, body(): rb = lax.ppermute(mb, everyone, pairs_b)  8.8 us
    pallas_call x6, Pallas kernels, body(): call(functools.partial(chain_kernel, t), [piece, piece, message, message]...  8.76 us
  transfers between devices with their start and end apart: 22, of which 17 were waited for; matrix products, arithmetic and copies ran while one was open for 0% of the time, Pallas kernels for 8%

profile of v4, /device:TPU:8, one launch (start us, length us, event | category | flops | bytes accessed | tf_op | source)
XLA Modules:
  0.0 183.4 jit_solution(1759234089434445836)
XLA Ops:
  0.6 3.6 %shard_map.50 = f32[16,192,128]{2,1,0:T(8,128)} custom-call(f32[128,1024]{1,0:T(8,128)} %bitcast.12, f32[128,1024]{1,0:T(8,128)} %bitcast.13, f32[128,1024]{1,0:T(8,128)} %bitcast.14), custom_call_target="tpu_custom_call" | custom-call | tf_op jit(solution)/shard_map/pallas_call | solution.py:472
  4.2 28.4 %all_to_all.20 = f32[16,192,128]{2,1,0:T(8,128)S(1)} all-to-all(f32[16,192,128]{2,1,0:T(8,128)} %shard_map.50), channel_id=1, replica_groups=mesh['z'=8,'core'=2,'space'=16] {'space'}, dimensions={0} | all-to-all | bytes 3145728 | tf_op jit(solution)/shard_map/all_to_all | solution.py:475
  33.2 2.3 %collective-permute-done.oth_ref = f32[96,16,128]{2,1,0:T(8,128)S(1)} collective-permute-done((f32[96,16,128]{2,1,0:T(8,128)S(1)}, f32[96,16,128]{2,1,0:T(8,128)S(1)}, u32[]{:S(2)}, u32[]{:S(2)}) %collective-permute-start) | collective-permute-done | bytes 786464 | tf_op jit(solution)/shard_map/ppermute | solution.py:470
  35.5 4.5 %shard_map.52 = (f32[96,16,128]{2,1,0:T(8,128)S(1)}, f32[64,16,128]{2,1,0:T(8,128)S(1)}, f32[24,16,128]{2,1,0:T(8,128)S(1)}, f32[24,16,128]{2,1,0:T(8,128)S(1)},...) custom-call(f32[3072,128]{1,0:T(8,128)S(1)} %bitcast.10, ...), custom_call_target="tpu_custom_call" | custom-call | tf_op jit(solution)/shard_map/pallas_call | solution.py:480
  40.0 5.6 %collective-permute-start.1 = (f32[64,16,128]{2,1,0:T(8,128)S(1)}, f32[64,16,128]{2,1,0:T(8,128)S(1)}, u32[]{:S(2)}, u32[]{:S(2)}) collective-permute-start(f32[64,16,128]{2,1,0:T(8,128)S(1)} %get-tuple-element.78), channel_id=1, source_target_pairs={{0,240},{1,241},{2,242},{3,243},{4,244},{5,245},{6,246},{7,247},{8... | collective-permute-start | bytes 1572872 | tf_op jit(solution)/shard_map/ppermute | solution.py:487
  45.7 3.3 %shard_map.53.w_ref = f32[64,16,128]{2,1,0:T(8,128)S(1)} custom-call(f32[96,16,128]{2,1,0:T(8,128)S(1)} %get-tuple-element.61.u_ref, f32[96,16,128]{2,1,0:T(8,128)S(1)} %get-tuple-element.62.inv_ref, f32[96,16,128]{2,1,0:T(8,128)S(1)} %get-tuple-element.63.cc_ref, f32[96,16,128]{2,1,0:T(8,128)S(1)} %get-tuple-element.64.sinv_ref), custom_call_target="tpu_custom_call" | custom-call | tf_op jit(solution)/shard_map/pallas_call | solution.py:488
  49.0 3.4 %collective-permute-done.1.next_ref = f32[64,16,128]{2,1,0:T(8,128)S(1)} collective-permute-done((f32[64,16,128]{2,1,0:T(8,128)S(1)}, f32[64,16,128]{2,1,0:T(8,128)S(1)}, u32[]{:S(2)}, u32[]{:S(2)}) %collective-permute-start.1) | collective-permute-done | bytes 524320 | tf_op jit(solution)/shard_map/ppermute | solution.py:487
  52.4 21.7 %all_to_all.21.own_ref = f32[8,8,16,128]{3,2,1,0:T(8,128)S(1)} all-to-all(f32[8,8,16,128]{3,2,1,0:T(8,128)S(1)} %get-tuple-element.66), channel_id=1, replica_groups=mesh['z'=8,'core'=2,'space'=16] {'z'}, dimensions={0} | all-to-all | bytes 1048576 | tf_op jit(solution)/shard_map/all_to_all | solution.py:492
  74.3 1.8 collective-permute-done.2.oth_ref
  76.4 1.1 collective-permute-start.4
  77.6 3.5 %collective-permute-done.3.ra_ref = f32[12,16,128]{2,1,0:T(8,128)S(1)} collective-permute-done((f32[12,16,128]{2,1,0:T(8,128)S(1)}, f32[12,16,128]{2,1,0:T(8,128)S(1)}, u32[]{:S(2)}, u32[]{:S(2)}) %collective-permute-start.3) | collective-permute-done | bytes 98336 | tf_op jit(solution)/shard_map/ppermute | solution.py:503
  81.4 1.5 shard_map.56
  82.9 1.6 collective-permute-start.5
  84.5 1.0 collective-permute-start.6
  85.5 2.5 %collective-permute-done.5.ra_ref = f32[12,16,128]{2,1,0:T(8,128)S(1)} collective-permute-done((f32[12,16,128]{2,1,0:T(8,128)S(1)}, f32[12,16,128]{2,1,0:T(8,128)S(1)}, u32[]{:S(2)}, u32[]{:S(2)}) %collective-permute-start.5) | collective-permute-done | bytes 98336 | tf_op jit(solution)/shard_map/ppermute | solution.py:503
  88.0 1.4 collective-permute-done.6.rb_ref
  89.4 1.5 shard_map.57
  90.9 1.1 collective-permute-start.9
  92.0 1.5 collective-permute-start.8
  93.5 2.2 %collective-permute-done.9.rb_ref = f32[12,16,128]{2,1,0:T(8,128)S(1)} collective-permute-done((f32[12,16,128]{2,1,0:T(8,128)S(1)}, f32[12,16,128]{2,1,0:T(8,128)S(1)}, u32[]{:S(2)}, u32[]{:S(2)}) %collective-permute-start.9) | collective-permute-done | bytes 98336 | tf_op jit(solution)/shard_map/ppermute | solution.py:504
  95.7 1.4 collective-permute-done.8.ra_ref
  97.1 1.6 collective-permute-start.12
  98.7 1.5 shard_map.58
  100.2 1.1 collective-permute-start.11
  101.3 5.5 %collective-permute-done.10.ra_ref = f32[12,16,128]{2,1,0:T(8,128)S(1)} collective-permute-done((f32[12,16,128]{2,1,0:T(8,128)S(1)}, f32[12,16,128]{2,1,0:T(8,128)S(1)}, u32[]{:S(2)}, u32[]{:S(2)}) %collective-permute-start.10) | collective-permute-done | bytes 98336 | tf_op jit(solution)/shard_map/ppermute | solution.py:503
  106.9 1.5 shard_map.59
  108.3 1.1 collective-permute-start.14
  109.5 2.0 %collective-permute-start.13 = (f32[12,16,128]{2,1,0:T(8,128)S(1)}, f32[12,16,128]{2,1,0:T(8,128)S(1)}, u32[]{:S(2)}, u32[]{:S(2)}) collective-permute-start(f32[12,16,128]{2,1,0:T(8,128)S(1)} %get-tuple-element.90), channel_id=1, source_target_pairs={{0,32},{32,0},{64,96},{96,64},{128,160},{160,128},{192,224},{224,1... | collective-permute-start | bytes 294920 | tf_op jit(solution)/shard_map/ppermute | solution.py:503
  111.5 1.5 collective-permute-done.14.rb_ref
  113.0 1.0 collective-permute-done.13.ra_ref
  114.1 2.0 %collective-permute-start.17 = (f32[4,8,16,128]{3,2,1,0:T(8,128)S(1)}, f32[4,8,16,128]{3,2,1,0:T(8,128)S(1)}, u32[]{:S(2)}, u32[]{:S(2)}) collective-permute-start(f32[4,8,16,128]{3,2,1,0:T(8,128)S(1)} %get-tuple-element.100), channel_id=1, source_target_pairs={{0,32},{1,33},{2,34},{3,35},{4,36},{5,37},{6,38},{7,39},{8,40},{9,... | collective-permute-start | bytes 786440 | tf_op jit(solution)/shard_map/ppermute | solution.py:508
  116.1 1.5 shard_map.60
  117.6 3.5 %collective-permute-start.15 = (f32[12,16,128]{2,1,0:T(8,128)S(1)}, f32[12,16,128]{2,1,0:T(8,128)S(1)}, u32[]{:S(2)}, u32[]{:S(2)}) collective-permute-start(f32[12,16,128]{2,1,0:T(8,128)S(1)} %get-tuple-element.96), channel_id=1, source_target_pairs={{0,32},{32,0},{64,96},{96,64},{128,160},{160,128},{192,224},{224,1... | collective-permute-start | bytes 294920 | tf_op jit(solution)/shard_map/ppermute | solution.py:503
  121.1 1.0 collective-permute-start.16
  122.1 1.6 collective-permute-done.15.ra_ref
  123.7 2.0 %collective-permute-done.16.rb_ref = f32[12,16,128]{2,1,0:T(8,128)S(1)} collective-permute-done((f32[12,16,128]{2,1,0:T(8,128)S(1)}, f32[12,16,128]{2,1,0:T(8,128)S(1)}, u32[]{:S(2)}, u32[]{:S(2)}) %collective-permute-start.16) | collective-permute-done | bytes 98336 | tf_op jit(solution)/shard_map/ppermute | solution.py:504
  125.7 1.5 shard_map.61
  127.1 1.1 collective-permute-start.19
  128.3 2.2 %collective-permute-start.18 = (f32[12,16,128]{2,1,0:T(8,128)S(1)}, f32[12,16,128]{2,1,0:T(8,128)S(1)}, u32[]{:S(2)}, u32[]{:S(2)}) collective-permute-start(f32[12,16,128]{2,1,0:T(8,128)S(1)} %get-tuple-element.101), channel_id=1, source_target_pairs={{0,32},{32,0},{64,96},{96,64},{128,160},{160,128},{192,224},{224,1... | collective-permute-start | bytes 294920 | tf_op jit(solution)/shard_map/ppermute | solution.py:503
  130.5 1.4 collective-permute-done.19.rb_ref
  131.9 1.2 collective-permute-done.18.ra_ref
  133.1 1.5 shard_map.62
  134.6 20.3 %all_to_all.22.e_ref = f32[8,8,16,128]{3,2,1,0:T(8,128)S(1)} all-to-all(f32[8,8,16,128]{3,2,1,0:T(8,128)S(1)} %shard_map.62), channel_id=1, replica_groups=mesh['z'=8,'core'=2,'space'=16] {'z'}, dimensions={0} | all-to-all | bytes 1048576 | tf_op jit(solution)/shard_map/all_to_all | solution.py:524
  155.0 1.7 collective-permute-start.20
  157.1 2.9 %shard_map.63 = (f32[3072,128]{1,0:T(8,128)S(1)}, f32[2,8,16,128]{3,2,1,0:T(8,128)S(1)}) custom-call(f32[8,8,16,128]{3,2,1,0:T(8,128)S(1)} %all_to_all.22.e_ref, f32[64,16,128]{2,1,0:T(8,128)S(1)} %collective-permute-done.7.cp_ref, f32[4,8,16,128]{3,2,1,0:T(8,128)S(1)} %collective-permute-done.12.low_ref, ...), custom_call_target="tpu_custom_call" | custom-call | tf_op jit(solution)/shard_map/pallas_call | solution.py:531
  160.6 0.7 shard_map.65
  161.4 20.4 %all_to_all.23.a_ref = f32[16,192,128]{2,1,0:T(8,128)S(1)} all-to-all(f32[16,192,128]{2,1,0:T(8,128)S(1)} %bitcast.11), channel_id=1, replica_groups=mesh['z'=8,'core'=2,'space'=16] {'space'}, dimensions={0} | all-to-all | bytes 3145728 | tf_op jit(solution)/shard_map/all_to_all | solution.py:542
  181.8 1.4 shard_map.66
  (18 shorter events, 2.6 us)
Async XLA Ops:
  33.1 2.4 %collective-permute-start = (f32[96,16,128]{2,1,0:T(8,128)S(1)}, f32[96,16,128]{2,1,0:T(8,128)S(1)}, u32[]{:S(2)}, u32[]{:S(2)}) collective-permute-start(f32[96,16,128]{2,1,0:T(8,128)S(1)} %shard_map.51.own_ref), channel_id=1, source_target_pairs={{0,16},{16,0},{1,17},{17,1},{2,18},{18,2},{3,19},{19,3},{4,20},{20... | collective-permute-start | bytes 2359304 | tf_op jit(solution)/shard_map/ppermute | solution.py:470
  40.0 12.3 %collective-permute-start.1 = (f32[64,16,128]{2,1,0:T(8,128)S(1)}, f32[64,16,128]{2,1,0:T(8,128)S(1)}, u32[]{:S(2)}, u32[]{:S(2)}) collective-permute-start(f32[64,16,128]{2,1,0:T(8,128)S(1)} %get-tuple-element.78), channel_id=1, source_target_pairs={{0,240},{1,241},{2,242},{3,243},{4,244},{5,245},{6,246},{7,247},{8... | collective-permute-start | bytes 1572872 | tf_op jit(solution)/shard_map/ppermute | solution.py:487
  74.2 1.9 %collective-permute-start.2 = (f32[8,8,16,128]{3,2,1,0:T(8,128)S(1)}, f32[8,8,16,128]{3,2,1,0:T(8,128)S(1)}, u32[]{:S(2)}, u32[]{:S(2)}) collective-permute-start(f32[8,8,16,128]{3,2,1,0:T(8,128)S(1)} %all_to_all.21.own_ref), channel_id=1, source_target_pairs={{0,16},{16,0},{1,17},{17,1},{2,18},{18,2},{3,19},{19,3},{4,20},{20... | collective-permute-start | bytes 1572872 | tf_op jit(solution)/shard_map/ppermute | solution.py:470
  76.2 4.9 %collective-permute-start.3 = (f32[12,16,128]{2,1,0:T(8,128)S(1)}, f32[12,16,128]{2,1,0:T(8,128)S(1)}, u32[]{:S(2)}, u32[]{:S(2)}) collective-permute-start(f32[12,16,128]{2,1,0:T(8,128)S(1)} %get-tuple-element.67), channel_id=1, source_target_pairs={{0,32},{32,0},{64,96},{96,64},{128,160},{160,128},{192,224},{224,1... | collective-permute-start | bytes 294920 | tf_op jit(solution)/shard_map/ppermute | solution.py:503
  76.4 4.9 %collective-permute-start.4 = (f32[12,16,128]{2,1,0:T(8,128)S(1)}, f32[12,16,128]{2,1,0:T(8,128)S(1)}, u32[]{:S(2)}, u32[]{:S(2)}) collective-permute-start(f32[12,16,128]{2,1,0:T(8,128)S(1)} %get-tuple-element.68), channel_id=1, source_target_pairs={{32,64},{64,32},{96,128},{128,96},{160,192},{192,160},{224,225},{2... | collective-permute-start | bytes 294920 | tf_op jit(solution)/shard_map/ppermute | solution.py:504
  81.4 10.6 %collective-permute-start.7 = (f32[64,16,128]{2,1,0:T(8,128)S(1)}, f32[64,16,128]{2,1,0:T(8,128)S(1)}, u32[]{:S(2)}, u32[]{:S(2)}) collective-permute-start(f32[64,16,128]{2,1,0:T(8,128)S(1)} %get-tuple-element.78), channel_id=1, source_target_pairs={{0,16},{1,17},{2,18},{3,19},{4,20},{5,21},{6,22},{7,23},{8,24},{9,... | collective-permute-start | bytes 1572872 | tf_op jit(solution)/shard_map/ppermute | solution.py:508
  82.9 5.1 %collective-permute-start.5 = (f32[12,16,128]{2,1,0:T(8,128)S(1)}, f32[12,16,128]{2,1,0:T(8,128)S(1)}, u32[]{:S(2)}, u32[]{:S(2)}) collective-permute-start(f32[12,16,128]{2,1,0:T(8,128)S(1)} %get-tuple-element.74), channel_id=1, source_target_pairs={{0,32},{32,0},{64,96},{96,64},{128,160},{160,128},{192,224},{224,1... | collective-permute-start | bytes 294920 | tf_op jit(solution)/shard_map/ppermute | solution.py:503
  84.5 4.9 %collective-permute-start.6 = (f32[12,16,128]{2,1,0:T(8,128)S(1)}, f32[12,16,128]{2,1,0:T(8,128)S(1)}, u32[]{:S(2)}, u32[]{:S(2)}) collective-permute-start(f32[12,16,128]{2,1,0:T(8,128)S(1)} %get-tuple-element.75), channel_id=1, source_target_pairs={{32,64},{64,32},{96,128},{128,96},{160,192},{192,160},{224,225},{2... | collective-permute-start | bytes 294920 | tf_op jit(solution)/shard_map/ppermute | solution.py:504
  90.9 4.9 %collective-permute-start.9 = (f32[12,16,128]{2,1,0:T(8,128)S(1)}, f32[12,16,128]{2,1,0:T(8,128)S(1)}, u32[]{:S(2)}, u32[]{:S(2)}) collective-permute-start(f32[12,16,128]{2,1,0:T(8,128)S(1)} %get-tuple-element.80), channel_id=1, source_target_pairs={{32,64},{64,32},{96,128},{128,96},{160,192},{192,160},{224,225},{2... | collective-permute-start | bytes 294920 | tf_op jit(solution)/shard_map/ppermute | solution.py:504
  92.0 5.1 %collective-permute-start.8 = (f32[12,16,128]{2,1,0:T(8,128)S(1)}, f32[12,16,128]{2,1,0:T(8,128)S(1)}, u32[]{:S(2)}, u32[]{:S(2)}) collective-permute-start(f32[12,16,128]{2,1,0:T(8,128)S(1)} %get-tuple-element.79), channel_id=1, source_target_pairs={{0,32},{32,0},{64,96},{96,64},{128,160},{160,128},{192,224},{224,1... | collective-permute-start | bytes 294920 | tf_op jit(solution)/shard_map/ppermute | solution.py:503
  97.1 12.4 %collective-permute-start.12 = (f32[4,8,16,128]{3,2,1,0:T(8,128)S(1)}, f32[4,8,16,128]{3,2,1,0:T(8,128)S(1)}, u32[]{:S(2)}, u32[]{:S(2)}) collective-permute-start(f32[4,8,16,128]{3,2,1,0:T(8,128)S(1)} %get-tuple-element.89), channel_id=1, source_target_pairs={{0,32},{1,33},{2,34},{3,35},{4,36},{5,37},{6,38},{7,39},{8,40},{9,... | collective-permute-start | bytes 786440 | tf_op jit(solution)/shard_map/ppermute | solution.py:508
  100.1 6.7 %collective-permute-start.10 = (f32[12,16,128]{2,1,0:T(8,128)S(1)}, f32[12,16,128]{2,1,0:T(8,128)S(1)}, u32[]{:S(2)}, u32[]{:S(2)}) collective-permute-start(f32[12,16,128]{2,1,0:T(8,128)S(1)} %get-tuple-element.85), channel_id=1, source_target_pairs={{0,32},{32,0},{64,96},{96,64},{128,160},{160,128},{192,224},{224,1... | collective-permute-start | bytes 294920 | tf_op jit(solution)/shard_map/ppermute | solution.py:503
  100.2 6.6 %collective-permute-start.11 = (f32[12,16,128]{2,1,0:T(8,128)S(1)}, f32[12,16,128]{2,1,0:T(8,128)S(1)}, u32[]{:S(2)}, u32[]{:S(2)}) collective-permute-start(f32[12,16,128]{2,1,0:T(8,128)S(1)} %get-tuple-element.86), channel_id=1, source_target_pairs={{32,64},{64,32},{96,128},{128,96},{160,192},{192,160},{224,225},{2... | collective-permute-start | bytes 294920 | tf_op jit(solution)/shard_map/ppermute | solution.py:504
  108.3 4.7 %collective-permute-start.14 = (f32[12,16,128]{2,1,0:T(8,128)S(1)}, f32[12,16,128]{2,1,0:T(8,128)S(1)}, u32[]{:S(2)}, u32[]{:S(2)}) collective-permute-start(f32[12,16,128]{2,1,0:T(8,128)S(1)} %get-tuple-element.91), channel_id=1, source_target_pairs={{32,64},{64,32},{96,128},{128,96},{160,192},{192,160},{224,225},{2... | collective-permute-start | bytes 294920 | tf_op jit(solution)/shard_map/ppermute | solution.py:504
  109.5 4.6 %collective-permute-start.13 = (f32[12,16,128]{2,1,0:T(8,128)S(1)}, f32[12,16,128]{2,1,0:T(8,128)S(1)}, u32[]{:S(2)}, u32[]{:S(2)}) collective-permute-start(f32[12,16,128]{2,1,0:T(8,128)S(1)} %get-tuple-element.90), channel_id=1, source_target_pairs={{0,32},{32,0},{64,96},{96,64},{128,160},{160,128},{192,224},{224,1... | collective-permute-start | bytes 294920 | tf_op jit(solution)/shard_map/ppermute | solution.py:503
  114.1 14.2 %collective-permute-start.17 = (f32[4,8,16,128]{3,2,1,0:T(8,128)S(1)}, f32[4,8,16,128]{3,2,1,0:T(8,128)S(1)}, u32[]{:S(2)}, u32[]{:S(2)}) collective-permute-start(f32[4,8,16,128]{3,2,1,0:T(8,128)S(1)} %get-tuple-element.100), channel_id=1, source_target_pairs={{0,32},{1,33},{2,34},{3,35},{4,36},{5,37},{6,38},{7,39},{8,40},{9,... | collective-permute-start | bytes 786440 | tf_op jit(solution)/shard_map/ppermute | solution.py:508
  117.6 6.1 %collective-permute-start.15 = (f32[12,16,128]{2,1,0:T(8,128)S(1)}, f32[12,16,128]{2,1,0:T(8,128)S(1)}, u32[]{:S(2)}, u32[]{:S(2)}) collective-permute-start(f32[12,16,128]{2,1,0:T(8,128)S(1)} %get-tuple-element.96), channel_id=1, source_target_pairs={{0,32},{32,0},{64,96},{96,64},{128,160},{160,128},{192,224},{224,1... | collective-permute-start | bytes 294920 | tf_op jit(solution)/shard_map/ppermute | solution.py:503
  121.1 4.6 %collective-permute-start.16 = (f32[12,16,128]{2,1,0:T(8,128)S(1)}, f32[12,16,128]{2,1,0:T(8,128)S(1)}, u32[]{:S(2)}, u32[]{:S(2)}) collective-permute-start(f32[12,16,128]{2,1,0:T(8,128)S(1)} %get-tuple-element.97), channel_id=1, source_target_pairs={{32,64},{64,32},{96,128},{128,96},{160,192},{192,160},{224,225},{2... | collective-permute-start | bytes 294920 | tf_op jit(solution)/shard_map/ppermute | solution.py:504
  127.1 4.7 %collective-permute-start.19 = (f32[12,16,128]{2,1,0:T(8,128)S(1)}, f32[12,16,128]{2,1,0:T(8,128)S(1)}, u32[]{:S(2)}, u32[]{:S(2)}) collective-permute-start(f32[12,16,128]{2,1,0:T(8,128)S(1)} %get-tuple-element.102), channel_id=1, source_target_pairs={{32,64},{64,32},{96,128},{128,96},{160,192},{192,160},{224,225},{2... | collective-permute-start | bytes 294920 | tf_op jit(solution)/shard_map/ppermute | solution.py:504
  128.3 4.8 %collective-permute-start.18 = (f32[12,16,128]{2,1,0:T(8,128)S(1)}, f32[12,16,128]{2,1,0:T(8,128)S(1)}, u32[]{:S(2)}, u32[]{:S(2)}) collective-permute-start(f32[12,16,128]{2,1,0:T(8,128)S(1)} %get-tuple-element.101), channel_id=1, source_target_pairs={{0,32},{32,0},{64,96},{96,64},{128,160},{160,128},{192,224},{224,1... | collective-permute-start | bytes 294920 | tf_op jit(solution)/shard_map/ppermute | solution.py:503
  155.0 5.0 %collective-permute-start.20 = (f32[4,16,128]{2,1,0:T(8,128)S(1)}, f32[4,16,128]{2,1,0:T(8,128)S(1)}, u32[]{:S(2)}, u32[]{:S(2)}) collective-permute-start(f32[4,16,128]{2,1,0:T(8,128)S(1)} %get-tuple-element.116), channel_id=1, source_target_pairs={{0,1},{1,0},{2,3},{3,2},{7,6},{6,7},{5,4},{4,5},{8,9},{9,8},{10,11... | collective-permute-start | bytes 98312 | tf_op jit(solution)/shard_map/ppermute | solution.py:529
  156.7 3.9 %collective-permute-start.21 = (f32[4,16,128]{2,1,0:T(8,128)S(1)}, f32[4,16,128]{2,1,0:T(8,128)S(1)}, u32[]{:S(2)}, u32[]{:S(2)}) collective-permute-start(f32[4,16,128]{2,1,0:T(8,128)S(1)} %get-tuple-element.117), channel_id=1, source_target_pairs={{1,2},{2,1},{3,7},{7,3},{6,5},{5,6},{4,8},{8,4},{9,10},{10,9},{11,... | collective-permute-start | bytes 98312 | tf_op jit(solution)/shard_map/ppermute | solution.py:530

commit v5 on v4

--- a/solution.py
+++ b/solution.py
@@ -222,12 +222,21 @@
         work(r_ref)
 
 
-def unpack_kernel(a_ref, q_ref):
+def unpack(base, g_ref, to_ref):
     def one(y, _):
-        q_ref[y] = a_ref[pl.ds(WIDE + y, NSP, stride=2 * WIDE), :]
+        to_ref[y] = g_ref[pl.ds(base + y, NSP, stride=2 * WIDE), :]
         return 0
 
     lax.fori_loop(0, WIDE, one, 0, unroll=8)
+
+
+def field_kernel(g_ref, q_ref):
+    unpack(WIDE, g_ref, q_ref)
+
+
+def state_kernel(g_ref, a_ref, c_ref):
+    unpack(0, g_ref, a_ref)
+    c_ref[...] = a_ref[HALO : HALO + CHUNK]
 
 
 def double_step(number, a_ref, b_ref, bb_ref, inv_ref, cc_ref, sinv_ref, m_ref):
@@ -245,19 +254,12 @@
 
 
 def first_kernel(
-    g_ref, own_ref, oth_ref, a_ref, u_ref, inv2_ref, cc2_ref, inv_ref, cc_ref, sinv_ref, c_ref,
+    _, own_ref, oth_ref, a_ref, u_ref, inv2_ref, cc2_ref, inv_ref, cc_ref, sinv_ref,
     b_ref, bb_ref, rate_ref, m_ref,
 ):
     _, core, _, sub = position()
     step = 8
     fill_mixer(m_ref)
-
-    def gather(y, _):
-        a_ref[y] = g_ref[pl.ds(y, NSP, stride=2 * WIDE), :]
-        return 0
-
-    lax.fori_loop(0, WIDE, gather, 0, unroll=8)
-    c_ref[...] = a_ref[HALO : HALO + CHUNK]
 
     def init(n, _):
         at = pl.ds(pl.multiple_of(n * step, step), step)
@@ -287,7 +289,7 @@
     w_ref[...] = a_ref[HALO : HALO + CHUNK]
 
 
-def difference_kernel(w_ref, next_ref, r_ref, low_ref, high_ref):
+def difference_kernel(w_ref, next_ref, r_ref, *part_refs):
     z, core, odd, _ = position()
     last = (z == NZD - 1) & (core == 1)
     for n in range(NZD):
@@ -295,8 +297,7 @@
         after = next_ref[pl.ds(PIECE * part, PIECE)]
         r = jnp.where(last, after, w_ref[pl.ds(PIECE * part, PIECE)]) - after
         r_ref[n] = r
-        half = low_ref if n < NZD // 2 else high_ref
-        half[n % (NZD // 2)] = r
+        part_refs[n // 2][n % 2] = r
 
 
 def messages(odd, e, r_next, a_ref, b_ref):
@@ -365,7 +366,7 @@
 
 
 def inner_kernel(
-    e_ref, cp_ref, low_ref, high_ref, c_ref, inv_ref, cc_ref, sinv_ref, o_ref, edge_ref,
+    e_ref, cp_ref, r0_ref, r1_ref, r2_ref, r3_ref, c_ref, inv_ref, cc_ref, sinv_ref, o_ref, edge_ref,
     a_ref, b_ref, bb_ref, m_ref, sems
 ):
     z, core, odd, _ = position()
@@ -395,11 +396,11 @@
         )
     keep(o_ref, 1, a_ref, STRIP, CHUNK - STRIP)
     for n in range(NZD):
-        half = low_ref if n < NZD // 2 else high_ref
+        r_ref = (r0_ref, r1_ref, r2_ref, r3_ref)[n // 2]
         part = jnp.where(odd == 1, NZD - 1 - n, n)
         for y in range(PIECE):
             row = 2 * CHUNK + part * PIECE + y
-            o_ref[pl.ds(row, NSP, stride=3 * CHUNK), :] = jnp.where(first, 0.0, half[n % (NZD // 2), y])
+            o_ref[pl.ds(row, NSP, stride=3 * CHUNK), :] = jnp.where(first, 0.0, r_ref[n % 2, y])
 
 
 def outer_kernel(s_ref, edge_ref, ra_ref, rb_ref, inv_ref, cc_ref, sinv_ref, o_ref):
@@ -473,21 +474,22 @@
         prep_kernel, [(NSP, 2 * WIDE, LANES)], [anywhere] * 3, [(LANES, 1024)] * 2 + [(NSP, 2 * WIDE, LANES)], sems=((16,), (2, NSP)), limit=MOST, to=anywhere
     )(c_guess.reshape(LANES, -1), source.reshape(LANES, -1), rate.reshape(LANES, -1))[0]
     got = lax.all_to_all(sent, "space", 0, 0).reshape(-1, LANES)
-    own = call(unpack_kernel, [(WIDE,) + plane], [VMEM])(got)[0]
+    wide, whole = (WIDE,) + plane, (CHUNK,) + plane
+    own = call(field_kernel, [wide], [VMEM])(got)[0]
     oth = swap(own)
-
-    wide, whole = (WIDE,) + plane, (CHUNK,) + plane
-    ahead, u, inv2, cc2, inv, cc, sinv, c = call(
+    state, c = call(state_kernel, [wide, whole], [VMEM])(got)
+
+    ahead, u, inv2, cc2, inv, cc, sinv = call(
         first_kernel,
-        [wide, whole] + [(3 * PIECE,) + plane] * 2 + [wide] * 3 + [whole],
+        [wide, whole] + [(3 * PIECE,) + plane] * 2 + [wide] * 3,
         [VMEM] * 3,
         [wide] * 3,
         mixer=True,
-    )(got, own, oth)
+        aliases={0: 0},
+    )(state, own, oth)
     after = lax.ppermute(u, everyone, interval_shift(-1))
     w = call(second_kernel, [whole], [VMEM] * 4, [wide] * 3, mixer=True)(ahead, inv, cc, sinv)[0]
-    half = (NZD // 2,) + piece
-    r, r_low, r_high = call(difference_kernel, [(NZD,) + piece, half, half], [VMEM] * 2)(w, after)
+    r, *r_parts = call(difference_kernel, [(NZD,) + piece] + [(2,) + piece] * 4, [VMEM] * 2)(w, after)
 
     mine = lax.all_to_all(r, "z", 0, 0)
     other = swap(mine)
@@ -495,14 +497,14 @@
         residual_kernel, [(NT,) + piece, message, message], [VMEM] * 2
     )(mine, other)
     pairs_a, pairs_b = piece_pairs(0), piece_pairs(1)
-    beside = {0: (u, 1), 2: (r_low, 2), 4: (r_high, 2)}
+    beside = [(u, 1)] + [(part, 2) for part in r_parts]
     moved = []
     errors = [res[1]]
     for turn in range(7):
         t = 2 * turn + 1
         ra = lax.ppermute(ma, everyone, pairs_a)
         rb = lax.ppermute(mb, everyone, pairs_b)
-        if turn in beside:
+        if turn < len(beside):
             part, step = beside[turn]
             ra, rb, part = lax.optimization_barrier((ra, rb, part))
             moved.append(lax.ppermute(part, everyone, interval_shift(step)))
@@ -512,9 +514,9 @@
             functools.partial(chain_kernel, t), [piece, piece, message, message], [VMEM] * 6
         )(ra, rb, errors[-1], res, inv2, cc2)
         errors += [e1, e2]
-        if turn - 1 in beside:
-            ma, moved[-1] = lax.optimization_barrier((ma, moved[-1]))
-    cpoint, low, high = moved
+        if turn > 0 and turn <= len(beside):
+            ma, moved[turn - 1] = lax.optimization_barrier((ma, moved[turn - 1]))
+    cpoint, *r_parts = moved
     errors = call(
         functools.partial(chain_end_kernel, NT - 3),
         [(NZD,) + piece],
@@ -531,11 +533,11 @@
     sent, edges_in = call(
         inner_kernel,
         [(NSP * 3 * CHUNK, LANES), (2, 2 * STRIP) + plane],
-        [VMEM] * 4 + [anywhere] + [VMEM] * 3,
+        [VMEM] * 6 + [anywhere] + [VMEM] * 3,
         [whole] * 3,
         mixer=True,
         sems=((1,),),
-    )(chunk, cpoint, low, high, c, inv, cc, sinv)
+    )(chunk, cpoint, *r_parts, c, inv, cc, sinv)
     sent = call(outer_kernel, [(NSP * 3 * CHUNK, LANES)], [VMEM] * 7, aliases={0: 0})(
         sent, edges_in, ra, rb, inv, cc, sinv
     )[0]

time: 184 us -> 182 us (0.989)
  waiting for transfers between devices: 33.6 us -> 30.6 us
  starting transfers between devices: 30.5 us -> 33.1 us
    ppermute x3 -> x5, starting transfers between devices: 3.6 us -> 7.34 us  [body(): moved.append(lax.ppermute(part, everyone, interval_shift(step)))]
    ppermute x7, waiting for transfers between devices: 8.8 us -> 6.69 us  [body(): rb = lax.ppermute(mb, everyone, pairs_b)]
  transfers between devices with their start and end apart: 22 -> 24, of which waited for: 17 -> 18; matrix products, arithmetic and copies ran while one was open for 0% -> 0% of each run, Pallas kernels for 8% -> 9%
where the time goes in v5:
time: 182 us
  blocking collectives  89.3 us (49%)
  starting transfers between devices  33.1 us (18%)
  waiting for transfers between devices  30.6 us (17%)
  Pallas kernels  27.4 us (15%)
    all_to_all x1, blocking collectives, body(): got = lax.all_to_all(sent, 'space', 0, 0).reshape(-1, LANES)  28.4 us
    all_to_all x1, blocking collectives, body(): mine = lax.all_to_all(r, 'z', 0, 0)  21.7 us
    all_to_all x1, blocking collectives, body(): got = lax.all_to_all(sent.reshape(NSP, 3 * CHUNK, LANES), 'space', 0, 0)  20.1 us
    all_to_all x1, blocking collectives, body(): chunk = lax.all_to_all(errors, 'z', 0, 0)  19.1 us
    ppermute x7, waiting for transfers between devices, body(): ra = lax.ppermute(ma, everyone, pairs_a)  16.3 us
    ppermute x7, starting transfers between devices, body(): ra = lax.ppermute(ma, everyone, pairs_a)  10.5 us
    pallas_call x6, Pallas kernels, body(): call(functools.partial(chain_kernel, t), [piece, piece, message, message]...  8.76 us
    ppermute x7, starting transfers between devices, body(): rb = lax.ppermute(mb, everyone, pairs_b)  7.63 us
  transfers between devices with their start and end apart: 24, of which 18 were waited for; matrix products, arithmetic and copies ran while one was open for 0% of the time, Pallas kernels for 9%

profile of v5, /device:TPU:8, one launch (start us, length us, event | category | flops | bytes accessed | tf_op | source)
XLA Modules:
  0.0 181.5 jit_solution(705129356717306188)
XLA Ops:
  0.6 3.6 %shard_map.50 = f32[16,192,128]{2,1,0:T(8,128)} custom-call(f32[128,1024]{1,0:T(8,128)} %bitcast.12, f32[128,1024]{1,0:T(8,128)} %bitcast.13, f32[128,1024]{1,0:T(8,128)} %bitcast.14), custom_call_target="tpu_custom_call" | custom-call | tf_op jit(solution)/shard_map/pallas_call | solution.py:473
  4.2 28.4 %all_to_all.20 = f32[16,192,128]{2,1,0:T(8,128)S(1)} all-to-all(f32[16,192,128]{2,1,0:T(8,128)} %shard_map.50), channel_id=1, replica_groups=mesh['z'=8,'core'=2,'space'=16] {'space'}, dimensions={0} | all-to-all | bytes 3145728 | tf_op jit(solution)/shard_map/all_to_all | solution.py:476
  33.8 1.7 collective-permute-done.oth_ref
  35.5 4.0 %shard_map.53 = (f32[96,16,128]{2,1,0:T(8,128)S(1)}, f32[64,16,128]{2,1,0:T(8,128)S(1)}, f32[24,16,128]{2,1,0:T(8,128)S(1)}, f32[24,16,128]{2,1,0:T(8,128)S(1)},...) custom-call(f32[96,16,128]{2,1,0:T(8,128)S(1)} %get-tuple-element.74, ...), custom_call_target="tpu_custom_call", output_to_operand_aliasing={{0}: (0, {})} | custom-call | tf_op jit(solution)/shard_map/pallas_call | solution.py:482
  39.5 5.6 %collective-permute-start.1 = (f32[64,16,128]{2,1,0:T(8,128)S(1)}, f32[64,16,128]{2,1,0:T(8,128)S(1)}, u32[]{:S(2)}, u32[]{:S(2)}) collective-permute-start(f32[64,16,128]{2,1,0:T(8,128)S(1)} %get-tuple-element.95), channel_id=1, source_target_pairs={{0,240},{1,241},{2,242},{3,243},{4,244},{5,245},{6,246},{7,247},{8... | collective-permute-start | bytes 1572872 | tf_op jit(solution)/shard_map/ppermute | solution.py:490
  45.1 3.3 %shard_map.54.w_ref = f32[64,16,128]{2,1,0:T(8,128)S(1)} custom-call(f32[96,16,128]{2,1,0:T(8,128)S(1)} %get-tuple-element.75.u_ref, f32[96,16,128]{2,1,0:T(8,128)S(1)} %get-tuple-element.76.inv_ref, f32[96,16,128]{2,1,0:T(8,128)S(1)} %get-tuple-element.77.cc_ref, f32[96,16,128]{2,1,0:T(8,128)S(1)} %get-tuple-element.78.sinv_ref), custom_call_target="tpu_custom_call" | custom-call | tf_op jit(solution)/shard_map/pallas_call | solution.py:491
  48.4 3.4 %collective-permute-done.1.next_ref = f32[64,16,128]{2,1,0:T(8,128)S(1)} collective-permute-done((f32[64,16,128]{2,1,0:T(8,128)S(1)}, f32[64,16,128]{2,1,0:T(8,128)S(1)}, u32[]{:S(2)}, u32[]{:S(2)}) %collective-permute-start.1) | collective-permute-done | bytes 524320 | tf_op jit(solution)/shard_map/ppermute | solution.py:490
  51.9 21.7 %all_to_all.21.own_ref = f32[8,8,16,128]{3,2,1,0:T(8,128)S(1)} all-to-all(f32[8,8,16,128]{3,2,1,0:T(8,128)S(1)} %get-tuple-element.80), channel_id=1, replica_groups=mesh['z'=8,'core'=2,'space'=16] {'z'}, dimensions={0} | all-to-all | bytes 1048576 | tf_op jit(solution)/shard_map/all_to_all | solution.py:494
  73.7 1.8 collective-permute-done.2.oth_ref
  75.9 1.1 collective-permute-start.4
  77.0 3.5 %collective-permute-done.3.ra_ref = f32[12,16,128]{2,1,0:T(8,128)S(1)} collective-permute-done((f32[12,16,128]{2,1,0:T(8,128)S(1)}, f32[12,16,128]{2,1,0:T(8,128)S(1)}, u32[]{:S(2)}, u32[]{:S(2)}) %collective-permute-start.3) | collective-permute-done | bytes 98336 | tf_op jit(solution)/shard_map/ppermute | solution.py:505
  80.8 1.5 shard_map.57
  82.3 1.6 collective-permute-start.5
  83.9 1.0 collective-permute-start.6
  85.0 2.5 %collective-permute-done.5.ra_ref = f32[12,16,128]{2,1,0:T(8,128)S(1)} collective-permute-done((f32[12,16,128]{2,1,0:T(8,128)S(1)}, f32[12,16,128]{2,1,0:T(8,128)S(1)}, u32[]{:S(2)}, u32[]{:S(2)}) %collective-permute-start.5) | collective-permute-done | bytes 98336 | tf_op jit(solution)/shard_map/ppermute | solution.py:505
  87.5 1.4 collective-permute-done.6.rb_ref
  88.8 1.0 collective-permute-start.10
  89.8 1.5 shard_map.58
  91.3 1.1 collective-permute-start.9
  92.4 1.9 %collective-permute-start.8 = (f32[12,16,128]{2,1,0:T(8,128)S(1)}, f32[12,16,128]{2,1,0:T(8,128)S(1)}, u32[]{:S(2)}, u32[]{:S(2)}) collective-permute-start(f32[12,16,128]{2,1,0:T(8,128)S(1)} %get-tuple-element.96), channel_id=1, source_target_pairs={{0,32},{32,0},{64,96},{96,64},{128,160},{160,128},{192,224},{224,1... | collective-permute-start | bytes 294920 | tf_op jit(solution)/shard_map/ppermute | solution.py:505
  94.3 1.7 collective-permute-done.9.rb_ref
  96.0 1.3 collective-permute-done.8.ra_ref
  97.2 2.5 %collective-permute-start.13 = (f32[2,8,16,128]{3,2,1,0:T(8,128)S(1)}, f32[2,8,16,128]{3,2,1,0:T(8,128)S(1)}, u32[]{:S(2)}, u32[]{:S(2)}) collective-permute-start(f32[2,8,16,128]{3,2,1,0:T(8,128)S(1)} %get-tuple-element.111), channel_id=1, source_target_pairs={{0,32},{1,33},{2,34},{3,35},{4,36},{5,37},{6,38},{7,39},{8,40},{9,... | collective-permute-start | bytes 393224 | tf_op jit(solution)/shard_map/ppermute | solution.py:510
  99.7 1.5 shard_map.59
  101.9 1.0 collective-permute-start.12
  102.9 3.0 %collective-permute-done.11.ra_ref = f32[12,16,128]{2,1,0:T(8,128)S(1)} collective-permute-done((f32[12,16,128]{2,1,0:T(8,128)S(1)}, f32[12,16,128]{2,1,0:T(8,128)S(1)}, u32[]{:S(2)}, u32[]{:S(2)}) %collective-permute-start.11) | collective-permute-done | bytes 98336 | tf_op jit(solution)/shard_map/ppermute | solution.py:505
  106.5 1.9 %collective-permute-start.16 = (f32[2,8,16,128]{3,2,1,0:T(8,128)S(1)}, f32[2,8,16,128]{3,2,1,0:T(8,128)S(1)}, u32[]{:S(2)}, u32[]{:S(2)}) collective-permute-start(f32[2,8,16,128]{3,2,1,0:T(8,128)S(1)} %get-tuple-element.119), channel_id=1, source_target_pairs={{0,32},{1,33},{2,34},{3,35},{4,36},{5,37},{6,38},{7,39},{8,40},{9,... | collective-permute-start | bytes 393224 | tf_op jit(solution)/shard_map/ppermute | solution.py:510
  108.4 1.5 shard_map.60
  109.9 1.1 collective-permute-start.15
  111.0 2.0 %collective-permute-start.14 = (f32[12,16,128]{2,1,0:T(8,128)S(1)}, f32[12,16,128]{2,1,0:T(8,128)S(1)}, u32[]{:S(2)}, u32[]{:S(2)}) collective-permute-start(f32[12,16,128]{2,1,0:T(8,128)S(1)} %get-tuple-element.112), channel_id=1, source_target_pairs={{0,32},{32,0},{64,96},{96,64},{128,160},{160,128},{192,224},{224,1... | collective-permute-start | bytes 294920 | tf_op jit(solution)/shard_map/ppermute | solution.py:505
  113.0 1.6 collective-permute-done.15.rb_ref
  114.6 1.0 collective-permute-done.14.ra_ref
  115.6 2.0 %collective-permute-start.19 = (f32[2,8,16,128]{3,2,1,0:T(8,128)S(1)}, f32[2,8,16,128]{3,2,1,0:T(8,128)S(1)}, u32[]{:S(2)}, u32[]{:S(2)}) collective-permute-start(f32[2,8,16,128]{3,2,1,0:T(8,128)S(1)} %get-tuple-element.124), channel_id=1, source_target_pairs={{0,32},{1,33},{2,34},{3,35},{4,36},{5,37},{6,38},{7,39},{8,40},{9,... | collective-permute-start | bytes 393224 | tf_op jit(solution)/shard_map/ppermute | solution.py:510
  117.6 1.5 shard_map.61
  119.1 0.9 collective-permute-start.17
  119.9 1.0 collective-permute-start.18
  121.0 2.8 %collective-permute-done.17.ra_ref = f32[12,16,128]{2,1,0:T(8,128)S(1)} collective-permute-done((f32[12,16,128]{2,1,0:T(8,128)S(1)}, f32[12,16,128]{2,1,0:T(8,128)S(1)}, u32[]{:S(2)}, u32[]{:S(2)}) %collective-permute-start.17) | collective-permute-done | bytes 98336 | tf_op jit(solution)/shard_map/ppermute | solution.py:505
  123.8 0.8 collective-permute-done.18.rb_ref
  124.6 1.5 shard_map.62
  126.0 1.1 collective-permute-start.21
  127.2 3.2 %collective-permute-start.20 = (f32[12,16,128]{2,1,0:T(8,128)S(1)}, f32[12,16,128]{2,1,0:T(8,128)S(1)}, u32[]{:S(2)}, u32[]{:S(2)}) collective-permute-start(f32[12,16,128]{2,1,0:T(8,128)S(1)} %get-tuple-element.125), channel_id=1, source_target_pairs={{0,32},{32,0},{64,96},{96,64},{128,160},{160,128},{192,224},{224,1... | collective-permute-start | bytes 294920 | tf_op jit(solution)/shard_map/ppermute | solution.py:505
  130.7 2.2 %collective-permute-done.20.ra_ref = f32[12,16,128]{2,1,0:T(8,128)S(1)} collective-permute-done((f32[12,16,128]{2,1,0:T(8,128)S(1)}, f32[12,16,128]{2,1,0:T(8,128)S(1)}, u32[]{:S(2)}, u32[]{:S(2)}) %collective-permute-start.20) | collective-permute-done | bytes 98336 | tf_op jit(solution)/shard_map/ppermute | solution.py:505
  132.9 1.5 shard_map.63
  134.4 19.1 %all_to_all.22.e_ref = f32[8,8,16,128]{3,2,1,0:T(8,128)S(1)} all-to-all(f32[8,8,16,128]{3,2,1,0:T(8,128)S(1)} %shard_map.63), channel_id=1, replica_groups=mesh['z'=8,'core'=2,'space'=16] {'z'}, dimensions={0} | all-to-all | bytes 1048576 | tf_op jit(solution)/shard_map/all_to_all | solution.py:526
  153.6 1.5 collective-permute-start.22
  155.4 2.9 %shard_map.64 = (f32[3072,128]{1,0:T(8,128)S(1)}, f32[2,8,16,128]{3,2,1,0:T(8,128)S(1)}) custom-call(f32[8,8,16,128]{3,2,1,0:T(8,128)S(1)} %all_to_all.22.e_ref, f32[64,16,128]{2,1,0:T(8,128)S(1)} %collective-permute-done.7.cp_ref, f32[2,8,16,128]{3,2,1,0:T(8,128)S(1)} %collective-permute-done.10.r0_ref, ...), custom_call_target="tpu_custom_call" | custom-call | tf_op jit(solution)/shard_map/pallas_call | solution.py:533
  159.8 20.1 %all_to_all.23.a_ref = f32[16,192,128]{2,1,0:T(8,128)S(1)} all-to-all(f32[16,192,128]{2,1,0:T(8,128)S(1)} %bitcast.11), channel_id=1, replica_groups=mesh['z'=8,'core'=2,'space'=16] {'space'}, dimensions={0} | all-to-all | bytes 3145728 | tf_op jit(solution)/shard_map/all_to_all | solution.py:544
  180.0 1.4 shard_map.67
  (23 shorter events, 5.5 us)
Async XLA Ops:
  33.1 2.4 %collective-permute-start = (f32[96,16,128]{2,1,0:T(8,128)S(1)}, f32[96,16,128]{2,1,0:T(8,128)S(1)}, u32[]{:S(2)}, u32[]{:S(2)}) collective-permute-start(f32[96,16,128]{2,1,0:T(8,128)S(1)} %shard_map.52.own_ref), channel_id=1, source_target_pairs={{0,16},{16,0},{1,17},{17,1},{2,18},{18,2},{3,19},{19,3},{4,20},{20... | collective-permute-start | bytes 2359304 | tf_op jit(solution)/shard_map/ppermute | solution.py:471
  39.5 12.3 %collective-permute-start.1 = (f32[64,16,128]{2,1,0:T(8,128)S(1)}, f32[64,16,128]{2,1,0:T(8,128)S(1)}, u32[]{:S(2)}, u32[]{:S(2)}) collective-permute-start(f32[64,16,128]{2,1,0:T(8,128)S(1)} %get-tuple-element.95), channel_id=1, source_target_pairs={{0,240},{1,241},{2,242},{3,243},{4,244},{5,245},{6,246},{7,247},{8... | collective-permute-start | bytes 1572872 | tf_op jit(solution)/shard_map/ppermute | solution.py:490
  73.6 1.9 %collective-permute-start.2 = (f32[8,8,16,128]{3,2,1,0:T(8,128)S(1)}, f32[8,8,16,128]{3,2,1,0:T(8,128)S(1)}, u32[]{:S(2)}, u32[]{:S(2)}) collective-permute-start(f32[8,8,16,128]{3,2,1,0:T(8,128)S(1)} %all_to_all.21.own_ref), channel_id=1, source_target_pairs={{0,16},{16,0},{1,17},{17,1},{2,18},{18,2},{3,19},{19,3},{4,20},{20... | collective-permute-start | bytes 1572872 | tf_op jit(solution)/shard_map/ppermute | solution.py:471
  75.6 4.9 %collective-permute-start.3 = (f32[12,16,128]{2,1,0:T(8,128)S(1)}, f32[12,16,128]{2,1,0:T(8,128)S(1)}, u32[]{:S(2)}, u32[]{:S(2)}) collective-permute-start(f32[12,16,128]{2,1,0:T(8,128)S(1)} %get-tuple-element.81), channel_id=1, source_target_pairs={{0,32},{32,0},{64,96},{96,64},{128,160},{160,128},{192,224},{224,1... | collective-permute-start | bytes 294920 | tf_op jit(solution)/shard_map/ppermute | solution.py:505
  75.9 4.9 %collective-permute-start.4 = (f32[12,16,128]{2,1,0:T(8,128)S(1)}, f32[12,16,128]{2,1,0:T(8,128)S(1)}, u32[]{:S(2)}, u32[]{:S(2)}) collective-permute-start(f32[12,16,128]{2,1,0:T(8,128)S(1)} %get-tuple-element.82), channel_id=1, source_target_pairs={{32,64},{64,32},{96,128},{128,96},{160,192},{192,160},{224,225},{2... | collective-permute-start | bytes 294920 | tf_op jit(solution)/shard_map/ppermute | solution.py:506
  80.8 11.6 %collective-permute-start.7 = (f32[64,16,128]{2,1,0:T(8,128)S(1)}, f32[64,16,128]{2,1,0:T(8,128)S(1)}, u32[]{:S(2)}, u32[]{:S(2)}) collective-permute-start(f32[64,16,128]{2,1,0:T(8,128)S(1)} %get-tuple-element.95), channel_id=1, source_target_pairs={{0,16},{1,17},{2,18},{3,19},{4,20},{5,21},{6,22},{7,23},{8,24},{9,... | collective-permute-start | bytes 1572872 | tf_op jit(solution)/shard_map/ppermute | solution.py:510
  82.3 5.1 %collective-permute-start.5 = (f32[12,16,128]{2,1,0:T(8,128)S(1)}, f32[12,16,128]{2,1,0:T(8,128)S(1)}, u32[]{:S(2)}, u32[]{:S(2)}) collective-permute-start(f32[12,16,128]{2,1,0:T(8,128)S(1)} %get-tuple-element.88), channel_id=1, source_target_pairs={{0,32},{32,0},{64,96},{96,64},{128,160},{160,128},{192,224},{224,1... | collective-permute-start | bytes 294920 | tf_op jit(solution)/shard_map/ppermute | solution.py:505
  83.9 4.9 %collective-permute-start.6 = (f32[12,16,128]{2,1,0:T(8,128)S(1)}, f32[12,16,128]{2,1,0:T(8,128)S(1)}, u32[]{:S(2)}, u32[]{:S(2)}) collective-permute-start(f32[12,16,128]{2,1,0:T(8,128)S(1)} %get-tuple-element.89), channel_id=1, source_target_pairs={{32,64},{64,32},{96,128},{128,96},{160,192},{192,160},{224,225},{2... | collective-permute-start | bytes 294920 | tf_op jit(solution)/shard_map/ppermute | solution.py:506
  88.8 12.3 %collective-permute-start.10 = (f32[2,8,16,128]{3,2,1,0:T(8,128)S(1)}, f32[2,8,16,128]{3,2,1,0:T(8,128)S(1)}, u32[]{:S(2)}, u32[]{:S(2)}) collective-permute-start(f32[2,8,16,128]{3,2,1,0:T(8,128)S(1)} %get-tuple-element.103), channel_id=1, source_target_pairs={{0,32},{1,33},{2,34},{3,35},{4,36},{5,37},{6,38},{7,39},{8,40},{9,... | collective-permute-start | bytes 393224 | tf_op jit(solution)/shard_map/ppermute | solution.py:510
  91.3 4.7 %collective-permute-start.9 = (f32[12,16,128]{2,1,0:T(8,128)S(1)}, f32[12,16,128]{2,1,0:T(8,128)S(1)}, u32[]{:S(2)}, u32[]{:S(2)}) collective-permute-start(f32[12,16,128]{2,1,0:T(8,128)S(1)} %get-tuple-element.97), channel_id=1, source_target_pairs={{32,64},{64,32},{96,128},{128,96},{160,192},{192,160},{224,225},{2... | collective-permute-start | bytes 294920 | tf_op jit(solution)/shard_map/ppermute | solution.py:506
  92.4 4.8 %collective-permute-start.8 = (f32[12,16,128]{2,1,0:T(8,128)S(1)}, f32[12,16,128]{2,1,0:T(8,128)S(1)}, u32[]{:S(2)}, u32[]{:S(2)}) collective-permute-start(f32[12,16,128]{2,1,0:T(8,128)S(1)} %get-tuple-element.96), channel_id=1, source_target_pairs={{0,32},{32,0},{64,96},{96,64},{128,160},{160,128},{192,224},{224,1... | collective-permute-start | bytes 294920 | tf_op jit(solution)/shard_map/ppermute | solution.py:505
  97.2 13.8 %collective-permute-start.13 = (f32[2,8,16,128]{3,2,1,0:T(8,128)S(1)}, f32[2,8,16,128]{3,2,1,0:T(8,128)S(1)}, u32[]{:S(2)}, u32[]{:S(2)}) collective-permute-start(f32[2,8,16,128]{3,2,1,0:T(8,128)S(1)} %get-tuple-element.111), channel_id=1, source_target_pairs={{0,32},{1,33},{2,34},{3,35},{4,36},{5,37},{6,38},{7,39},{8,40},{9,... | collective-permute-start | bytes 393224 | tf_op jit(solution)/shard_map/ppermute | solution.py:510
  101.2 4.7 %collective-permute-start.11 = (f32[12,16,128]{2,1,0:T(8,128)S(1)}, f32[12,16,128]{2,1,0:T(8,128)S(1)}, u32[]{:S(2)}, u32[]{:S(2)}) collective-permute-start(f32[12,16,128]{2,1,0:T(8,128)S(1)} %get-tuple-element.104), channel_id=1, source_target_pairs={{0,32},{32,0},{64,96},{96,64},{128,160},{160,128},{192,224},{224,1... | collective-permute-start | bytes 294920 | tf_op jit(solution)/shard_map/ppermute | solution.py:505
  101.9 4.6 %collective-permute-start.12 = (f32[12,16,128]{2,1,0:T(8,128)S(1)}, f32[12,16,128]{2,1,0:T(8,128)S(1)}, u32[]{:S(2)}, u32[]{:S(2)}) collective-permute-start(f32[12,16,128]{2,1,0:T(8,128)S(1)} %get-tuple-element.105), channel_id=1, source_target_pairs={{32,64},{64,32},{96,128},{128,96},{160,192},{192,160},{224,225},{2... | collective-permute-start | bytes 294920 | tf_op jit(solution)/shard_map/ppermute | solution.py:506
  106.5 12.6 %collective-permute-start.16 = (f32[2,8,16,128]{3,2,1,0:T(8,128)S(1)}, f32[2,8,16,128]{3,2,1,0:T(8,128)S(1)}, u32[]{:S(2)}, u32[]{:S(2)}) collective-permute-start(f32[2,8,16,128]{3,2,1,0:T(8,128)S(1)} %get-tuple-element.119), channel_id=1, source_target_pairs={{0,32},{1,33},{2,34},{3,35},{4,36},{5,37},{6,38},{7,39},{8,40},{9,... | collective-permute-start | bytes 393224 | tf_op jit(solution)/shard_map/ppermute | solution.py:510
  109.9 4.7 %collective-permute-start.15 = (f32[12,16,128]{2,1,0:T(8,128)S(1)}, f32[12,16,128]{2,1,0:T(8,128)S(1)}, u32[]{:S(2)}, u32[]{:S(2)}) collective-permute-start(f32[12,16,128]{2,1,0:T(8,128)S(1)} %get-tuple-element.113), channel_id=1, source_target_pairs={{32,64},{64,32},{96,128},{128,96},{160,192},{192,160},{224,225},{2... | collective-permute-start | bytes 294920 | tf_op jit(solution)/shard_map/ppermute | solution.py:506
  111.0 4.6 %collective-permute-start.14 = (f32[12,16,128]{2,1,0:T(8,128)S(1)}, f32[12,16,128]{2,1,0:T(8,128)S(1)}, u32[]{:S(2)}, u32[]{:S(2)}) collective-permute-start(f32[12,16,128]{2,1,0:T(8,128)S(1)} %get-tuple-element.112), channel_id=1, source_target_pairs={{0,32},{32,0},{64,96},{96,64},{128,160},{160,128},{192,224},{224,1... | collective-permute-start | bytes 294920 | tf_op jit(solution)/shard_map/ppermute | solution.py:505
  115.6 11.5 %collective-permute-start.19 = (f32[2,8,16,128]{3,2,1,0:T(8,128)S(1)}, f32[2,8,16,128]{3,2,1,0:T(8,128)S(1)}, u32[]{:S(2)}, u32[]{:S(2)}) collective-permute-start(f32[2,8,16,128]{3,2,1,0:T(8,128)S(1)} %get-tuple-element.124), channel_id=1, source_target_pairs={{0,32},{1,33},{2,34},{3,35},{4,36},{5,37},{6,38},{7,39},{8,40},{9,... | collective-permute-start | bytes 393224 | tf_op jit(solution)/shard_map/ppermute | solution.py:510
  119.1 4.7 %collective-permute-start.17 = (f32[12,16,128]{2,1,0:T(8,128)S(1)}, f32[12,16,128]{2,1,0:T(8,128)S(1)}, u32[]{:S(2)}, u32[]{:S(2)}) collective-permute-start(f32[12,16,128]{2,1,0:T(8,128)S(1)} %get-tuple-element.120), channel_id=1, source_target_pairs={{0,32},{32,0},{64,96},{96,64},{128,160},{160,128},{192,224},{224,1... | collective-permute-start | bytes 294920 | tf_op jit(solution)/shard_map/ppermute | solution.py:505
  119.9 4.6 %collective-permute-start.18 = (f32[12,16,128]{2,1,0:T(8,128)S(1)}, f32[12,16,128]{2,1,0:T(8,128)S(1)}, u32[]{:S(2)}, u32[]{:S(2)}) collective-permute-start(f32[12,16,128]{2,1,0:T(8,128)S(1)} %get-tuple-element.121), channel_id=1, source_target_pairs={{32,64},{64,32},{96,128},{128,96},{160,192},{192,160},{224,225},{2... | collective-permute-start | bytes 294920 | tf_op jit(solution)/shard_map/ppermute | solution.py:506
  126.0 4.7 %collective-permute-start.21 = (f32[12,16,128]{2,1,0:T(8,128)S(1)}, f32[12,16,128]{2,1,0:T(8,128)S(1)}, u32[]{:S(2)}, u32[]{:S(2)}) collective-permute-start(f32[12,16,128]{2,1,0:T(8,128)S(1)} %get-tuple-element.126), channel_id=1, source_target_pairs={{32,64},{64,32},{96,128},{128,96},{160,192},{192,160},{224,225},{2... | collective-permute-start | bytes 294920 | tf_op jit(solution)/shard_map/ppermute | solution.py:506
  127.2 5.8 %collective-permute-start.20 = (f32[12,16,128]{2,1,0:T(8,128)S(1)}, f32[12,16,128]{2,1,0:T(8,128)S(1)}, u32[]{:S(2)}, u32[]{:S(2)}) collective-permute-start(f32[12,16,128]{2,1,0:T(8,128)S(1)} %get-tuple-element.125), channel_id=1, source_target_pairs={{0,32},{32,0},{64,96},{96,64},{128,160},{160,128},{192,224},{224,1... | collective-permute-start | bytes 294920 | tf_op jit(solution)/shard_map/ppermute | solution.py:505
  153.6 4.7 %collective-permute-start.22 = (f32[4,16,128]{2,1,0:T(8,128)S(1)}, f32[4,16,128]{2,1,0:T(8,128)S(1)}, u32[]{:S(2)}, u32[]{:S(2)}) collective-permute-start(f32[4,16,128]{2,1,0:T(8,128)S(1)} %get-tuple-element.142), channel_id=1, source_target_pairs={{0,1},{1,0},{2,3},{3,2},{7,6},{6,7},{5,4},{4,5},{8,9},{9,8},{10,11... | collective-permute-start | bytes 98312 | tf_op jit(solution)/shard_map/ppermute | solution.py:531
  155.2 3.9 %collective-permute-start.23 = (f32[4,16,128]{2,1,0:T(8,128)S(1)}, f32[4,16,128]{2,1,0:T(8,128)S(1)}, u32[]{:S(2)}, u32[]{:S(2)}) collective-permute-start(f32[4,16,128]{2,1,0:T(8,128)S(1)} %get-tuple-element.143), channel_id=1, source_target_pairs={{1,2},{2,1},{3,7},{7,3},{6,5},{5,6},{4,8},{8,4},{9,10},{10,9},{11,... | collective-permute-start | bytes 98312 | tf_op jit(solution)/shard_map/ppermute | solution.py:532

commit v6 on v5

--- a/solution.py
+++ b/solution.py
@@ -167,15 +167,16 @@
     zero = jnp.zeros((HALO, LANES), F32)
 
     def copies(ref, to, first):
+        bands = [pl.ds(m * 16, 16) for m in range(8)]
         return [
-            pltpu.make_async_copy(
-                ref.at[:, pl.ds(m * LANES, LANES)], to.at[:, pl.ds(m * LANES, LANES)], sems.at[first + m]
-            )
-            for m in range(8)
+            pltpu.make_async_copy(ref.at[band], to.at[band], sems.at[first + m])
+            for m, band in enumerate(bands)
         ]
 
     def spread(arriving, ref, base):
         leaving = []
+        for copy in arriving:
+            copy.wait()
 
         def send(k):
             rows = pl.ds(base, WIDE)
@@ -189,7 +190,6 @@
         o_ref[SNAKE[0], base : base + HALO] = zero
         o_ref[SNAKE[NSP - 1], base + HALO + CHUNK : base + WIDE] = zero
         for m in range(8):
-            arriving[m].wait()
             tile = ref[:, m * LANES : (m + 1) * LANES].T
             for half in range(2):
                 k = 2 * m + half
@@ -334,16 +334,18 @@
     right = jnp.where(top & (sub == NZD - 1), 0.0, jnp.where(odd == 0, ra, rb))
     e = jnp.concatenate([left[:PIECE], e_ref[...], right[:PIECE]], 0)
     r1 = jnp.concatenate([left[PIECE:], r_ref[t + 1], right[PIECE:]], 0)
-    inv, cc = inv_ref[...], cc_ref[...]
-    e1 = coarse_step(e, inv, cc) + r1
-    e2 = coarse_step(e1, inv[STRIP:-STRIP], cc[STRIP:-STRIP]) + r_ref[t + 2]
-    return e1[STRIP:-STRIP], e2
+    return coarse_step(e, inv_ref[...], cc_ref[...]) + r1
+
+
+def next_step(t, e1, r_ref, inv_ref, cc_ref):
+    return coarse_step(e1, inv_ref[STRIP:-STRIP], cc_ref[STRIP:-STRIP]) + r_ref[t + 2]
 
 
 def chain_kernel(t, ra_ref, rb_ref, e_ref, r_ref, inv_ref, cc_ref, e1_ref, e2_ref, a_ref, b_ref):
     sub = position()[3]
-    e1, e2 = chain_step(t, ra_ref, rb_ref, e_ref, r_ref, inv_ref, cc_ref)
-    e1_ref[...] = e1
+    e1 = chain_step(t, ra_ref, rb_ref, e_ref, r_ref, inv_ref, cc_ref)
+    e1_ref[...] = e1[STRIP:-STRIP]
+    e2 = next_step(t, e1, r_ref, inv_ref, cc_ref)
     e2_ref[...] = e2
     messages(sub % 2, e2, r_ref[t + 3], a_ref, b_ref)
 
@@ -351,10 +353,18 @@
 def chain_end_kernel(t, ra_ref, rb_ref, r_ref, inv_ref, cc_ref, *refs):
     core = lax.axis_index("core")
     e_refs, o_ref = refs[:-1], refs[-1]
-    e1, e2 = chain_step(t, ra_ref, rb_ref, e_refs[-1], r_ref, inv_ref, cc_ref)
-    errors = [jnp.zeros(e1.shape, F32)] + [ref[...] for ref in e_refs] + [e1, e2]
-    for n in range(NT // 2):
+    errors = [jnp.zeros(e_refs[0].shape, F32)] + [ref[...] for ref in e_refs]
+    for n in range(NT // 2 - 1):
         o_ref[n] = jnp.where(core == 0, errors[2 * n], errors[2 * n + 1])
+    e1 = chain_step(t, ra_ref, rb_ref, e_refs[-1], r_ref, inv_ref, cc_ref)
+
+    @pl.when(core == 0)
+    def _():
+        o_ref[NT // 2 - 1] = e1[STRIP:-STRIP]
+
+    @pl.when(core != 0)
+    def _():
+        o_ref[NT // 2 - 1] = next_step(t, e1, r_ref, inv_ref, cc_ref)
 
 
 def keep(o_ref, which, values_ref, low, high):

time: 182 us -> 182 us (level)
  no operation moved by 1% of the time
where the time goes in v6:
time: 182 us; the launch traced here: 181 us
  blocking collectives  90.1 us (50%)
  starting transfers between devices  33.7 us (19%)
  waiting for transfers between devices  30.6 us (17%)
  Pallas kernels  26.1 us (14%)
    all_to_all x1, blocking collectives, body(): got = lax.all_to_all(sent, 'space', 0, 0).reshape(-1, LANES)  28.4 us
    all_to_all x1, blocking collectives, body(): mine = lax.all_to_all(r, 'z', 0, 0)  21.7 us
    all_to_all x1, blocking collectives, body(): got = lax.all_to_all(sent.reshape(NSP, 3 * CHUNK, LANES), 'space', 0, 0)  20.9 us
    all_to_all x1, blocking collectives, body(): chunk = lax.all_to_all(errors, 'z', 0, 0)  19.1 us
    ppermute x7, waiting for transfers between devices, body(): ra = lax.ppermute(ma, everyone, pairs_a)  16.3 us
    ppermute x7, starting transfers between devices, body(): ra = lax.ppermute(ma, everyone, pairs_a)  10.5 us
    pallas_call x6, Pallas kernels, body(): call(functools.partial(chain_kernel, t), [piece, piece, message, message]...  8.76 us
    ppermute x7, starting transfers between devices, body(): rb = lax.ppermute(mb, everyone, pairs_b)  7.59 us
  transfers between devices with their start and end apart: 24, of which 18 were waited for; matrix products, arithmetic and copies ran while one was open for 0% of the time, Pallas kernels for 9%

profile of v6, /device:TPU:8, one launch (start us, length us, event | category | flops | bytes accessed | tf_op | source)
XLA Modules:
  0.0 181.4 jit_solution(12724007238992373433)
XLA Ops:
  0.6 2.8 %shard_map.50 = f32[16,192,128]{2,1,0:T(8,128)} custom-call(f32[128,1024]{1,0:T(8,128)} %bitcast.12, f32[128,1024]{1,0:T(8,128)} %bitcast.13, f32[128,1024]{1,0:T(8,128)} %bitcast.14), custom_call_target="tpu_custom_call" | custom-call | tf_op jit(solution)/shard_map/pallas_call | solution.py:483
  3.4 28.4 %all_to_all.20 = f32[16,192,128]{2,1,0:T(8,128)S(1)} all-to-all(f32[16,192,128]{2,1,0:T(8,128)} %shard_map.50), channel_id=1, replica_groups=mesh['z'=8,'core'=2,'space'=16] {'space'}, dimensions={0} | all-to-all | bytes 3145728 | tf_op jit(solution)/shard_map/all_to_all | solution.py:486
  33.0 1.7 collective-permute-done.oth_ref
  34.7 4.0 %shard_map.53 = (f32[96,16,128]{2,1,0:T(8,128)S(1)}, f32[64,16,128]{2,1,0:T(8,128)S(1)}, f32[24,16,128]{2,1,0:T(8,128)S(1)}, f32[24,16,128]{2,1,0:T(8,128)S(1)},...) custom-call(f32[96,16,128]{2,1,0:T(8,128)S(1)} %get-tuple-element.74, ...), custom_call_target="tpu_custom_call", output_to_operand_aliasing={{0}: (0, {})} | custom-call | tf_op jit(solution)/shard_map/pallas_call | solution.py:492
  38.7 5.6 %collective-permute-start.1 = (f32[64,16,128]{2,1,0:T(8,128)S(1)}, f32[64,16,128]{2,1,0:T(8,128)S(1)}, u32[]{:S(2)}, u32[]{:S(2)}) collective-permute-start(f32[64,16,128]{2,1,0:T(8,128)S(1)} %get-tuple-element.95), channel_id=1, source_target_pairs={{0,240},{1,241},{2,242},{3,243},{4,244},{5,245},{6,246},{7,247},{8... | collective-permute-start | bytes 1572872 | tf_op jit(solution)/shard_map/ppermute | solution.py:500
  44.3 3.3 %shard_map.54.w_ref = f32[64,16,128]{2,1,0:T(8,128)S(1)} custom-call(f32[96,16,128]{2,1,0:T(8,128)S(1)} %get-tuple-element.75.u_ref, f32[96,16,128]{2,1,0:T(8,128)S(1)} %get-tuple-element.76.inv_ref, f32[96,16,128]{2,1,0:T(8,128)S(1)} %get-tuple-element.77.cc_ref, f32[96,16,128]{2,1,0:T(8,128)S(1)} %get-tuple-element.78.sinv_ref), custom_call_target="tpu_custom_call" | custom-call | tf_op jit(solution)/shard_map/pallas_call | solution.py:501
  47.6 3.4 %collective-permute-done.1.next_ref = f32[64,16,128]{2,1,0:T(8,128)S(1)} collective-permute-done((f32[64,16,128]{2,1,0:T(8,128)S(1)}, f32[64,16,128]{2,1,0:T(8,128)S(1)}, u32[]{:S(2)}, u32[]{:S(2)}) %collective-permute-start.1) | collective-permute-done | bytes 524320 | tf_op jit(solution)/shard_map/ppermute | solution.py:500
  51.1 21.7 %all_to_all.21.own_ref = f32[8,8,16,128]{3,2,1,0:T(8,128)S(1)} all-to-all(f32[8,8,16,128]{3,2,1,0:T(8,128)S(1)} %get-tuple-element.80), channel_id=1, replica_groups=mesh['z'=8,'core'=2,'space'=16] {'z'}, dimensions={0} | all-to-all | bytes 1048576 | tf_op jit(solution)/shard_map/all_to_all | solution.py:504
  72.9 1.8 collective-permute-done.2.oth_ref
  75.1 1.1 collective-permute-start.4
  76.2 3.5 %collective-permute-done.3.ra_ref = f32[12,16,128]{2,1,0:T(8,128)S(1)} collective-permute-done((f32[12,16,128]{2,1,0:T(8,128)S(1)}, f32[12,16,128]{2,1,0:T(8,128)S(1)}, u32[]{:S(2)}, u32[]{:S(2)}) %collective-permute-start.3) | collective-permute-done | bytes 98336 | tf_op jit(solution)/shard_map/ppermute | solution.py:515
  80.0 1.5 shard_map.57
  81.5 1.6 collective-permute-start.5
  83.1 1.0 collective-permute-start.6
  84.2 2.5 %collective-permute-done.5.ra_ref = f32[12,16,128]{2,1,0:T(8,128)S(1)} collective-permute-done((f32[12,16,128]{2,1,0:T(8,128)S(1)}, f32[12,16,128]{2,1,0:T(8,128)S(1)}, u32[]{:S(2)}, u32[]{:S(2)}) %collective-permute-start.5) | collective-permute-done | bytes 98336 | tf_op jit(solution)/shard_map/ppermute | solution.py:515
  86.6 1.4 collective-permute-done.6.rb_ref
  88.0 1.0 collective-permute-start.10
  89.0 1.5 shard_map.58
  90.5 1.1 collective-permute-start.9
  91.6 1.9 %collective-permute-start.8 = (f32[12,16,128]{2,1,0:T(8,128)S(1)}, f32[12,16,128]{2,1,0:T(8,128)S(1)}, u32[]{:S(2)}, u32[]{:S(2)}) collective-permute-start(f32[12,16,128]{2,1,0:T(8,128)S(1)} %get-tuple-element.96), channel_id=1, source_target_pairs={{0,32},{32,0},{64,96},{96,64},{128,160},{160,128},{192,224},{224,1... | collective-permute-start | bytes 294920 | tf_op jit(solution)/shard_map/ppermute | solution.py:515
  93.5 1.7 collective-permute-done.9.rb_ref
  95.2 1.3 collective-permute-done.8.ra_ref
  96.4 2.5 %collective-permute-start.13 = (f32[2,8,16,128]{3,2,1,0:T(8,128)S(1)}, f32[2,8,16,128]{3,2,1,0:T(8,128)S(1)}, u32[]{:S(2)}, u32[]{:S(2)}) collective-permute-start(f32[2,8,16,128]{3,2,1,0:T(8,128)S(1)} %get-tuple-element.111), channel_id=1, source_target_pairs={{0,32},{1,33},{2,34},{3,35},{4,36},{5,37},{6,38},{7,39},{8,40},{9,... | collective-permute-start | bytes 393224 | tf_op jit(solution)/shard_map/ppermute | solution.py:520
  98.9 1.5 shard_map.59
  101.1 1.0 collective-permute-start.12
  102.1 3.0 %collective-permute-done.11.ra_ref = f32[12,16,128]{2,1,0:T(8,128)S(1)} collective-permute-done((f32[12,16,128]{2,1,0:T(8,128)S(1)}, f32[12,16,128]{2,1,0:T(8,128)S(1)}, u32[]{:S(2)}, u32[]{:S(2)}) %collective-permute-start.11) | collective-permute-done | bytes 98336 | tf_op jit(solution)/shard_map/ppermute | solution.py:515
  105.7 2.0 %collective-permute-start.16 = (f32[2,8,16,128]{3,2,1,0:T(8,128)S(1)}, f32[2,8,16,128]{3,2,1,0:T(8,128)S(1)}, u32[]{:S(2)}, u32[]{:S(2)}) collective-permute-start(f32[2,8,16,128]{3,2,1,0:T(8,128)S(1)} %get-tuple-element.119), channel_id=1, source_target_pairs={{0,32},{1,33},{2,34},{3,35},{4,36},{5,37},{6,38},{7,39},{8,40},{9,... | collective-permute-start | bytes 393224 | tf_op jit(solution)/shard_map/ppermute | solution.py:520
  107.6 1.5 shard_map.60
  109.1 1.1 collective-permute-start.15
  110.2 2.0 %collective-permute-start.14 = (f32[12,16,128]{2,1,0:T(8,128)S(1)}, f32[12,16,128]{2,1,0:T(8,128)S(1)}, u32[]{:S(2)}, u32[]{:S(2)}) collective-permute-start(f32[12,16,128]{2,1,0:T(8,128)S(1)} %get-tuple-element.112), channel_id=1, source_target_pairs={{0,32},{32,0},{64,96},{96,64},{128,160},{160,128},{192,224},{224,1... | collective-permute-start | bytes 294920 | tf_op jit(solution)/shard_map/ppermute | solution.py:515
  112.2 1.6 collective-permute-done.15.rb_ref
  113.8 1.0 collective-permute-done.14.ra_ref
  114.8 2.0 %collective-permute-start.19 = (f32[2,8,16,128]{3,2,1,0:T(8,128)S(1)}, f32[2,8,16,128]{3,2,1,0:T(8,128)S(1)}, u32[]{:S(2)}, u32[]{:S(2)}) collective-permute-start(f32[2,8,16,128]{3,2,1,0:T(8,128)S(1)} %get-tuple-element.124), channel_id=1, source_target_pairs={{0,32},{1,33},{2,34},{3,35},{4,36},{5,37},{6,38},{7,39},{8,40},{9,... | collective-permute-start | bytes 393224 | tf_op jit(solution)/shard_map/ppermute | solution.py:520
  116.8 1.5 shard_map.61
  118.3 0.9 collective-permute-start.17
  119.1 1.0 collective-permute-start.18
  120.2 2.8 %collective-permute-done.17.ra_ref = f32[12,16,128]{2,1,0:T(8,128)S(1)} collective-permute-done((f32[12,16,128]{2,1,0:T(8,128)S(1)}, f32[12,16,128]{2,1,0:T(8,128)S(1)}, u32[]{:S(2)}, u32[]{:S(2)}) %collective-permute-start.17) | collective-permute-done | bytes 98336 | tf_op jit(solution)/shard_map/ppermute | solution.py:515
  123.0 0.8 collective-permute-done.18.rb_ref
  123.8 1.5 shard_map.62
  125.2 1.1 collective-permute-start.21
  126.3 3.2 %collective-permute-start.20 = (f32[12,16,128]{2,1,0:T(8,128)S(1)}, f32[12,16,128]{2,1,0:T(8,128)S(1)}, u32[]{:S(2)}, u32[]{:S(2)}) collective-permute-start(f32[12,16,128]{2,1,0:T(8,128)S(1)} %get-tuple-element.125), channel_id=1, source_target_pairs={{0,32},{32,0},{64,96},{96,64},{128,160},{160,128},{192,224},{224,1... | collective-permute-start | bytes 294920 | tf_op jit(solution)/shard_map/ppermute | solution.py:515
  129.9 2.2 %collective-permute-done.20.ra_ref = f32[12,16,128]{2,1,0:T(8,128)S(1)} collective-permute-done((f32[12,16,128]{2,1,0:T(8,128)S(1)}, f32[12,16,128]{2,1,0:T(8,128)S(1)}, u32[]{:S(2)}, u32[]{:S(2)}) %collective-permute-start.20) | collective-permute-done | bytes 98336 | tf_op jit(solution)/shard_map/ppermute | solution.py:515
  132.1 0.9 shard_map.63
  133.0 19.1 %all_to_all.22.e_ref = f32[8,8,16,128]{3,2,1,0:T(8,128)S(1)} all-to-all(f32[8,8,16,128]{3,2,1,0:T(8,128)S(1)} %shard_map.63), channel_id=1, replica_groups=mesh['z'=8,'core'=2,'space'=16] {'z'}, dimensions={0} | all-to-all | bytes 1048576 | tf_op jit(solution)/shard_map/all_to_all | solution.py:536
  152.2 2.1 %collective-permute-start.22 = (f32[4,16,128]{2,1,0:T(8,128)S(1)}, f32[4,16,128]{2,1,0:T(8,128)S(1)}, u32[]{:S(2)}, u32[]{:S(2)}) collective-permute-start(f32[4,16,128]{2,1,0:T(8,128)S(1)} %get-tuple-element.142), channel_id=1, source_target_pairs={{0,1},{1,0},{2,3},{3,2},{7,6},{6,7},{5,4},{4,5},{8,9},{9,8},{10,11... | collective-permute-start | bytes 98312 | tf_op jit(solution)/shard_map/ppermute | solution.py:541
  154.7 2.9 %shard_map.64 = (f32[3072,128]{1,0:T(8,128)S(1)}, f32[2,8,16,128]{3,2,1,0:T(8,128)S(1)}) custom-call(f32[8,8,16,128]{3,2,1,0:T(8,128)S(1)} %all_to_all.22.e_ref, f32[64,16,128]{2,1,0:T(8,128)S(1)} %collective-permute-done.7.cp_ref, f32[2,8,16,128]{3,2,1,0:T(8,128)S(1)} %collective-permute-done.10.r0_ref, ...), custom_call_target="tpu_custom_call" | custom-call | tf_op jit(solution)/shard_map/pallas_call | solution.py:543
  159.0 20.9 %all_to_all.23.a_ref = f32[16,192,128]{2,1,0:T(8,128)S(1)} all-to-all(f32[16,192,128]{2,1,0:T(8,128)S(1)} %bitcast.11), channel_id=1, replica_groups=mesh['z'=8,'core'=2,'space'=16] {'space'}, dimensions={0} | all-to-all | bytes 3145728 | tf_op jit(solution)/shard_map/all_to_all | solution.py:554
  179.9 1.4 shard_map.67
  (23 shorter events, 5.5 us)
Async XLA Ops:
  32.3 2.4 %collective-permute-start = (f32[96,16,128]{2,1,0:T(8,128)S(1)}, f32[96,16,128]{2,1,0:T(8,128)S(1)}, u32[]{:S(2)}, u32[]{:S(2)}) collective-permute-start(f32[96,16,128]{2,1,0:T(8,128)S(1)} %shard_map.52.own_ref), channel_id=1, source_target_pairs={{0,16},{16,0},{1,17},{17,1},{2,18},{18,2},{3,19},{19,3},{4,20},{20... | collective-permute-start | bytes 2359304 | tf_op jit(solution)/shard_map/ppermute | solution.py:481
  38.7 12.3 %collective-permute-start.1 = (f32[64,16,128]{2,1,0:T(8,128)S(1)}, f32[64,16,128]{2,1,0:T(8,128)S(1)}, u32[]{:S(2)}, u32[]{:S(2)}) collective-permute-start(f32[64,16,128]{2,1,0:T(8,128)S(1)} %get-tuple-element.95), channel_id=1, source_target_pairs={{0,240},{1,241},{2,242},{3,243},{4,244},{5,245},{6,246},{7,247},{8... | collective-permute-start | bytes 1572872 | tf_op jit(solution)/shard_map/ppermute | solution.py:500
  72.8 1.9 %collective-permute-start.2 = (f32[8,8,16,128]{3,2,1,0:T(8,128)S(1)}, f32[8,8,16,128]{3,2,1,0:T(8,128)S(1)}, u32[]{:S(2)}, u32[]{:S(2)}) collective-permute-start(f32[8,8,16,128]{3,2,1,0:T(8,128)S(1)} %all_to_all.21.own_ref), channel_id=1, source_target_pairs={{0,16},{16,0},{1,17},{17,1},{2,18},{18,2},{3,19},{19,3},{4,20},{20... | collective-permute-start | bytes 1572872 | tf_op jit(solution)/shard_map/ppermute | solution.py:481
  74.8 4.9 %collective-permute-start.3 = (f32[12,16,128]{2,1,0:T(8,128)S(1)}, f32[12,16,128]{2,1,0:T(8,128)S(1)}, u32[]{:S(2)}, u32[]{:S(2)}) collective-permute-start(f32[12,16,128]{2,1,0:T(8,128)S(1)} %get-tuple-element.81), channel_id=1, source_target_pairs={{0,32},{32,0},{64,96},{96,64},{128,160},{160,128},{192,224},{224,1... | collective-permute-start | bytes 294920 | tf_op jit(solution)/shard_map/ppermute | solution.py:515
  75.1 4.9 %collective-permute-start.4 = (f32[12,16,128]{2,1,0:T(8,128)S(1)}, f32[12,16,128]{2,1,0:T(8,128)S(1)}, u32[]{:S(2)}, u32[]{:S(2)}) collective-permute-start(f32[12,16,128]{2,1,0:T(8,128)S(1)} %get-tuple-element.82), channel_id=1, source_target_pairs={{32,64},{64,32},{96,128},{128,96},{160,192},{192,160},{224,225},{2... | collective-permute-start | bytes 294920 | tf_op jit(solution)/shard_map/ppermute | solution.py:516
  80.0 11.6 %collective-permute-start.7 = (f32[64,16,128]{2,1,0:T(8,128)S(1)}, f32[64,16,128]{2,1,0:T(8,128)S(1)}, u32[]{:S(2)}, u32[]{:S(2)}) collective-permute-start(f32[64,16,128]{2,1,0:T(8,128)S(1)} %get-tuple-element.95), channel_id=1, source_target_pairs={{0,16},{1,17},{2,18},{3,19},{4,20},{5,21},{6,22},{7,23},{8,24},{9,... | collective-permute-start | bytes 1572872 | tf_op jit(solution)/shard_map/ppermute | solution.py:520
  81.5 5.1 %collective-permute-start.5 = (f32[12,16,128]{2,1,0:T(8,128)S(1)}, f32[12,16,128]{2,1,0:T(8,128)S(1)}, u32[]{:S(2)}, u32[]{:S(2)}) collective-permute-start(f32[12,16,128]{2,1,0:T(8,128)S(1)} %get-tuple-element.88), channel_id=1, source_target_pairs={{0,32},{32,0},{64,96},{96,64},{128,160},{160,128},{192,224},{224,1... | collective-permute-start | bytes 294920 | tf_op jit(solution)/shard_map/ppermute | solution.py:515
  83.1 4.9 %collective-permute-start.6 = (f32[12,16,128]{2,1,0:T(8,128)S(1)}, f32[12,16,128]{2,1,0:T(8,128)S(1)}, u32[]{:S(2)}, u32[]{:S(2)}) collective-permute-start(f32[12,16,128]{2,1,0:T(8,128)S(1)} %get-tuple-element.89), channel_id=1, source_target_pairs={{32,64},{64,32},{96,128},{128,96},{160,192},{192,160},{224,225},{2... | collective-permute-start | bytes 294920 | tf_op jit(solution)/shard_map/ppermute | solution.py:516
  88.0 12.3 %collective-permute-start.10 = (f32[2,8,16,128]{3,2,1,0:T(8,128)S(1)}, f32[2,8,16,128]{3,2,1,0:T(8,128)S(1)}, u32[]{:S(2)}, u32[]{:S(2)}) collective-permute-start(f32[2,8,16,128]{3,2,1,0:T(8,128)S(1)} %get-tuple-element.103), channel_id=1, source_target_pairs={{0,32},{1,33},{2,34},{3,35},{4,36},{5,37},{6,38},{7,39},{8,40},{9,... | collective-permute-start | bytes 393224 | tf_op jit(solution)/shard_map/ppermute | solution.py:520
  90.5 4.7 %collective-permute-start.9 = (f32[12,16,128]{2,1,0:T(8,128)S(1)}, f32[12,16,128]{2,1,0:T(8,128)S(1)}, u32[]{:S(2)}, u32[]{:S(2)}) collective-permute-start(f32[12,16,128]{2,1,0:T(8,128)S(1)} %get-tuple-element.97), channel_id=1, source_target_pairs={{32,64},{64,32},{96,128},{128,96},{160,192},{192,160},{224,225},{2... | collective-permute-start | bytes 294920 | tf_op jit(solution)/shard_map/ppermute | solution.py:516
  91.6 4.8 %collective-permute-start.8 = (f32[12,16,128]{2,1,0:T(8,128)S(1)}, f32[12,16,128]{2,1,0:T(8,128)S(1)}, u32[]{:S(2)}, u32[]{:S(2)}) collective-permute-start(f32[12,16,128]{2,1,0:T(8,128)S(1)} %get-tuple-element.96), channel_id=1, source_target_pairs={{0,32},{32,0},{64,96},{96,64},{128,160},{160,128},{192,224},{224,1... | collective-permute-start | bytes 294920 | tf_op jit(solution)/shard_map/ppermute | solution.py:515
  96.4 13.8 %collective-permute-start.13 = (f32[2,8,16,128]{3,2,1,0:T(8,128)S(1)}, f32[2,8,16,128]{3,2,1,0:T(8,128)S(1)}, u32[]{:S(2)}, u32[]{:S(2)}) collective-permute-start(f32[2,8,16,128]{3,2,1,0:T(8,128)S(1)} %get-tuple-element.111), channel_id=1, source_target_pairs={{0,32},{1,33},{2,34},{3,35},{4,36},{5,37},{6,38},{7,39},{8,40},{9,... | collective-permute-start | bytes 393224 | tf_op jit(solution)/shard_map/ppermute | solution.py:520
  100.4 4.7 %collective-permute-start.11 = (f32[12,16,128]{2,1,0:T(8,128)S(1)}, f32[12,16,128]{2,1,0:T(8,128)S(1)}, u32[]{:S(2)}, u32[]{:S(2)}) collective-permute-start(f32[12,16,128]{2,1,0:T(8,128)S(1)} %get-tuple-element.104), channel_id=1, source_target_pairs={{0,32},{32,0},{64,96},{96,64},{128,160},{160,128},{192,224},{224,1... | collective-permute-start | bytes 294920 | tf_op jit(solution)/shard_map/ppermute | solution.py:515
  101.1 4.6 %collective-permute-start.12 = (f32[12,16,128]{2,1,0:T(8,128)S(1)}, f32[12,16,128]{2,1,0:T(8,128)S(1)}, u32[]{:S(2)}, u32[]{:S(2)}) collective-permute-start(f32[12,16,128]{2,1,0:T(8,128)S(1)} %get-tuple-element.105), channel_id=1, source_target_pairs={{32,64},{64,32},{96,128},{128,96},{160,192},{192,160},{224,225},{2... | collective-permute-start | bytes 294920 | tf_op jit(solution)/shard_map/ppermute | solution.py:516
  105.7 12.6 %collective-permute-start.16 = (f32[2,8,16,128]{3,2,1,0:T(8,128)S(1)}, f32[2,8,16,128]{3,2,1,0:T(8,128)S(1)}, u32[]{:S(2)}, u32[]{:S(2)}) collective-permute-start(f32[2,8,16,128]{3,2,1,0:T(8,128)S(1)} %get-tuple-element.119), channel_id=1, source_target_pairs={{0,32},{1,33},{2,34},{3,35},{4,36},{5,37},{6,38},{7,39},{8,40},{9,... | collective-permute-start | bytes 393224 | tf_op jit(solution)/shard_map/ppermute | solution.py:520
  109.1 4.7 %collective-permute-start.15 = (f32[12,16,128]{2,1,0:T(8,128)S(1)}, f32[12,16,128]{2,1,0:T(8,128)S(1)}, u32[]{:S(2)}, u32[]{:S(2)}) collective-permute-start(f32[12,16,128]{2,1,0:T(8,128)S(1)} %get-tuple-element.113), channel_id=1, source_target_pairs={{32,64},{64,32},{96,128},{128,96},{160,192},{192,160},{224,225},{2... | collective-permute-start | bytes 294920 | tf_op jit(solution)/shard_map/ppermute | solution.py:516
  110.2 4.6 %collective-permute-start.14 = (f32[12,16,128]{2,1,0:T(8,128)S(1)}, f32[12,16,128]{2,1,0:T(8,128)S(1)}, u32[]{:S(2)}, u32[]{:S(2)}) collective-permute-start(f32[12,16,128]{2,1,0:T(8,128)S(1)} %get-tuple-element.112), channel_id=1, source_target_pairs={{0,32},{32,0},{64,96},{96,64},{128,160},{160,128},{192,224},{224,1... | collective-permute-start | bytes 294920 | tf_op jit(solution)/shard_map/ppermute | solution.py:515
  114.8 11.5 %collective-permute-start.19 = (f32[2,8,16,128]{3,2,1,0:T(8,128)S(1)}, f32[2,8,16,128]{3,2,1,0:T(8,128)S(1)}, u32[]{:S(2)}, u32[]{:S(2)}) collective-permute-start(f32[2,8,16,128]{3,2,1,0:T(8,128)S(1)} %get-tuple-element.124), channel_id=1, source_target_pairs={{0,32},{1,33},{2,34},{3,35},{4,36},{5,37},{6,38},{7,39},{8,40},{9,... | collective-permute-start | bytes 393224 | tf_op jit(solution)/shard_map/ppermute | solution.py:520
  118.3 4.7 %collective-permute-start.17 = (f32[12,16,128]{2,1,0:T(8,128)S(1)}, f32[12,16,128]{2,1,0:T(8,128)S(1)}, u32[]{:S(2)}, u32[]{:S(2)}) collective-permute-start(f32[12,16,128]{2,1,0:T(8,128)S(1)} %get-tuple-element.120), channel_id=1, source_target_pairs={{0,32},{32,0},{64,96},{96,64},{128,160},{160,128},{192,224},{224,1... | collective-permute-start | bytes 294920 | tf_op jit(solution)/shard_map/ppermute | solution.py:515
  119.1 4.6 %collective-permute-start.18 = (f32[12,16,128]{2,1,0:T(8,128)S(1)}, f32[12,16,128]{2,1,0:T(8,128)S(1)}, u32[]{:S(2)}, u32[]{:S(2)}) collective-permute-start(f32[12,16,128]{2,1,0:T(8,128)S(1)} %get-tuple-element.121), channel_id=1, source_target_pairs={{32,64},{64,32},{96,128},{128,96},{160,192},{192,160},{224,225},{2... | collective-permute-start | bytes 294920 | tf_op jit(solution)/shard_map/ppermute | solution.py:516
  125.2 4.7 %collective-permute-start.21 = (f32[12,16,128]{2,1,0:T(8,128)S(1)}, f32[12,16,128]{2,1,0:T(8,128)S(1)}, u32[]{:S(2)}, u32[]{:S(2)}) collective-permute-start(f32[12,16,128]{2,1,0:T(8,128)S(1)} %get-tuple-element.126), channel_id=1, source_target_pairs={{32,64},{64,32},{96,128},{128,96},{160,192},{192,160},{224,225},{2... | collective-permute-start | bytes 294920 | tf_op jit(solution)/shard_map/ppermute | solution.py:516
  126.3 5.8 %collective-permute-start.20 = (f32[12,16,128]{2,1,0:T(8,128)S(1)}, f32[12,16,128]{2,1,0:T(8,128)S(1)}, u32[]{:S(2)}, u32[]{:S(2)}) collective-permute-start(f32[12,16,128]{2,1,0:T(8,128)S(1)} %get-tuple-element.125), channel_id=1, source_target_pairs={{0,32},{32,0},{64,96},{96,64},{128,160},{160,128},{192,224},{224,1... | collective-permute-start | bytes 294920 | tf_op jit(solution)/shard_map/ppermute | solution.py:515
  152.2 5.4 %collective-permute-start.22 = (f32[4,16,128]{2,1,0:T(8,128)S(1)}, f32[4,16,128]{2,1,0:T(8,128)S(1)}, u32[]{:S(2)}, u32[]{:S(2)}) collective-permute-start(f32[4,16,128]{2,1,0:T(8,128)S(1)} %get-tuple-element.142), channel_id=1, source_target_pairs={{0,1},{1,0},{2,3},{3,2},{7,6},{6,7},{5,4},{4,5},{8,9},{9,8},{10,11... | collective-permute-start | bytes 98312 | tf_op jit(solution)/shard_map/ppermute | solution.py:541
  154.3 3.9 %collective-permute-start.23 = (f32[4,16,128]{2,1,0:T(8,128)S(1)}, f32[4,16,128]{2,1,0:T(8,128)S(1)}, u32[]{:S(2)}, u32[]{:S(2)}) collective-permute-start(f32[4,16,128]{2,1,0:T(8,128)S(1)} %get-tuple-element.143), channel_id=1, source_target_pairs={{1,2},{2,1},{3,7},{7,3},{6,5},{5,6},{4,8},{8,4},{9,10},{10,9},{11,... | collective-permute-start | bytes 98312 | tf_op jit(solution)/shard_map/ppermute | solution.py:542

commit v7 on v6

--- a/solution.py
+++ b/solution.py
@@ -254,7 +254,7 @@
 
 
 def first_kernel(
-    _, own_ref, oth_ref, a_ref, u_ref, inv2_ref, cc2_ref, inv_ref, cc_ref, sinv_ref,
+    _, own_ref, oth_ref, a_ref, u_ref, low_ref, high_ref, inv2_ref, cc2_ref, inv_ref, cc_ref, sinv_ref,
     b_ref, bb_ref, rate_ref, m_ref,
 ):
     _, core, _, sub = position()
@@ -276,6 +276,8 @@
     lax.fori_loop(0, WIDE // step, init, 0)
     double_step(0, a_ref, b_ref, bb_ref, inv_ref, cc_ref, sinv_ref, m_ref)
     u_ref[...] = a_ref[HALO : HALO + CHUNK]
+    low_ref[...] = a_ref[HALO : HALO + CHUNK // 2]
+    high_ref[...] = a_ref[HALO + CHUNK // 2 : HALO + CHUNK]
     rate = 2.0 * rate_ref[pl.ds(HALO - PIECE + PIECE * sub, 3 * PIECE)]
     inv = 1.0 / (1.0 + 6.0 * rate)
     inv2_ref[...] = inv
@@ -376,7 +378,7 @@
 
 
 def inner_kernel(
-    e_ref, cp_ref, r0_ref, r1_ref, r2_ref, r3_ref, c_ref, inv_ref, cc_ref, sinv_ref, o_ref, edge_ref,
+    e_ref, cp_low_ref, cp_high_ref, r0_ref, r1_ref, r2_ref, r3_ref, c_ref, inv_ref, cc_ref, sinv_ref, o_ref, edge_ref,
     a_ref, b_ref, bb_ref, m_ref, sems
 ):
     z, core, odd, _ = position()
@@ -384,7 +386,9 @@
     fill_mixer(m_ref)
     for n in range(NZD):
         at = n * PIECE
-        a_ref[at : at + PIECE] = cp_ref[at : at + PIECE] + e_ref[jnp.where(odd == 1, NZD - 1 - n, n)]
+        cp_ref = cp_low_ref if at < CHUNK // 2 else cp_high_ref
+        row = at % (CHUNK // 2)
+        a_ref[at : at + PIECE] = cp_ref[row : row + PIECE] + e_ref[jnp.where(odd == 1, NZD - 1 - n, n)]
 
     @pl.when(first)
     def _():
@@ -448,11 +452,11 @@
         copy.wait()
 
 
-def strips_kernel(e_ref, cp_ref, c_ref, a_ref, b_ref, head_ref, tail_ref, sems):
+def strips_kernel(e_ref, cp_low_ref, cp_high_ref, c_ref, a_ref, b_ref, head_ref, tail_ref, sems):
     z, core, odd, _ = position()
     low, high = odd * (NZD - 1), (1 - odd) * (NZD - 1)
-    head_ref[...] = cp_ref[:STRIP] + e_ref[low, :STRIP]
-    tail_ref[...] = cp_ref[CHUNK - STRIP :] + e_ref[high, STRIP:]
+    head_ref[...] = cp_low_ref[:STRIP] + e_ref[low, :STRIP]
+    tail_ref[...] = cp_high_ref[CHUNK // 2 - STRIP :] + e_ref[high, STRIP:]
 
     @pl.when((z == 0) & (core == 0))
     def _():
@@ -489,9 +493,10 @@
     oth = swap(own)
     state, c = call(state_kernel, [wide, whole], [VMEM])(got)
 
-    ahead, u, inv2, cc2, inv, cc, sinv = call(
+    half = (CHUNK // 2,) + plane
+    ahead, u, u_low, u_high, inv2, cc2, inv, cc, sinv = call(
         first_kernel,
-        [wide, whole] + [(3 * PIECE,) + plane] * 2 + [wide] * 3,
+        [wide, whole, half, half] + [(3 * PIECE,) + plane] * 2 + [wide] * 3,
         [VMEM] * 3,
         [wide] * 3,
         mixer=True,
@@ -507,7 +512,7 @@
         residual_kernel, [(NT,) + piece, message, message], [VMEM] * 2
     )(mine, other)
     pairs_a, pairs_b = piece_pairs(0), piece_pairs(1)
-    beside = [(u, 1)] + [(part, 2) for part in r_parts]
+    beside = [(u_low, 1)] + [(part, 2) for part in r_parts] + [(u_high, 1)]
     moved = []
     errors = [res[1]]
     for turn in range(7):
@@ -526,7 +531,7 @@
         errors += [e1, e2]
         if turn > 0 and turn <= len(beside):
             ma, moved[turn - 1] = lax.optimization_barrier((ma, moved[turn - 1]))
-    cpoint, *r_parts = moved
+    cp_low, *r_parts, cp_high = moved
     errors = call(
         functools.partial(chain_end_kernel, NT - 3),
         [(NZD,) + piece],
@@ -535,19 +540,19 @@
 
     chunk = lax.all_to_all(errors, "z", 0, 0)
     edge = (STRIP,) + plane
-    ma, mb = call(strips_kernel, [edge] * 2, [VMEM] * 2 + [anywhere], [edge] * 2, sems=((2,),))(
-        chunk, cpoint, c
+    ma, mb = call(strips_kernel, [edge] * 2, [VMEM] * 3 + [anywhere], [edge] * 2, sems=((2,),))(
+        chunk, cp_low, cp_high, c
     )
     ra = lax.ppermute(ma, "space", chunk_pairs(0))
     rb = lax.ppermute(mb, "space", chunk_pairs(1))
     sent, edges_in = call(
         inner_kernel,
         [(NSP * 3 * CHUNK, LANES), (2, 2 * STRIP) + plane],
-        [VMEM] * 6 + [anywhere] + [VMEM] * 3,
+        [VMEM] * 7 + [anywhere] + [VMEM] * 3,
         [whole] * 3,
         mixer=True,
         sems=((1,),),
-    )(chunk, cpoint, *r_parts, c, inv, cc, sinv)
+    )(chunk, cp_low, cp_high, *r_parts, c, inv, cc, sinv)
     sent = call(outer_kernel, [(NSP * 3 * CHUNK, LANES)], [VMEM] * 7, aliases={0: 0})(
         sent, edges_in, ra, rb, inv, cc, sinv
     )[0]

time: 182 us -> 186 us (1.022)
  blocking collectives: 90.1 us -> 71.3 us
  waiting for transfers between devices: 30.6 us -> 46.9 us
  local copies, waits for them, and re-layouts: 0.01 us -> 3.58 us
  starting transfers between devices: 33.7 us -> 36.7 us
    all_to_all x1 -> x0, blocking collectives: 19.1 us -> none  [body(): chunk = lax.all_to_all(errors, 'z', 0, 0)]
    ppermute x5 -> x6, waiting for transfers between devices: 0.01 us -> 12.2 us  [body(): moved.append(lax.ppermute(part, everyone, interval_shift(step)))]
    all_to_all x0 -> x1, starting transfers between devices: none -> 6.03 us  [body(): chunk = lax.all_to_all(errors, 'z', 0, 0)]
    unnamed x0 -> x24, local copies, waits for them, and re-layouts: none -> 3.58 us
    all_to_all x0 -> x1, waiting for transfers between devices: none -> 3.24 us  [body(): chunk = lax.all_to_all(errors, 'z', 0, 0)]
    ppermute x5 -> x6, starting transfers between devices: 7.36 us -> 7.1 us  [body(): moved.append(lax.ppermute(part, everyone, interval_shift(step)))]
  transfers between devices with their start and end apart: 24 -> 26, of which waited for: 18 -> 21; matrix products, arithmetic and copies ran while one was open for 0% -> 0% of each run, Pallas kernels for 9% -> 8%
where the time goes in v7:
time: 186 us
  blocking collectives  71.3 us (38%)
  waiting for transfers between devices  46.9 us (25%)
  starting transfers between devices  36.7 us (20%)
  Pallas kernels  26.1 us (14%)
  local copies, waits for them, and re-layouts  3.58 us (2%)
    all_to_all x1, blocking collectives, body(): got = lax.all_to_all(sent, 'space', 0, 0).reshape(-1, LANES)  28.4 us
    all_to_all x1, blocking collectives, body(): mine = lax.all_to_all(r, 'z', 0, 0)  21.7 us
    all_to_all x1, blocking collectives, body(): got = lax.all_to_all(sent.reshape(NSP, 3 * CHUNK, LANES), 'space', 0, 0)  21.1 us
    ppermute x7, waiting for transfers between devices, body(): ra = lax.ppermute(ma, everyone, pairs_a)  17.2 us
    ppermute x6, waiting for transfers between devices, body(): moved.append(lax.ppermute(part, everyone, interval_shift(step)))  12.2 us
    ppermute x7, starting transfers between devices, body(): ra = lax.ppermute(ma, everyone, pairs_a)  9.4 us
    pallas_call x6, Pallas kernels, body(): call(functools.partial(chain_kernel, t), [piece, piece, message, message]...  8.76 us
    ppermute x7, starting transfers between devices, body(): rb = lax.ppermute(mb, everyone, pairs_b)  7.62 us
  transfers between devices with their start and end apart: 26, of which 21 were waited for; matrix products, arithmetic and copies ran while one was open for 0% of the time, Pallas kernels for 8%

profile of v7, /device:TPU:8, one launch (start us, length us, event | category | flops | bytes accessed | tf_op | source)
XLA Modules:
  0.0 185.6 jit_solution(16978501475534249730)
XLA Ops:
  0.6 2.8 %shard_map.50 = f32[16,192,128]{2,1,0:T(8,128)} custom-call(f32[128,1024]{1,0:T(8,128)} %bitcast.12, f32[128,1024]{1,0:T(8,128)} %bitcast.13, f32[128,1024]{1,0:T(8,128)} %bitcast.14), custom_call_target="tpu_custom_call" | custom-call | tf_op jit(solution)/shard_map/pallas_call | solution.py:487
  3.4 28.4 %all_to_all.20 = f32[16,192,128]{2,1,0:T(8,128)S(1)} all-to-all(f32[16,192,128]{2,1,0:T(8,128)} %shard_map.50), channel_id=1, replica_groups=mesh['z'=8,'core'=2,'space'=16] {'space'}, dimensions={0} | all-to-all | bytes 3145728 | tf_op jit(solution)/shard_map/all_to_all | solution.py:490
  33.0 1.7 collective-permute-done.oth_ref
  34.7 4.0 %shard_map.53 = (f32[96,16,128]{2,1,0:T(8,128)S(1)}, f32[64,16,128]{2,1,0:T(8,128)S(1)}, f32[32,16,128]{2,1,0:T(8,128)S(1)}, f32[32,16,128]{2,1,0:T(8,128)S(1)},...) custom-call(f32[96,16,128]{2,1,0:T(8,128)S(1)} %get-tuple-element.79, ...), custom_call_target="tpu_custom_call", output_to_operand_aliasing={{0}: (0, {})} | custom-call | tf_op jit(solution)/shard_map/pallas_call | solution.py:497
  38.7 5.6 %collective-permute-start.1 = (f32[64,16,128]{2,1,0:T(8,128)S(1)}, f32[64,16,128]{2,1,0:T(8,128)S(1)}, u32[]{:S(2)}, u32[]{:S(2)}) collective-permute-start(f32[64,16,128]{2,1,0:T(8,128)S(1)} %get-tuple-element.84), channel_id=1, source_target_pairs={{0,240},{1,241},{2,242},{3,243},{4,244},{5,245},{6,246},{7,247},{8... | collective-permute-start | bytes 1572872 | tf_op jit(solution)/shard_map/ppermute | solution.py:505
  44.3 3.3 %shard_map.54.w_ref = f32[64,16,128]{2,1,0:T(8,128)S(1)} custom-call(f32[96,16,128]{2,1,0:T(8,128)S(1)} %get-tuple-element.80.u_ref, f32[96,16,128]{2,1,0:T(8,128)S(1)} %get-tuple-element.81.inv_ref, f32[96,16,128]{2,1,0:T(8,128)S(1)} %get-tuple-element.82.cc_ref, f32[96,16,128]{2,1,0:T(8,128)S(1)} %get-tuple-element.83.sinv_ref), custom_call_target="tpu_custom_call" | custom-call | tf_op jit(solution)/shard_map/pallas_call | solution.py:506
  47.7 3.4 %collective-permute-done.1.next_ref = f32[64,16,128]{2,1,0:T(8,128)S(1)} collective-permute-done((f32[64,16,128]{2,1,0:T(8,128)S(1)}, f32[64,16,128]{2,1,0:T(8,128)S(1)}, u32[]{:S(2)}, u32[]{:S(2)}) %collective-permute-start.1) | collective-permute-done | bytes 524320 | tf_op jit(solution)/shard_map/ppermute | solution.py:505
  51.1 21.7 %all_to_all.21.own_ref = f32[8,8,16,128]{3,2,1,0:T(8,128)S(1)} all-to-all(f32[8,8,16,128]{3,2,1,0:T(8,128)S(1)} %get-tuple-element.85), channel_id=1, replica_groups=mesh['z'=8,'core'=2,'space'=16] {'z'}, dimensions={0} | all-to-all | bytes 1048576 | tf_op jit(solution)/shard_map/all_to_all | solution.py:509
  73.0 1.8 collective-permute-done.2.oth_ref
  75.1 1.2 collective-permute-start.4
  76.3 3.5 %collective-permute-done.3.ra_ref = f32[12,16,128]{2,1,0:T(8,128)S(1)} collective-permute-done((f32[12,16,128]{2,1,0:T(8,128)S(1)}, f32[12,16,128]{2,1,0:T(8,128)S(1)}, u32[]{:S(2)}, u32[]{:S(2)}) %collective-permute-start.3) | collective-permute-done | bytes 98336 | tf_op jit(solution)/shard_map/ppermute | solution.py:520
  80.1 1.5 shard_map.57
  81.5 1.6 collective-permute-start.5
  83.2 1.0 collective-permute-start.6
  84.2 2.5 %collective-permute-done.5.ra_ref = f32[12,16,128]{2,1,0:T(8,128)S(1)} collective-permute-done((f32[12,16,128]{2,1,0:T(8,128)S(1)}, f32[12,16,128]{2,1,0:T(8,128)S(1)}, u32[]{:S(2)}, u32[]{:S(2)}) %collective-permute-start.5) | collective-permute-done | bytes 98336 | tf_op jit(solution)/shard_map/ppermute | solution.py:520
  86.7 1.4 collective-permute-done.6.rb_ref
  88.1 1.0 collective-permute-start.10
  89.0 1.5 shard_map.58
  90.5 1.1 collective-permute-start.9
  91.6 1.9 %collective-permute-start.8 = (f32[12,16,128]{2,1,0:T(8,128)S(1)}, f32[12,16,128]{2,1,0:T(8,128)S(1)}, u32[]{:S(2)}, u32[]{:S(2)}) collective-permute-start(f32[12,16,128]{2,1,0:T(8,128)S(1)} %get-tuple-element.102), channel_id=1, source_target_pairs={{0,32},{32,0},{64,96},{96,64},{128,160},{160,128},{192,224},{224,1... | collective-permute-start | bytes 294920 | tf_op jit(solution)/shard_map/ppermute | solution.py:520
  93.6 1.7 collective-permute-done.9.rb_ref
  95.3 1.0 collective-permute-done.8.ra_ref
  96.3 1.9 %collective-permute-start.13 = (f32[2,8,16,128]{3,2,1,0:T(8,128)S(1)}, f32[2,8,16,128]{3,2,1,0:T(8,128)S(1)}, u32[]{:S(2)}, u32[]{:S(2)}) collective-permute-start(f32[2,8,16,128]{3,2,1,0:T(8,128)S(1)} %get-tuple-element.117), channel_id=1, source_target_pairs={{0,32},{1,33},{2,34},{3,35},{4,36},{5,37},{6,38},{7,39},{8,40},{9,... | collective-permute-start | bytes 393224 | tf_op jit(solution)/shard_map/ppermute | solution.py:525
  98.2 1.5 shard_map.59
  100.1 1.0 collective-permute-start.12
  101.2 3.2 %collective-permute-done.11.ra_ref = f32[12,16,128]{2,1,0:T(8,128)S(1)} collective-permute-done((f32[12,16,128]{2,1,0:T(8,128)S(1)}, f32[12,16,128]{2,1,0:T(8,128)S(1)}, u32[]{:S(2)}, u32[]{:S(2)}) %collective-permute-start.11) | collective-permute-done | bytes 98336 | tf_op jit(solution)/shard_map/ppermute | solution.py:520
  104.7 1.7 collective-permute-start.16
  106.5 1.5 shard_map.60
  107.9 1.1 collective-permute-start.15
  109.1 2.3 %collective-permute-start.14 = (f32[12,16,128]{2,1,0:T(8,128)S(1)}, f32[12,16,128]{2,1,0:T(8,128)S(1)}, u32[]{:S(2)}, u32[]{:S(2)}) collective-permute-start(f32[12,16,128]{2,1,0:T(8,128)S(1)} %get-tuple-element.118), channel_id=1, source_target_pairs={{0,32},{32,0},{64,96},{96,64},{128,160},{160,128},{192,224},{224,1... | collective-permute-start | bytes 294920 | tf_op jit(solution)/shard_map/ppermute | solution.py:520
  111.4 1.3 collective-permute-done.15.rb_ref
  112.6 1.9 %collective-permute-done.14.ra_ref = f32[12,16,128]{2,1,0:T(8,128)S(1)} collective-permute-done((f32[12,16,128]{2,1,0:T(8,128)S(1)}, f32[12,16,128]{2,1,0:T(8,128)S(1)}, u32[]{:S(2)}, u32[]{:S(2)}) %collective-permute-start.14) | collective-permute-done | bytes 98336 | tf_op jit(solution)/shard_map/ppermute | solution.py:520
  114.6 2.5 %collective-permute-start.19 = (f32[2,8,16,128]{3,2,1,0:T(8,128)S(1)}, f32[2,8,16,128]{3,2,1,0:T(8,128)S(1)}, u32[]{:S(2)}, u32[]{:S(2)}) collective-permute-start(f32[2,8,16,128]{3,2,1,0:T(8,128)S(1)} %get-tuple-element.133), channel_id=1, source_target_pairs={{0,32},{1,33},{2,34},{3,35},{4,36},{5,37},{6,38},{7,39},{8,40},{9,... | collective-permute-start | bytes 393224 | tf_op jit(solution)/shard_map/ppermute | solution.py:525
  117.0 1.5 shard_map.61
  118.6 1.1 collective-permute-start.18
  119.8 3.5 %collective-permute-done.17.ra_ref = f32[12,16,128]{2,1,0:T(8,128)S(1)} collective-permute-done((f32[12,16,128]{2,1,0:T(8,128)S(1)}, f32[12,16,128]{2,1,0:T(8,128)S(1)}, u32[]{:S(2)}, u32[]{:S(2)}) %collective-permute-start.17) | collective-permute-done | bytes 98336 | tf_op jit(solution)/shard_map/ppermute | solution.py:520
  123.9 1.5 shard_map.62
  125.3 1.0 collective-permute-start.21
  126.3 2.8 %collective-permute-start.20 = (f32[12,16,128]{2,1,0:T(8,128)S(1)}, f32[12,16,128]{2,1,0:T(8,128)S(1)}, u32[]{:S(2)}, u32[]{:S(2)}) collective-permute-start(f32[12,16,128]{2,1,0:T(8,128)S(1)} %get-tuple-element.134), channel_id=1, source_target_pairs={{0,32},{32,0},{64,96},{96,64},{128,160},{160,128},{192,224},{224,1... | collective-permute-start | bytes 294920 | tf_op jit(solution)/shard_map/ppermute | solution.py:520
  130.1 1.6 collective-permute-done.20.ra_ref
  133.4 6.0 %all-to-all-start.2 = ((f32[8,8,16,128]{3,2,1,0:T(8,128)}), f32[8,8,16,128]{3,2,1,0:T(8,128)S(1)}, u32[]{:S(2)}, u32[]{:S(2)}) async-start(f32[8,8,16,128]{3,2,1,0:T(8,128)} %copy-done), calls=%async_computation.2 | async-start | bytes 1048576 | tf_op jit(solution)/shard_map/all_to_all | solution.py:541
  139.5 12.2 %collective-permute-done.22.cp_high_ref = f32[32,16,128]{2,1,0:T(8,128)S(1)} collective-permute-done((f32[32,16,128]{2,1,0:T(8,128)}, f32[32,16,128]{2,1,0:T(8,128)S(1)}, u32[]{:S(2)}, u32[]{:S(2)}) %collective-permute-start.22) | collective-permute-done | bytes 262176 | tf_op jit(solution)/shard_map/ppermute | solution.py:525
  152.3 3.2 %all-to-all-done.2.e_ref = f32[8,8,16,128]{3,2,1,0:T(8,128)S(1)} async-done(((f32[8,8,16,128]{3,2,1,0:T(8,128)}), f32[8,8,16,128]{3,2,1,0:T(8,128)S(1)}, u32[]{:S(2)}, u32[]{:S(2)}) %all-to-all-start.2) | async-done | bytes 524320 | tf_op jit(solution)/shard_map/all_to_all | solution.py:541
  155.5 0.9 copy-done.2
  156.5 0.9 copy-done.4
  158.5 2.9 %shard_map.64 = (f32[3072,128]{1,0:T(8,128)S(1)}, f32[2,8,16,128]{3,2,1,0:T(8,128)S(1)}) custom-call(f32[8,8,16,128]{3,2,1,0:T(8,128)S(1)} %all-to-all-done.2.e_ref, f32[32,16,128]{2,1,0:T(8,128)S(1)} %copy-done.2, f32[32,16,128]{2,1,0:T(8,128)S(1)} %copy-done.4, f32[2,8,16,128]{3,2,1,0:T(8,128)S(1)} %collective-permute-done.10.r0_ref, ...), custom_call_target="tpu_custom_call" | custom-call | tf_op jit(solution)/shard_map/pallas_call | solution.py:548
  162.9 21.1 %all_to_all.22.a_ref = f32[16,192,128]{2,1,0:T(8,128)S(1)} all-to-all(f32[16,192,128]{2,1,0:T(8,128)S(1)} %bitcast.11), channel_id=1, replica_groups=mesh['z'=8,'core'=2,'space'=16] {'space'}, dimensions={0} | all-to-all | bytes 3145728 | tf_op jit(solution)/shard_map/all_to_all | solution.py:559
  184.0 1.4 shard_map.67
  (50 shorter events, 9.4 us)
Async XLA Ops:
  32.3 2.4 %collective-permute-start = (f32[96,16,128]{2,1,0:T(8,128)S(1)}, f32[96,16,128]{2,1,0:T(8,128)S(1)}, u32[]{:S(2)}, u32[]{:S(2)}) collective-permute-start(f32[96,16,128]{2,1,0:T(8,128)S(1)} %shard_map.52.own_ref), channel_id=1, source_target_pairs={{0,16},{16,0},{1,17},{17,1},{2,18},{18,2},{3,19},{19,3},{4,20},{20... | collective-permute-start | bytes 2359304 | tf_op jit(solution)/shard_map/ppermute | solution.py:485
  38.7 51.8 %copy-start.11 = (f32[32,16,128]{2,1,0:T(8,128)}, f32[32,16,128]{2,1,0:T(8,128)S(1)}, u32[]{:S(2)}) copy-start(f32[32,16,128]{2,1,0:T(8,128)S(1)} %get-tuple-element.144) | copy-start | bytes 786436
  38.7 12.3 %collective-permute-start.1 = (f32[64,16,128]{2,1,0:T(8,128)S(1)}, f32[64,16,128]{2,1,0:T(8,128)S(1)}, u32[]{:S(2)}, u32[]{:S(2)}) collective-permute-start(f32[64,16,128]{2,1,0:T(8,128)S(1)} %get-tuple-element.84), channel_id=1, source_target_pairs={{0,240},{1,241},{2,242},{3,243},{4,244},{5,245},{6,246},{7,247},{8... | collective-permute-start | bytes 1572872 | tf_op jit(solution)/shard_map/ppermute | solution.py:505
  72.8 1.9 %collective-permute-start.2 = (f32[8,8,16,128]{3,2,1,0:T(8,128)S(1)}, f32[8,8,16,128]{3,2,1,0:T(8,128)S(1)}, u32[]{:S(2)}, u32[]{:S(2)}) collective-permute-start(f32[8,8,16,128]{3,2,1,0:T(8,128)S(1)} %all_to_all.21.own_ref), channel_id=1, source_target_pairs={{0,16},{16,0},{1,17},{17,1},{2,18},{18,2},{3,19},{19,3},{4,20},{20... | collective-permute-start | bytes 1572872 | tf_op jit(solution)/shard_map/ppermute | solution.py:485
  74.9 4.9 %collective-permute-start.3 = (f32[12,16,128]{2,1,0:T(8,128)S(1)}, f32[12,16,128]{2,1,0:T(8,128)S(1)}, u32[]{:S(2)}, u32[]{:S(2)}) collective-permute-start(f32[12,16,128]{2,1,0:T(8,128)S(1)} %get-tuple-element.86), channel_id=1, source_target_pairs={{0,32},{32,0},{64,96},{96,64},{128,160},{160,128},{192,224},{224,1... | collective-permute-start | bytes 294920 | tf_op jit(solution)/shard_map/ppermute | solution.py:520
  75.1 4.9 %collective-permute-start.4 = (f32[12,16,128]{2,1,0:T(8,128)S(1)}, f32[12,16,128]{2,1,0:T(8,128)S(1)}, u32[]{:S(2)}, u32[]{:S(2)}) collective-permute-start(f32[12,16,128]{2,1,0:T(8,128)S(1)} %get-tuple-element.87), channel_id=1, source_target_pairs={{32,64},{64,32},{96,128},{128,96},{160,192},{192,160},{224,225},{2... | collective-permute-start | bytes 294920 | tf_op jit(solution)/shard_map/ppermute | solution.py:521
  80.1 11.6 %collective-permute-start.7 = (f32[32,16,128]{2,1,0:T(8,128)S(1)}, f32[32,16,128]{2,1,0:T(8,128)S(1)}, u32[]{:S(2)}, u32[]{:S(2)}) collective-permute-start(f32[32,16,128]{2,1,0:T(8,128)S(1)} %get-tuple-element.101), channel_id=1, source_target_pairs={{0,16},{1,17},{2,18},{3,19},{4,20},{5,21},{6,22},{7,23},{8,24},{9,... | collective-permute-start | bytes 786440 | tf_op jit(solution)/shard_map/ppermute | solution.py:525
  81.5 5.1 %collective-permute-start.5 = (f32[12,16,128]{2,1,0:T(8,128)S(1)}, f32[12,16,128]{2,1,0:T(8,128)S(1)}, u32[]{:S(2)}, u32[]{:S(2)}) collective-permute-start(f32[12,16,128]{2,1,0:T(8,128)S(1)} %get-tuple-element.94), channel_id=1, source_target_pairs={{0,32},{32,0},{64,96},{96,64},{128,160},{160,128},{192,224},{224,1... | collective-permute-start | bytes 294920 | tf_op jit(solution)/shard_map/ppermute | solution.py:520
  83.2 4.9 %collective-permute-start.6 = (f32[12,16,128]{2,1,0:T(8,128)S(1)}, f32[12,16,128]{2,1,0:T(8,128)S(1)}, u32[]{:S(2)}, u32[]{:S(2)}) collective-permute-start(f32[12,16,128]{2,1,0:T(8,128)S(1)} %get-tuple-element.95), channel_id=1, source_target_pairs={{32,64},{64,32},{96,128},{128,96},{160,192},{192,160},{224,225},{2... | collective-permute-start | bytes 294920 | tf_op jit(solution)/shard_map/ppermute | solution.py:521
  88.1 11.6 %collective-permute-start.10 = (f32[2,8,16,128]{3,2,1,0:T(8,128)S(1)}, f32[2,8,16,128]{3,2,1,0:T(8,128)S(1)}, u32[]{:S(2)}, u32[]{:S(2)}) collective-permute-start(f32[2,8,16,128]{3,2,1,0:T(8,128)S(1)} %get-tuple-element.109), channel_id=1, source_target_pairs={{0,32},{1,33},{2,34},{3,35},{4,36},{5,37},{6,38},{7,39},{8,40},{9,... | collective-permute-start | bytes 393224 | tf_op jit(solution)/shard_map/ppermute | solution.py:525
  90.5 4.8 %collective-permute-start.9 = (f32[12,16,128]{2,1,0:T(8,128)S(1)}, f32[12,16,128]{2,1,0:T(8,128)S(1)}, u32[]{:S(2)}, u32[]{:S(2)}) collective-permute-start(f32[12,16,128]{2,1,0:T(8,128)S(1)} %get-tuple-element.103), channel_id=1, source_target_pairs={{32,64},{64,32},{96,128},{128,96},{160,192},{192,160},{224,225},{2... | collective-permute-start | bytes 294920 | tf_op jit(solution)/shard_map/ppermute | solution.py:521
  91.6 16.3 %copy-start.1 = (f32[32,16,128]{2,1,0:T(8,128)}, f32[32,16,128]{2,1,0:T(8,128)S(1)}, u32[]{:S(2)}) copy-start(f32[32,16,128]{2,1,0:T(8,128)S(1)} %collective-permute-done.7.cp_low_ref) | copy-start | bytes 786436
  91.6 4.6 %collective-permute-start.8 = (f32[12,16,128]{2,1,0:T(8,128)S(1)}, f32[12,16,128]{2,1,0:T(8,128)S(1)}, u32[]{:S(2)}, u32[]{:S(2)}) collective-permute-start(f32[12,16,128]{2,1,0:T(8,128)S(1)} %get-tuple-element.102), channel_id=1, source_target_pairs={{0,32},{32,0},{64,96},{96,64},{128,160},{160,128},{192,224},{224,1... | collective-permute-start | bytes 294920 | tf_op jit(solution)/shard_map/ppermute | solution.py:520
  96.3 12.8 %collective-permute-start.13 = (f32[2,8,16,128]{3,2,1,0:T(8,128)S(1)}, f32[2,8,16,128]{3,2,1,0:T(8,128)S(1)}, u32[]{:S(2)}, u32[]{:S(2)}) collective-permute-start(f32[2,8,16,128]{3,2,1,0:T(8,128)S(1)} %get-tuple-element.117), channel_id=1, source_target_pairs={{0,32},{1,33},{2,34},{3,35},{4,36},{5,37},{6,38},{7,39},{8,40},{9,... | collective-permute-start | bytes 393224 | tf_op jit(solution)/shard_map/ppermute | solution.py:525
  99.7 4.7 %collective-permute-start.11 = (f32[12,16,128]{2,1,0:T(8,128)S(1)}, f32[12,16,128]{2,1,0:T(8,128)S(1)}, u32[]{:S(2)}, u32[]{:S(2)}) collective-permute-start(f32[12,16,128]{2,1,0:T(8,128)S(1)} %get-tuple-element.110), channel_id=1, source_target_pairs={{0,32},{32,0},{64,96},{96,64},{128,160},{160,128},{192,224},{224,1... | collective-permute-start | bytes 294920 | tf_op jit(solution)/shard_map/ppermute | solution.py:520
  100.1 4.6 %collective-permute-start.12 = (f32[12,16,128]{2,1,0:T(8,128)S(1)}, f32[12,16,128]{2,1,0:T(8,128)S(1)}, u32[]{:S(2)}, u32[]{:S(2)}) collective-permute-start(f32[12,16,128]{2,1,0:T(8,128)S(1)} %get-tuple-element.111), channel_id=1, source_target_pairs={{32,64},{64,32},{96,128},{128,96},{160,192},{192,160},{224,225},{2... | collective-permute-start | bytes 294920 | tf_op jit(solution)/shard_map/ppermute | solution.py:521
  104.7 13.8 %collective-permute-start.16 = (f32[2,8,16,128]{3,2,1,0:T(8,128)S(1)}, f32[2,8,16,128]{3,2,1,0:T(8,128)S(1)}, u32[]{:S(2)}, u32[]{:S(2)}) collective-permute-start(f32[2,8,16,128]{3,2,1,0:T(8,128)S(1)} %get-tuple-element.125), channel_id=1, source_target_pairs={{0,32},{1,33},{2,34},{3,35},{4,36},{5,37},{6,38},{7,39},{8,40},{9,... | collective-permute-start | bytes 393224 | tf_op jit(solution)/shard_map/ppermute | solution.py:525
  107.9 4.7 %collective-permute-start.15 = (f32[12,16,128]{2,1,0:T(8,128)S(1)}, f32[12,16,128]{2,1,0:T(8,128)S(1)}, u32[]{:S(2)}, u32[]{:S(2)}) collective-permute-start(f32[12,16,128]{2,1,0:T(8,128)S(1)} %get-tuple-element.119), channel_id=1, source_target_pairs={{32,64},{64,32},{96,128},{128,96},{160,192},{192,160},{224,225},{2... | collective-permute-start | bytes 294920 | tf_op jit(solution)/shard_map/ppermute | solution.py:521
  109.1 16.3 %copy-start.5 = (f32[2,8,16,128]{3,2,1,0:T(8,128)}, f32[2,8,16,128]{3,2,1,0:T(8,128)S(1)}, u32[]{:S(2)}) copy-start(f32[2,8,16,128]{3,2,1,0:T(8,128)S(1)} %collective-permute-done.13.r1_ref) | copy-start | bytes 393220
  109.1 5.5 %collective-permute-start.14 = (f32[12,16,128]{2,1,0:T(8,128)S(1)}, f32[12,16,128]{2,1,0:T(8,128)S(1)}, u32[]{:S(2)}, u32[]{:S(2)}) collective-permute-start(f32[12,16,128]{2,1,0:T(8,128)S(1)} %get-tuple-element.118), channel_id=1, source_target_pairs={{0,32},{32,0},{64,96},{96,64},{128,160},{160,128},{192,224},{224,1... | collective-permute-start | bytes 294920 | tf_op jit(solution)/shard_map/ppermute | solution.py:520
  114.6 11.8 %collective-permute-start.19 = (f32[2,8,16,128]{3,2,1,0:T(8,128)S(1)}, f32[2,8,16,128]{3,2,1,0:T(8,128)S(1)}, u32[]{:S(2)}, u32[]{:S(2)}) collective-permute-start(f32[2,8,16,128]{3,2,1,0:T(8,128)S(1)} %get-tuple-element.133), channel_id=1, source_target_pairs={{0,32},{1,33},{2,34},{3,35},{4,36},{5,37},{6,38},{7,39},{8,40},{9,... | collective-permute-start | bytes 393224 | tf_op jit(solution)/shard_map/ppermute | solution.py:525
  118.5 13.2 %copy-start.7 = (f32[2,8,16,128]{3,2,1,0:T(8,128)}, f32[2,8,16,128]{3,2,1,0:T(8,128)S(1)}, u32[]{:S(2)}) copy-start(f32[2,8,16,128]{3,2,1,0:T(8,128)S(1)} %collective-permute-done.16.r2_ref) | copy-start | bytes 393220
  118.5 4.7 %collective-permute-start.17 = (f32[12,16,128]{2,1,0:T(8,128)S(1)}, f32[12,16,128]{2,1,0:T(8,128)S(1)}, u32[]{:S(2)}, u32[]{:S(2)}) collective-permute-start(f32[12,16,128]{2,1,0:T(8,128)S(1)} %get-tuple-element.126), channel_id=1, source_target_pairs={{0,32},{32,0},{64,96},{96,64},{128,160},{160,128},{192,224},{224,1... | collective-permute-start | bytes 294920 | tf_op jit(solution)/shard_map/ppermute | solution.py:520
  118.6 5.2 %collective-permute-start.18 = (f32[12,16,128]{2,1,0:T(8,128)S(1)}, f32[12,16,128]{2,1,0:T(8,128)S(1)}, u32[]{:S(2)}, u32[]{:S(2)}) collective-permute-start(f32[12,16,128]{2,1,0:T(8,128)S(1)} %get-tuple-element.127), channel_id=1, source_target_pairs={{32,64},{64,32},{96,128},{128,96},{160,192},{192,160},{224,225},{2... | collective-permute-start | bytes 294920 | tf_op jit(solution)/shard_map/ppermute | solution.py:521
  125.3 4.7 %collective-permute-start.21 = (f32[12,16,128]{2,1,0:T(8,128)S(1)}, f32[12,16,128]{2,1,0:T(8,128)S(1)}, u32[]{:S(2)}, u32[]{:S(2)}) collective-permute-start(f32[12,16,128]{2,1,0:T(8,128)S(1)} %get-tuple-element.135), channel_id=1, source_target_pairs={{32,64},{64,32},{96,128},{128,96},{160,192},{192,160},{224,225},{2... | collective-permute-start | bytes 294920 | tf_op jit(solution)/shard_map/ppermute | solution.py:521
  126.3 7.1 %copy-start.9 = (f32[2,8,16,128]{3,2,1,0:T(8,128)}, f32[2,8,16,128]{3,2,1,0:T(8,128)S(1)}, u32[]{:S(2)}) copy-start(f32[2,8,16,128]{3,2,1,0:T(8,128)S(1)} %collective-permute-done.19.r3_ref) | copy-start | bytes 393220
  126.3 5.3 %collective-permute-start.20 = (f32[12,16,128]{2,1,0:T(8,128)S(1)}, f32[12,16,128]{2,1,0:T(8,128)S(1)}, u32[]{:S(2)}, u32[]{:S(2)}) collective-permute-start(f32[12,16,128]{2,1,0:T(8,128)S(1)} %get-tuple-element.134), channel_id=1, source_target_pairs={{0,32},{32,0},{64,96},{96,64},{128,160},{160,128},{192,224},{224,1... | collective-permute-start | bytes 294920 | tf_op jit(solution)/shard_map/ppermute | solution.py:520
  132.6 0.8 copy-start
  133.4 22.1 %all-to-all-start.2 = ((f32[8,8,16,128]{3,2,1,0:T(8,128)}), f32[8,8,16,128]{3,2,1,0:T(8,128)S(1)}, u32[]{:S(2)}, u32[]{:S(2)}) async-start(f32[8,8,16,128]{3,2,1,0:T(8,128)} %copy-done), calls=%async_computation.2 | async-start | bytes 1048576 | tf_op jit(solution)/shard_map/all_to_all | solution.py:541
  139.4 12.2 %collective-permute-start.22 = (f32[32,16,128]{2,1,0:T(8,128)}, f32[32,16,128]{2,1,0:T(8,128)S(1)}, u32[]{:S(2)}, u32[]{:S(2)}) collective-permute-start(f32[32,16,128]{2,1,0:T(8,128)} %copy-done.11), channel_id=1, source_target_pairs={{0,16},{1,17},{2,18},{3,19},{4,20},{5,21},{6,22},{7,23},{8,24},{9,... | collective-permute-start | bytes 786440 | tf_op jit(solution)/shard_map/ppermute | solution.py:525
  151.6 0.7 copy-start.3
  155.5 1.0 copy-start.2
  156.5 0.9 copy-start.4
  157.4 0.9 copy-start.6
  157.4 1.0 copy-start.8
  157.4 1.0 copy-start.10
  157.6 4.0 %collective-permute-start.23 = (f32[4,16,128]{2,1,0:T(8,128)S(1)}, f32[4,16,128]{2,1,0:T(8,128)S(1)}, u32[]{:S(2)}, u32[]{:S(2)}) collective-permute-start(f32[4,16,128]{2,1,0:T(8,128)S(1)} %get-tuple-element.152), channel_id=1, source_target_pairs={{0,1},{1,0},{2,3},{3,2},{7,6},{6,7},{5,4},{4,5},{8,9},{9,8},{10,11... | collective-permute-start | bytes 98312 | tf_op jit(solution)/shard_map/ppermute | solution.py:546
  158.2 3.9 %collective-permute-start.24 = (f32[4,16,128]{2,1,0:T(8,128)S(1)}, f32[4,16,128]{2,1,0:T(8,128)S(1)}, u32[]{:S(2)}, u32[]{:S(2)}) collective-permute-start(f32[4,16,128]{2,1,0:T(8,128)S(1)} %get-tuple-element.153), channel_id=1, source_target_pairs={{1,2},{2,1},{3,7},{7,3},{6,5},{5,6},{4,8},{8,4},{9,10},{10,9},{11,... | collective-permute-start | bytes 98312 | tf_op jit(solution)/shard_map/ppermute | solution.py:547

commit v8 on v7

--- a/solution.py
+++ b/solution.py
@@ -524,6 +524,7 @@
             ra, rb, part = lax.optimization_barrier((ra, rb, part))
             moved.append(lax.ppermute(part, everyone, interval_shift(step)))
         if turn == 6:
+            ra, moved[-1] = lax.optimization_barrier((ra, moved[-1]))
             break
         e1, e2, ma, mb = call(
             functools.partial(chain_kernel, t), [piece, piece, message, message], [VMEM] * 6

time: 186 us -> 195 us (1.048)
  blocking collectives: 71.3 us -> 103 us
  waiting for transfers between devices: 46.9 us -> 36.4 us
  starting transfers between devices: 36.7 us -> 28.6 us
  local copies, waits for them, and re-layouts: 3.58 us -> 0.01 us
    all_to_all x0 -> x1, blocking collectives: none -> 26 us  [body(): chunk = lax.all_to_all(errors, 'z', 0, 0)]
    ppermute x6, waiting for transfers between devices: 12.2 us -> 4.9 us  [body(): moved.append(lax.ppermute(part, everyone, interval_shift(step)))]
    all_to_all x1 -> x0, starting transfers between devices: 6.03 us -> none  [body(): chunk = lax.all_to_all(errors, 'z', 0, 0)]
    all_to_all x1, blocking collectives: 21.1 us -> 26.4 us  [body(): got = lax.all_to_all(sent.reshape(NSP, 3 * CHUNK, LANES), 'space', 0, 0)]
    unnamed x24 -> x0, local copies, waits for them, and re-layouts: 3.58 us -> none
    all_to_all x1 -> x0, waiting for transfers between devices: 3.24 us -> none  [body(): chunk = lax.all_to_all(errors, 'z', 0, 0)]
  transfers between devices with their start and end apart: 26 -> 25, of which waited for: 21 -> 19; matrix products, arithmetic and copies ran while one was open for 0% -> 0% of each run, Pallas kernels for 8% -> 8%
where the time goes in v8:
time: 195 us
  blocking collectives  103 us (53%)
  waiting for transfers between devices  36.4 us (19%)
  starting transfers between devices  28.6 us (15%)
  Pallas kernels  26.1 us (13%)
    all_to_all x1, blocking collectives, body(): got = lax.all_to_all(sent, 'space', 0, 0).reshape(-1, LANES)  28.4 us
    all_to_all x1, blocking collectives, body(): got = lax.all_to_all(sent.reshape(NSP, 3 * CHUNK, LANES), 'space', 0, 0)  26.4 us
    all_to_all x1, blocking collectives, body(): chunk = lax.all_to_all(errors, 'z', 0, 0)  26 us
    all_to_all x1, blocking collectives, body(): mine = lax.all_to_all(r, 'z', 0, 0)  21.7 us
    ppermute x7, waiting for transfers between devices, body(): ra = lax.ppermute(ma, everyone, pairs_a)  16.6 us
    pallas_call x6, Pallas kernels, body(): call(functools.partial(chain_kernel, t), [piece, piece, message, message]...  8.76 us
    ppermute x7, starting transfers between devices, body(): ra = lax.ppermute(ma, everyone, pairs_a)  8.67 us
    ppermute x7, starting transfers between devices, body(): rb = lax.ppermute(mb, everyone, pairs_b)  7.59 us
  transfers between devices with their start and end apart: 25, of which 19 were waited for; matrix products, arithmetic and copies ran while one was open for 0% of the time, Pallas kernels for 8%

profile of v8, /device:TPU:8, one launch (start us, length us, event | category | flops | bytes accessed | tf_op | source)
XLA Modules:
  0.0 194.7 jit_solution(8663186252794399803)
XLA Ops:
  0.6 2.8 %shard_map.50 = f32[16,192,128]{2,1,0:T(8,128)} custom-call(f32[128,1024]{1,0:T(8,128)} %bitcast.12, f32[128,1024]{1,0:T(8,128)} %bitcast.13, f32[128,1024]{1,0:T(8,128)} %bitcast.14), custom_call_target="tpu_custom_call" | custom-call | tf_op jit(solution)/shard_map/pallas_call | solution.py:487
  3.4 28.4 %all_to_all.20 = f32[16,192,128]{2,1,0:T(8,128)S(1)} all-to-all(f32[16,192,128]{2,1,0:T(8,128)} %shard_map.50), channel_id=1, replica_groups=mesh['z'=8,'core'=2,'space'=16] {'space'}, dimensions={0} | all-to-all | bytes 3145728 | tf_op jit(solution)/shard_map/all_to_all | solution.py:490
  33.0 1.7 collective-permute-done.oth_ref
  34.7 4.0 %shard_map.53 = (f32[96,16,128]{2,1,0:T(8,128)S(1)}, f32[64,16,128]{2,1,0:T(8,128)S(1)}, f32[32,16,128]{2,1,0:T(8,128)S(1)}, f32[32,16,128]{2,1,0:T(8,128)S(1)},...) custom-call(f32[96,16,128]{2,1,0:T(8,128)S(1)} %get-tuple-element.81, ...), custom_call_target="tpu_custom_call", output_to_operand_aliasing={{0}: (0, {})} | custom-call | tf_op jit(solution)/shard_map/pallas_call | solution.py:497
  38.7 5.6 %collective-permute-start.1 = (f32[64,16,128]{2,1,0:T(8,128)S(1)}, f32[64,16,128]{2,1,0:T(8,128)S(1)}, u32[]{:S(2)}, u32[]{:S(2)}) collective-permute-start(f32[64,16,128]{2,1,0:T(8,128)S(1)} %get-tuple-element.86), channel_id=1, source_target_pairs={{0,240},{1,241},{2,242},{3,243},{4,244},{5,245},{6,246},{7,247},{8... | collective-permute-start | bytes 1572872 | tf_op jit(solution)/shard_map/ppermute | solution.py:505
  44.3 3.3 %shard_map.54.w_ref = f32[64,16,128]{2,1,0:T(8,128)S(1)} custom-call(f32[96,16,128]{2,1,0:T(8,128)S(1)} %get-tuple-element.82.u_ref, f32[96,16,128]{2,1,0:T(8,128)S(1)} %get-tuple-element.83.inv_ref, f32[96,16,128]{2,1,0:T(8,128)S(1)} %get-tuple-element.84.cc_ref, f32[96,16,128]{2,1,0:T(8,128)S(1)} %get-tuple-element.85.sinv_ref), custom_call_target="tpu_custom_call" | custom-call | tf_op jit(solution)/shard_map/pallas_call | solution.py:506
  47.7 3.4 %collective-permute-done.1.next_ref = f32[64,16,128]{2,1,0:T(8,128)S(1)} collective-permute-done((f32[64,16,128]{2,1,0:T(8,128)S(1)}, f32[64,16,128]{2,1,0:T(8,128)S(1)}, u32[]{:S(2)}, u32[]{:S(2)}) %collective-permute-start.1) | collective-permute-done | bytes 524320 | tf_op jit(solution)/shard_map/ppermute | solution.py:505
  51.1 21.7 %all_to_all.21.own_ref = f32[8,8,16,128]{3,2,1,0:T(8,128)S(1)} all-to-all(f32[8,8,16,128]{3,2,1,0:T(8,128)S(1)} %get-tuple-element.87), channel_id=1, replica_groups=mesh['z'=8,'core'=2,'space'=16] {'z'}, dimensions={0} | all-to-all | bytes 1048576 | tf_op jit(solution)/shard_map/all_to_all | solution.py:509
  73.0 1.8 collective-permute-done.2.oth_ref
  75.1 1.2 collective-permute-start.4
  76.3 3.5 %collective-permute-done.3.ra_ref = f32[12,16,128]{2,1,0:T(8,128)S(1)} collective-permute-done((f32[12,16,128]{2,1,0:T(8,128)S(1)}, f32[12,16,128]{2,1,0:T(8,128)S(1)}, u32[]{:S(2)}, u32[]{:S(2)}) %collective-permute-start.3) | collective-permute-done | bytes 98336 | tf_op jit(solution)/shard_map/ppermute | solution.py:520
  80.1 1.5 shard_map.57
  81.5 1.6 collective-permute-start.5
  83.2 1.0 collective-permute-start.6
  84.2 2.5 %collective-permute-done.5.ra_ref = f32[12,16,128]{2,1,0:T(8,128)S(1)} collective-permute-done((f32[12,16,128]{2,1,0:T(8,128)S(1)}, f32[12,16,128]{2,1,0:T(8,128)S(1)}, u32[]{:S(2)}, u32[]{:S(2)}) %collective-permute-start.5) | collective-permute-done | bytes 98336 | tf_op jit(solution)/shard_map/ppermute | solution.py:520
  86.7 1.4 collective-permute-done.6.rb_ref
  88.1 1.0 collective-permute-start.10
  89.0 1.5 shard_map.58
  90.5 1.1 collective-permute-start.9
  91.6 1.9 collective-permute-start.8
  93.5 1.7 collective-permute-done.9.rb_ref
  95.3 1.0 collective-permute-done.8.ra_ref
  96.2 1.9 collective-permute-start.13
  98.2 1.5 shard_map.59
  100.1 1.0 collective-permute-start.12
  101.2 3.2 %collective-permute-done.11.ra_ref = f32[12,16,128]{2,1,0:T(8,128)S(1)} collective-permute-done((f32[12,16,128]{2,1,0:T(8,128)S(1)}, f32[12,16,128]{2,1,0:T(8,128)S(1)}, u32[]{:S(2)}, u32[]{:S(2)}) %collective-permute-start.11) | collective-permute-done | bytes 98336 | tf_op jit(solution)/shard_map/ppermute | solution.py:520
  104.7 1.7 collective-permute-start.16
  106.4 1.5 shard_map.60
  107.9 1.1 collective-permute-start.15
  109.0 2.3 %collective-permute-start.14 = (f32[12,16,128]{2,1,0:T(8,128)S(1)}, f32[12,16,128]{2,1,0:T(8,128)S(1)}, u32[]{:S(2)}, u32[]{:S(2)}) collective-permute-start(f32[12,16,128]{2,1,0:T(8,128)S(1)} %get-tuple-element.120), channel_id=1, source_target_pairs={{0,32},{32,0},{64,96},{96,64},{128,160},{160,128},{192,224},{224,1... | collective-permute-start | bytes 294920 | tf_op jit(solution)/shard_map/ppermute | solution.py:520
  111.4 1.3 collective-permute-done.15.rb_ref
  112.6 1.3 collective-permute-done.14.ra_ref
  113.9 1.5 shard_map.61
  115.4 2.1 %collective-permute-start.17 = (f32[12,16,128]{2,1,0:T(8,128)S(1)}, f32[12,16,128]{2,1,0:T(8,128)S(1)}, u32[]{:S(2)}, u32[]{:S(2)}) collective-permute-start(f32[12,16,128]{2,1,0:T(8,128)S(1)} %get-tuple-element.128), channel_id=1, source_target_pairs={{0,32},{32,0},{64,96},{96,64},{128,160},{160,128},{192,224},{224,1... | collective-permute-start | bytes 294920 | tf_op jit(solution)/shard_map/ppermute | solution.py:520
  117.5 1.0 collective-permute-start.18
  118.6 1.6 collective-permute-done.17.ra_ref
  120.1 2.0 %collective-permute-done.18.rb_ref = f32[12,16,128]{2,1,0:T(8,128)S(1)} collective-permute-done((f32[12,16,128]{2,1,0:T(8,128)S(1)}, f32[12,16,128]{2,1,0:T(8,128)S(1)}, u32[]{:S(2)}, u32[]{:S(2)}) %collective-permute-start.18) | collective-permute-done | bytes 98336 | tf_op jit(solution)/shard_map/ppermute | solution.py:521
  122.2 1.2 collective-permute-start.19
  123.4 1.5 shard_map.62
  124.8 4.9 %collective-permute-done.19.r3_ref = f32[2,8,16,128]{3,2,1,0:T(8,128)S(1)} collective-permute-done((f32[2,8,16,128]{3,2,1,0:T(8,128)S(1)}, f32[2,8,16,128]{3,2,1,0:T(8,128)S(1)}, u32[]{:S(2)}, u32[]{:S(2)}) %collective-permute-start.19) | collective-permute-done | bytes 131104 | tf_op jit(solution)/shard_map/ppermute | solution.py:525
  129.7 1.0 collective-permute-start.22
  130.8 3.6 %collective-permute-done.20.ra_ref = f32[12,16,128]{2,1,0:T(8,128)S(1)} collective-permute-done((f32[12,16,128]{2,1,0:T(8,128)S(1)}, f32[12,16,128]{2,1,0:T(8,128)S(1)}, u32[]{:S(2)}, u32[]{:S(2)}) %collective-permute-start.20) | collective-permute-done | bytes 98336 | tf_op jit(solution)/shard_map/ppermute | solution.py:520
  134.3 0.9 shard_map.63
  135.2 26.0 %all_to_all.22.e_ref = f32[8,8,16,128]{3,2,1,0:T(8,128)S(1)} all-to-all(f32[8,8,16,128]{3,2,1,0:T(8,128)S(1)} %shard_map.63), channel_id=1, replica_groups=mesh['z'=8,'core'=2,'space'=16] {'z'}, dimensions={0} | all-to-all | bytes 1048576 | tf_op jit(solution)/shard_map/all_to_all | solution.py:542
  162.1 2.9 %shard_map.64 = (f32[3072,128]{1,0:T(8,128)S(1)}, f32[2,8,16,128]{3,2,1,0:T(8,128)S(1)}) custom-call(f32[8,8,16,128]{3,2,1,0:T(8,128)S(1)} %all_to_all.22.e_ref, f32[32,16,128]{2,1,0:T(8,128)S(1)} %collective-permute-done.7.cp_low_ref, f32[32,16,128]{2,1,0:T(8,128)S(1)} %collective-permute-done.21.cp_high_ref, ...), custom_call_target="tpu_custom_call" | custom-call | tf_op jit(solution)/shard_map/pallas_call | solution.py:549
  166.0 0.7 shard_map.66
  166.7 26.4 %all_to_all.23.a_ref = f32[16,192,128]{2,1,0:T(8,128)S(1)} all-to-all(f32[16,192,128]{2,1,0:T(8,128)S(1)} %bitcast.11), channel_id=1, replica_groups=mesh['z'=8,'core'=2,'space'=16] {'space'}, dimensions={0} | all-to-all | bytes 3145728 | tf_op jit(solution)/shard_map/all_to_all | solution.py:560
  193.2 1.4 shard_map.67
  (25 shorter events, 4.6 us)
Async XLA Ops:
  32.4 2.4 %collective-permute-start = (f32[96,16,128]{2,1,0:T(8,128)S(1)}, f32[96,16,128]{2,1,0:T(8,128)S(1)}, u32[]{:S(2)}, u32[]{:S(2)}) collective-permute-start(f32[96,16,128]{2,1,0:T(8,128)S(1)} %shard_map.52.own_ref), channel_id=1, source_target_pairs={{0,16},{16,0},{1,17},{17,1},{2,18},{18,2},{3,19},{19,3},{4,20},{20... | collective-permute-start | bytes 2359304 | tf_op jit(solution)/shard_map/ppermute | solution.py:485
  38.7 12.3 %collective-permute-start.1 = (f32[64,16,128]{2,1,0:T(8,128)S(1)}, f32[64,16,128]{2,1,0:T(8,128)S(1)}, u32[]{:S(2)}, u32[]{:S(2)}) collective-permute-start(f32[64,16,128]{2,1,0:T(8,128)S(1)} %get-tuple-element.86), channel_id=1, source_target_pairs={{0,240},{1,241},{2,242},{3,243},{4,244},{5,245},{6,246},{7,247},{8... | collective-permute-start | bytes 1572872 | tf_op jit(solution)/shard_map/ppermute | solution.py:505
  72.8 1.9 collective-permute-start.2
  74.9 4.9 %collective-permute-start.3 = (f32[12,16,128]{2,1,0:T(8,128)S(1)}, f32[12,16,128]{2,1,0:T(8,128)S(1)}, u32[]{:S(2)}, u32[]{:S(2)}) collective-permute-start(f32[12,16,128]{2,1,0:T(8,128)S(1)} %get-tuple-element.88), channel_id=1, source_target_pairs={{0,32},{32,0},{64,96},{96,64},{128,160},{160,128},{192,224},{224,1... | collective-permute-start | bytes 294920 | tf_op jit(solution)/shard_map/ppermute | solution.py:520
  75.1 4.9 %collective-permute-start.4 = (f32[12,16,128]{2,1,0:T(8,128)S(1)}, f32[12,16,128]{2,1,0:T(8,128)S(1)}, u32[]{:S(2)}, u32[]{:S(2)}) collective-permute-start(f32[12,16,128]{2,1,0:T(8,128)S(1)} %get-tuple-element.89), channel_id=1, source_target_pairs={{32,64},{64,32},{96,128},{128,96},{160,192},{192,160},{224,225},{2... | collective-permute-start | bytes 294920 | tf_op jit(solution)/shard_map/ppermute | solution.py:521
  80.1 11.6 %collective-permute-start.7 = (f32[32,16,128]{2,1,0:T(8,128)S(1)}, f32[32,16,128]{2,1,0:T(8,128)S(1)}, u32[]{:S(2)}, u32[]{:S(2)}) collective-permute-start(f32[32,16,128]{2,1,0:T(8,128)S(1)} %get-tuple-element.103), channel_id=1, source_target_pairs={{0,16},{1,17},{2,18},{3,19},{4,20},{5,21},{6,22},{7,23},{8,24},{9,... | collective-permute-start | bytes 786440 | tf_op jit(solution)/shard_map/ppermute | solution.py:525
  81.5 5.1 %collective-permute-start.5 = (f32[12,16,128]{2,1,0:T(8,128)S(1)}, f32[12,16,128]{2,1,0:T(8,128)S(1)}, u32[]{:S(2)}, u32[]{:S(2)}) collective-permute-start(f32[12,16,128]{2,1,0:T(8,128)S(1)} %get-tuple-element.96), channel_id=1, source_target_pairs={{0,32},{32,0},{64,96},{96,64},{128,160},{160,128},{192,224},{224,1... | collective-permute-start | bytes 294920 | tf_op jit(solution)/shard_map/ppermute | solution.py:520
  83.2 4.9 %collective-permute-start.6 = (f32[12,16,128]{2,1,0:T(8,128)S(1)}, f32[12,16,128]{2,1,0:T(8,128)S(1)}, u32[]{:S(2)}, u32[]{:S(2)}) collective-permute-start(f32[12,16,128]{2,1,0:T(8,128)S(1)} %get-tuple-element.97), channel_id=1, source_target_pairs={{32,64},{64,32},{96,128},{128,96},{160,192},{192,160},{224,225},{2... | collective-permute-start | bytes 294920 | tf_op jit(solution)/shard_map/ppermute | solution.py:521
  88.1 11.6 %collective-permute-start.10 = (f32[2,8,16,128]{3,2,1,0:T(8,128)S(1)}, f32[2,8,16,128]{3,2,1,0:T(8,128)S(1)}, u32[]{:S(2)}, u32[]{:S(2)}) collective-permute-start(f32[2,8,16,128]{3,2,1,0:T(8,128)S(1)} %get-tuple-element.111), channel_id=1, source_target_pairs={{0,32},{1,33},{2,34},{3,35},{4,36},{5,37},{6,38},{7,39},{8,40},{9,... | collective-permute-start | bytes 393224 | tf_op jit(solution)/shard_map/ppermute | solution.py:525
  90.5 4.8 %collective-permute-start.9 = (f32[12,16,128]{2,1,0:T(8,128)S(1)}, f32[12,16,128]{2,1,0:T(8,128)S(1)}, u32[]{:S(2)}, u32[]{:S(2)}) collective-permute-start(f32[12,16,128]{2,1,0:T(8,128)S(1)} %get-tuple-element.105), channel_id=1, source_target_pairs={{32,64},{64,32},{96,128},{128,96},{160,192},{192,160},{224,225},{2... | collective-permute-start | bytes 294920 | tf_op jit(solution)/shard_map/ppermute | solution.py:521
  91.6 4.6 %collective-permute-start.8 = (f32[12,16,128]{2,1,0:T(8,128)S(1)}, f32[12,16,128]{2,1,0:T(8,128)S(1)}, u32[]{:S(2)}, u32[]{:S(2)}) collective-permute-start(f32[12,16,128]{2,1,0:T(8,128)S(1)} %get-tuple-element.104), channel_id=1, source_target_pairs={{0,32},{32,0},{64,96},{96,64},{128,160},{160,128},{192,224},{224,1... | collective-permute-start | bytes 294920 | tf_op jit(solution)/shard_map/ppermute | solution.py:520
  96.2 12.8 %collective-permute-start.13 = (f32[2,8,16,128]{3,2,1,0:T(8,128)S(1)}, f32[2,8,16,128]{3,2,1,0:T(8,128)S(1)}, u32[]{:S(2)}, u32[]{:S(2)}) collective-permute-start(f32[2,8,16,128]{3,2,1,0:T(8,128)S(1)} %get-tuple-element.119), channel_id=1, source_target_pairs={{0,32},{1,33},{2,34},{3,35},{4,36},{5,37},{6,38},{7,39},{8,40},{9,... | collective-permute-start | bytes 393224 | tf_op jit(solution)/shard_map/ppermute | solution.py:525
  99.7 4.7 %collective-permute-start.11 = (f32[12,16,128]{2,1,0:T(8,128)S(1)}, f32[12,16,128]{2,1,0:T(8,128)S(1)}, u32[]{:S(2)}, u32[]{:S(2)}) collective-permute-start(f32[12,16,128]{2,1,0:T(8,128)S(1)} %get-tuple-element.112), channel_id=1, source_target_pairs={{0,32},{32,0},{64,96},{96,64},{128,160},{160,128},{192,224},{224,1... | collective-permute-start | bytes 294920 | tf_op jit(solution)/shard_map/ppermute | solution.py:520
  100.1 4.6 %collective-permute-start.12 = (f32[12,16,128]{2,1,0:T(8,128)S(1)}, f32[12,16,128]{2,1,0:T(8,128)S(1)}, u32[]{:S(2)}, u32[]{:S(2)}) collective-permute-start(f32[12,16,128]{2,1,0:T(8,128)S(1)} %get-tuple-element.113), channel_id=1, source_target_pairs={{32,64},{64,32},{96,128},{128,96},{160,192},{192,160},{224,225},{2... | collective-permute-start | bytes 294920 | tf_op jit(solution)/shard_map/ppermute | solution.py:521
  104.7 10.7 %collective-permute-start.16 = (f32[2,8,16,128]{3,2,1,0:T(8,128)S(1)}, f32[2,8,16,128]{3,2,1,0:T(8,128)S(1)}, u32[]{:S(2)}, u32[]{:S(2)}) collective-permute-start(f32[2,8,16,128]{3,2,1,0:T(8,128)S(1)} %get-tuple-element.127), channel_id=1, source_target_pairs={{0,32},{1,33},{2,34},{3,35},{4,36},{5,37},{6,38},{7,39},{8,40},{9,... | collective-permute-start | bytes 393224 | tf_op jit(solution)/shard_map/ppermute | solution.py:525
  107.9 4.7 %collective-permute-start.15 = (f32[12,16,128]{2,1,0:T(8,128)S(1)}, f32[12,16,128]{2,1,0:T(8,128)S(1)}, u32[]{:S(2)}, u32[]{:S(2)}) collective-permute-start(f32[12,16,128]{2,1,0:T(8,128)S(1)} %get-tuple-element.121), channel_id=1, source_target_pairs={{32,64},{64,32},{96,128},{128,96},{160,192},{192,160},{224,225},{2... | collective-permute-start | bytes 294920 | tf_op jit(solution)/shard_map/ppermute | solution.py:521
  109.0 4.9 %collective-permute-start.14 = (f32[12,16,128]{2,1,0:T(8,128)S(1)}, f32[12,16,128]{2,1,0:T(8,128)S(1)}, u32[]{:S(2)}, u32[]{:S(2)}) collective-permute-start(f32[12,16,128]{2,1,0:T(8,128)S(1)} %get-tuple-element.120), channel_id=1, source_target_pairs={{0,32},{32,0},{64,96},{96,64},{128,160},{160,128},{192,224},{224,1... | collective-permute-start | bytes 294920 | tf_op jit(solution)/shard_map/ppermute | solution.py:520
  115.4 4.7 %collective-permute-start.17 = (f32[12,16,128]{2,1,0:T(8,128)S(1)}, f32[12,16,128]{2,1,0:T(8,128)S(1)}, u32[]{:S(2)}, u32[]{:S(2)}) collective-permute-start(f32[12,16,128]{2,1,0:T(8,128)S(1)} %get-tuple-element.128), channel_id=1, source_target_pairs={{0,32},{32,0},{64,96},{96,64},{128,160},{160,128},{192,224},{224,1... | collective-permute-start | bytes 294920 | tf_op jit(solution)/shard_map/ppermute | solution.py:520
  117.5 4.6 %collective-permute-start.18 = (f32[12,16,128]{2,1,0:T(8,128)S(1)}, f32[12,16,128]{2,1,0:T(8,128)S(1)}, u32[]{:S(2)}, u32[]{:S(2)}) collective-permute-start(f32[12,16,128]{2,1,0:T(8,128)S(1)} %get-tuple-element.129), channel_id=1, source_target_pairs={{32,64},{64,32},{96,128},{128,96},{160,192},{192,160},{224,225},{2... | collective-permute-start | bytes 294920 | tf_op jit(solution)/shard_map/ppermute | solution.py:521
  122.2 12.2 %collective-permute-start.21 = (f32[32,16,128]{2,1,0:T(8,128)S(1)}, f32[32,16,128]{2,1,0:T(8,128)S(1)}, u32[]{:S(2)}, u32[]{:S(2)}) collective-permute-start(f32[32,16,128]{2,1,0:T(8,128)S(1)} %get-tuple-element.137), channel_id=1, source_target_pairs={{0,16},{1,17},{2,18},{3,19},{4,20},{5,21},{6,22},{7,23},{8,24},{9,... | collective-permute-start | bytes 786440 | tf_op jit(solution)/shard_map/ppermute | solution.py:525
  122.2 7.6 %collective-permute-start.19 = (f32[2,8,16,128]{3,2,1,0:T(8,128)S(1)}, f32[2,8,16,128]{3,2,1,0:T(8,128)S(1)}, u32[]{:S(2)}, u32[]{:S(2)}) collective-permute-start(f32[2,8,16,128]{3,2,1,0:T(8,128)S(1)} %get-tuple-element.135), channel_id=1, source_target_pairs={{0,32},{1,33},{2,34},{3,35},{4,36},{5,37},{6,38},{7,39},{8,40},{9,... | collective-permute-start | bytes 393224 | tf_op jit(solution)/shard_map/ppermute | solution.py:525
  129.7 4.6 %collective-permute-start.20 = (f32[12,16,128]{2,1,0:T(8,128)S(1)}, f32[12,16,128]{2,1,0:T(8,128)S(1)}, u32[]{:S(2)}, u32[]{:S(2)}) collective-permute-start(f32[12,16,128]{2,1,0:T(8,128)S(1)} %get-tuple-element.136), channel_id=1, source_target_pairs={{0,32},{32,0},{64,96},{96,64},{128,160},{160,128},{192,224},{224,1... | collective-permute-start | bytes 294920 | tf_op jit(solution)/shard_map/ppermute | solution.py:520
  129.7 4.6 %collective-permute-start.22 = (f32[12,16,128]{2,1,0:T(8,128)S(1)}, f32[12,16,128]{2,1,0:T(8,128)S(1)}, u32[]{:S(2)}, u32[]{:S(2)}) collective-permute-start(f32[12,16,128]{2,1,0:T(8,128)S(1)} %get-tuple-element.139), channel_id=1, source_target_pairs={{32,64},{64,32},{96,128},{128,96},{160,192},{192,160},{224,225},{2... | collective-permute-start | bytes 294920 | tf_op jit(solution)/shard_map/ppermute | solution.py:521
  161.4 4.0 %collective-permute-start.23 = (f32[4,16,128]{2,1,0:T(8,128)S(1)}, f32[4,16,128]{2,1,0:T(8,128)S(1)}, u32[]{:S(2)}, u32[]{:S(2)}) collective-permute-start(f32[4,16,128]{2,1,0:T(8,128)S(1)} %get-tuple-element.156), channel_id=1, source_target_pairs={{0,1},{1,0},{2,3},{3,2},{7,6},{6,7},{5,4},{4,5},{8,9},{9,8},{10,11... | collective-permute-start | bytes 98312 | tf_op jit(solution)/shard_map/ppermute | solution.py:547
  162.1 3.9 %collective-permute-start.24 = (f32[4,16,128]{2,1,0:T(8,128)S(1)}, f32[4,16,128]{2,1,0:T(8,128)S(1)}, u32[]{:S(2)}, u32[]{:S(2)}) collective-permute-start(f32[4,16,128]{2,1,0:T(8,128)S(1)} %get-tuple-element.157), channel_id=1, source_target_pairs={{1,2},{2,1},{3,7},{7,3},{6,5},{5,6},{4,8},{8,4},{9,10},{10,9},{11,... | collective-permute-start | bytes 98312 | tf_op jit(solution)/shard_map/ppermute | solution.py:548
